TPU v7x, 32 devices: a whole 2x2x4 slice. The times are simulated.
32 devices in a mesh: dp: 8 (over z, x), shard: 4 (over y, core).
Axes of the slice: x: 2, y: 2, z: 4, core: 2. Of those that a mesh axis runs over, the one named last changes fastest.
Arguments:
- tokens: bfloat16 [4096, 1024], P(('dp', 'shard')), may hold values from -6 to 6
- cotangent: bfloat16 [4096, 1024], P(('dp', 'shard')), may hold values from -6 to 6
- query_key: float32 [2, 1024, 1024], P(None, ('dp', 'shard')), may hold values from -0.1875 to 0.1875
- value_gate: float32 [2, 1024, 2048], P(None, ('dp', 'shard')), may hold values from -0.1875 to 0.1875
- output_weight: float32 [2048, 1024], P(('dp', 'shard')), may hold values from -0.125 to 0.125
- gate_up: float32 [2, 1024, 2816], P(None, ('dp', 'shard')), may hold values from -0.1875 to 0.1875
- down_weight: float32 [2816, 1024], P(('dp', 'shard')), may hold values from -0.109375 to 0.109375
- small_params: float32 [35088], replicated, may hold values from -7 to 3
- momentum_query_key: float32 [2, 1024, 1024], P(None, ('dp', 'shard')), may hold values from -80 to 80
- momentum_value_gate: float32 [2, 1024, 2048], P(None, ('dp', 'shard')), may hold values from -80 to 80
- momentum_output: float32 [2048, 1024], P(('dp', 'shard')), may hold values from -80 to 80
- momentum_gate_up: float32 [2, 1024, 2816], P(None, ('dp', 'shard')), may hold values from -80 to 80
- momentum_down: float32 [2816, 1024], P(('dp', 'shard')), may hold values from -80 to 80
- moment_one: float32 [35088], replicated, may hold values from -40 to 40
- moment_two: float32 [35088], replicated, may hold values from 4.096 to 409.6
- seq_lengths: int32 [8, 4], P('dp'), may hold values from 1 to 256, 512 in all within a row
Outputs:
- block_out: bfloat16 [4096, 1024], P(('dp', 'shard'))
- input_grad: bfloat16 [4096, 1024], P(('dp', 'shard'))
- grad_query_key: float32 [2, 1024, 1024], P(None, ('dp', 'shard'))
- grad_value_gate: float32 [2, 1024, 2048], P(None, ('dp', 'shard'))
- grad_output: float32 [2048, 1024], P(('dp', 'shard'))
- grad_gate_up: float32 [2, 1024, 2816], P(None, ('dp', 'shard'))
- grad_down: float32 [2816, 1024], P(('dp', 'shard'))
- step_query_key: float32 [2, 1024, 1024], P(None, ('dp', 'shard'))
- step_value_gate: float32 [2, 1024, 2048], P(None, ('dp', 'shard'))
- step_output: float32 [2048, 1024], P(('dp', 'shard'))
- step_gate_up: float32 [2, 1024, 2816], P(None, ('dp', 'shard'))
- step_down: float32 [2816, 1024], P(('dp', 'shard'))
- new_momentum_query_key: float32 [2, 1024, 1024], P(None, ('dp', 'shard'))
- new_momentum_value_gate: float32 [2, 1024, 2048], P(None, ('dp', 'shard'))
- new_momentum_output: float32 [2048, 1024], P(('dp', 'shard'))
- new_momentum_gate_up: float32 [2, 1024, 2816], P(None, ('dp', 'shard'))
- new_momentum_down: float32 [2816, 1024], P(('dp', 'shard'))
- small_grad: float32 [35088], replicated
- small_step: float32 [35088], replicated
- new_moment_one: float32 [35088], replicated
- new_moment_two: float32 [35088], replicated
Inputs may be any that keep to these rules, and one draw needn't show every extreme that they name: `seq_lengths`: each row sums to 512, and its largest length is exactly 256.
All inputs are finite; a program needn't handle non-finite values.
Results may differ from a plain program's by a relative error of at most 0.015.
The roundings to bfloat16 on the way count: a program that leaves them out, or rounds other values in their place, can miss the bound.
Values may be sent and summed in bfloat16 or wider, within the bound.
A program may use at most 384 MiB of HBM per device.

v0:
```python
import math

import jax
import jax.numpy as jnp
from jax import lax
from jax.sharding import PartitionSpec as P

D = 1024
H = 8
DK = 128
DV = 256
KCONV = 4
SPAN = 64
NS_STEPS = 2
STEP_COUNT = 10


PRECISION_LEVEL = lax.Precision.HIGHEST
NORM_EPS = 1e-06
GATE_EPS = 1e-05
UNIT_EPS = 1e-06
COEF_A = 3.4445
COEF_B = -4.775
COEF_C = 2.0315
MOMENTUM = 0.95
MUON_RATE = 0.1
MUON_DECAY = 0.01
ADAM_RATE = 0.05
BETA_ONE = 0.9
BETA_TWO = 0.95
ADAM_EPS = 1e-08


def unpack(packed):
    amounts = [D * H, D * H, KCONV * H * DK, KCONV * H * DK, KCONV * H * DV, D, D, DV, H, H]
    layouts = [
        (D, H),
        (D, H),
        (KCONV, H * DK),
        (KCONV, H * DK),
        (KCONV, H * DV),
        (D,),
        (D,),
        (DV,),
        (H,),
        (H,),
    ]
    pieces = []
    offset = 0
    for amount, layout in zip(amounts, layouts):
        pieces.append(packed[offset : offset + amount].reshape(layout))
        offset = offset + amount
    return pieces


def rms_norm(values, norm_gain, epsilon):
    return (
        values * lax.rsqrt(jnp.mean(values * values, axis=-1, keepdims=True) + epsilon) * norm_gain
    )


def plain_norm(values, norm_gain):
    return rms_norm(values, norm_gain, NORM_EPS)


def unit_norm(values):
    return values * lax.rsqrt(jnp.sum(values * values, axis=-1, keepdims=True) + UNIT_EPS)


def swiglu(gate_pair):
    return jax.nn.silu(gate_pair[0]) * gate_pair[1]


def contract_rows(left_side, right_side):
    return lax.dot_general(
        left_side, right_side, (((0,), (0,)), ((), ())), preferred_element_type=jnp.float32
    )


def contract_cols(left_side, right_side):
    return lax.dot_general(
        left_side, right_side, (((1,), (1,)), ((), ())), preferred_element_type=jnp.float32
    )


def causal_conv(values, weight):
    summed = weight[KCONV - 1] * values
    for delay in range(1, KCONV):
        shifted = jnp.concatenate(
            [jnp.zeros((delay, values.shape[1]), jnp.float32), values[:-delay]], axis=0
        )
        summed = summed + weight[KCONV - 1 - delay] * shifted
    return jax.nn.silu(summed)


def spanned_rule(queries, key_rows, value_rows, log_decay, beta_gate):
    row_count = queries.shape[0]
    heads = queries.shape[1]
    blocks = row_count // SPAN

    def arrange(array):
        return jnp.swapaxes(array.reshape((blocks, SPAN) + array.shape[1:]), 1, 2)

    query_blocks = arrange(queries)
    key_blocks = arrange(key_rows)
    value_blocks = arrange(value_rows)
    decay_blocks = arrange(log_decay)
    beta_blocks = arrange(beta_gate)
    cumul = jnp.cumsum(decay_blocks, axis=-1)
    lower = jnp.tril(jnp.ones((SPAN, SPAN), jnp.float32))
    strict = jnp.tril(jnp.ones((SPAN, SPAN), jnp.float32), -1)
    ratio = jnp.exp(jnp.where(lower > 0, cumul[..., :, None] - cumul[..., None, :], 0.0)) * lower
    key_key = jnp.einsum("bhik,bhjk->bhij", key_blocks, key_blocks, precision=PRECISION_LEVEL)
    coupling = beta_blocks[..., :, None] * key_key * ratio * strict
    inverse = jnp.eye(SPAN, dtype=jnp.float32) - coupling
    power = coupling
    for level in range(1, SPAN.bit_length() - 1):
        power = jnp.einsum("bhij,bhjk->bhik", power, power, precision=PRECISION_LEVEL)
        inverse = inverse + jnp.einsum("bhij,bhjk->bhik", inverse, power, precision=PRECISION_LEVEL)
    first_part = jnp.einsum(
        "bhij,bhjv->bhiv", inverse, beta_blocks[..., None] * value_blocks, precision=PRECISION_LEVEL
    )
    second_part = jnp.einsum(
        "bhij,bhjk->bhik",
        inverse,
        (beta_blocks * jnp.exp(cumul))[..., None] * key_blocks,
        precision=PRECISION_LEVEL,
    )
    scores = (
        jnp.einsum("bhik,bhjk->bhij", query_blocks, key_blocks, precision=PRECISION_LEVEL) * ratio
    )
    tail_decay = jnp.exp(cumul[..., -1:] - cumul)

    def carry_step(memory_state, inputs):
        (
            leading_block,
            following_block,
            query_block_tile,
            key_block_tile,
            score_blk,
            cumul_blk,
            trailing_block,
        ) = inputs
        state_update = leading_block - jnp.einsum(
            "tpy,tyx->tpx", following_block, memory_state, precision=PRECISION_LEVEL
        )
        result = jnp.exp(cumul_blk)[..., None] * jnp.einsum(
            "tpy,tyx->tpx", query_block_tile, memory_state, precision=PRECISION_LEVEL
        )
        result = result + jnp.einsum(
            "hij,hjv->hiv", score_blk, state_update, precision=PRECISION_LEVEL
        )
        memory_state = jnp.exp(cumul_blk[:, -1])[:, None, None] * memory_state
        memory_state = memory_state + jnp.einsum(
            "bgr,bgo->bro",
            trailing_block[..., None] * key_block_tile,
            state_update,
            precision=PRECISION_LEVEL,
        )
        return (memory_state, result)

    initial = jnp.zeros((heads, DK, DV), jnp.float32)
    _, results = lax.scan(
        carry_step,
        initial,
        (first_part, second_part, query_blocks, key_blocks, scores, cumul, tail_decay),
    )
    return jnp.swapaxes(results, 1, 2).reshape(row_count, heads, DV)


def mixer(
    raw_query,
    raw_keys,
    raw_value,
    raw_gate,
    raw_decay,
    raw_beta,
    conv_query,
    conv_keys,
    conv_value,
    gain_out,
    a_log,
    dt_bias,
):
    row_count = raw_query.shape[0]
    queries = unit_norm(causal_conv(raw_query, conv_query).reshape(row_count, H, DK)) * DK ** (-0.5)
    key_rows = unit_norm(causal_conv(raw_keys, conv_keys).reshape(row_count, H, DK))
    value_rows = causal_conv(raw_value, conv_value).reshape(row_count, H, DV)
    beta_gate = jax.nn.sigmoid(raw_beta)
    log_decay = -jnp.exp(a_log) * jax.nn.softplus(raw_decay + dt_bias)
    mixed = spanned_rule(queries, key_rows, value_rows, log_decay, beta_gate)
    gated = rms_norm(mixed, gain_out, GATE_EPS) * jax.nn.silu(raw_gate).reshape(row_count, H, DV)
    return gated.reshape(row_count, H * DV)


def layer_forward(inputs_x, weights, packed):
    qk_full, vg_full, out_full, gu_full, down_full = weights
    (
        w_decay,
        w_beta,
        conv_query,
        conv_keys,
        conv_value,
        gain_one,
        gain_two,
        gain_out,
        a_log,
        dt_bias,
    ) = unpack(packed)
    normed_f, norm_one_pull = jax.vjp(plain_norm, inputs_x, gain_one)
    normed = normed_f.astype(jnp.bfloat16)
    raw_qk = jnp.einsum("nd,sdc->snc", normed, qk_full, preferred_element_type=jnp.float32)
    raw_vg = jnp.einsum("nd,sdc->snc", normed, vg_full, preferred_element_type=jnp.float32)
    raw_decay = jnp.dot(normed, w_decay.astype(jnp.bfloat16), preferred_element_type=jnp.float32)
    raw_beta = jnp.dot(normed, w_beta.astype(jnp.bfloat16), preferred_element_type=jnp.float32)
    gated_f, mix_pull = jax.vjp(
        mixer,
        raw_qk[0],
        raw_qk[1],
        raw_vg[0],
        raw_vg[1],
        raw_decay,
        raw_beta,
        conv_query,
        conv_keys,
        conv_value,
        gain_out,
        a_log,
        dt_bias,
    )
    gated = gated_f.astype(jnp.bfloat16)
    middle = inputs_x + jnp.dot(gated, out_full, preferred_element_type=jnp.float32)
    normed_two_f, norm_two_pull = jax.vjp(plain_norm, middle, gain_two)
    normed_two = normed_two_f.astype(jnp.bfloat16)
    gate_upper = jnp.einsum("nd,sdf->snf", normed_two, gu_full, preferred_element_type=jnp.float32)
    hidden_f, act_pull = jax.vjp(swiglu, gate_upper)
    hidden_act = hidden_f.astype(jnp.bfloat16)
    block_y = middle + jnp.dot(hidden_act, down_full, preferred_element_type=jnp.float32)
    saved = (
        normed,
        gated,
        normed_two,
        hidden_act,
        norm_one_pull,
        mix_pull,
        norm_two_pull,
        act_pull,
    )
    return (block_y, saved)


def layer_backward(grad_rows, weights, packed, saved):
    qk_full, vg_full, out_full, gu_full, down_full = weights
    (
        w_decay,
        w_beta,
        conv_query,
        conv_keys,
        conv_value,
        gain_one,
        gain_two,
        gain_out,
        a_log,
        dt_bias,
    ) = unpack(packed)
    normed, gated, normed_two, hidden_act, norm_one_pull, mix_pull, norm_two_pull, act_pull = saved
    grad_bf = grad_rows.astype(jnp.bfloat16)
    grad_dn = contract_rows(hidden_act, grad_bf)
    d_hidden = contract_cols(grad_bf, down_full)
    d_gate_upper = act_pull(d_hidden)[0].astype(jnp.bfloat16)
    grad_gu = jnp.einsum(
        "nd,snf->sdf", normed_two, d_gate_upper, preferred_element_type=jnp.float32
    )
    d_normed_two = jnp.einsum(
        "snf,sdf->nd", d_gate_upper, gu_full, preferred_element_type=jnp.float32
    )
    d_mid_norm, d_gain_two = norm_two_pull(d_normed_two)
    d_middle = grad_rows + d_mid_norm
    d_branch = d_middle.astype(jnp.bfloat16)
    grad_out = contract_rows(gated, d_branch)
    d_gated = contract_cols(d_branch, out_full)
    (
        d_query,
        d_keys,
        d_value,
        d_gate,
        d_decay,
        d_beta,
        g_conv_query,
        g_conv_keys,
        g_conv_value,
        g_gain_out,
        g_a_log,
        g_dt_bias,
    ) = mix_pull(d_gated)
    d_qk = jnp.stack([d_query, d_keys]).astype(jnp.bfloat16)
    d_vg = jnp.stack([d_value, d_gate]).astype(jnp.bfloat16)
    d_decay_bf = d_decay.astype(jnp.bfloat16)
    d_beta_bf = d_beta.astype(jnp.bfloat16)
    grad_qk = jnp.einsum("nd,snc->sdc", normed, d_qk, preferred_element_type=jnp.float32)
    grad_vg = jnp.einsum("nd,snc->sdc", normed, d_vg, preferred_element_type=jnp.float32)
    grad_w_decay = contract_rows(normed, d_decay_bf)
    grad_w_beta = contract_rows(normed, d_beta_bf)
    d_normed = jnp.einsum("snc,sdc->nd", d_qk, qk_full, preferred_element_type=jnp.float32)
    d_normed = d_normed + jnp.einsum(
        "snc,sdc->nd", d_vg, vg_full, preferred_element_type=jnp.float32
    )
    d_normed = d_normed + contract_cols(d_decay_bf, w_decay.astype(jnp.bfloat16))
    d_normed = d_normed + contract_cols(d_beta_bf, w_beta.astype(jnp.bfloat16))
    d_in_norm, d_gain_one = norm_one_pull(d_normed)
    d_input = d_middle + d_in_norm
    small_local = jnp.concatenate(
        [
            grad_w_decay.reshape(-1),
            grad_w_beta.reshape(-1),
            g_conv_query.reshape(-1),
            g_conv_keys.reshape(-1),
            g_conv_value.reshape(-1),
            d_gain_one,
            d_gain_two,
            g_gain_out,
            g_a_log,
            g_dt_bias,
        ]
    )
    return (d_input, (grad_qk, grad_vg, grad_out, grad_gu, grad_dn), small_local)


def orthogonalize(matrix):
    values = matrix.astype(jnp.float32)
    scaled = (values / (jnp.sqrt(jnp.sum(values * values)) + 1e-07)).astype(jnp.bfloat16)
    for iteration in range(NS_STEPS):
        gram = contract_cols(scaled, scaled).astype(jnp.bfloat16)
        poly = (
            COEF_B * gram.astype(jnp.float32)
            + COEF_C * jnp.dot(gram, gram, preferred_element_type=jnp.float32)
        ).astype(jnp.bfloat16)
        scaled = (
            COEF_A * scaled.astype(jnp.float32)
            + jnp.dot(poly, scaled, preferred_element_type=jnp.float32)
        ).astype(jnp.bfloat16)
    return scaled


def short_shape(rows_count, cols_count):
    return (min(rows_count, cols_count), max(rows_count, cols_count))


def to_padded(matrix, pad_rows, pad_cols):
    tall = matrix.shape[0] > matrix.shape[1]
    current = matrix.T if tall else matrix
    return jnp.pad(current, ((0, pad_rows - current.shape[0]), (0, pad_cols - current.shape[1])))


def from_padded(padded, rows_count, cols_count):
    tall = rows_count > cols_count
    short_rows, short_cols = short_shape(rows_count, cols_count)
    piece = padded[:short_rows, :short_cols]
    return piece.T if tall else piece


def muon_step(ortho_part, master_part, full_rows, full_cols):
    scale = 0.2 * math.sqrt(max(full_rows, full_cols))
    return -MUON_RATE * (scale * ortho_part.astype(jnp.float32) + MUON_DECAY * master_part)


def body(
    tokens,
    cotangent,
    query_key,
    value_gate,
    output_weight,
    gate_up,
    down_weight,
    small_params,
    momentum_query_key,
    momentum_value_gate,
    momentum_output,
    momentum_gate_up,
    momentum_down,
    moment_one,
    moment_two,
    seq_lengths,
):
    local_rows = tokens.shape[0]
    capacity = 2 * local_rows
    group_size = lax.axis_size("shard")
    member = lax.axis_index("shard")
    lengths = seq_lengths[0]
    ends = jnp.cumsum(lengths)
    starts = ends - lengths
    slots = jnp.arange(capacity, dtype=jnp.int32)
    anchor = starts[:, None] + slots[None, :] - member * local_rows
    taken = (slots[None, :] < lengths[:, None]) & (anchor >= 0) & (anchor < local_rows)
    source_rows = jnp.clip(anchor, 0, local_rows - 1)
    send_x = jnp.where(taken[..., None], tokens[source_rows], jnp.zeros((), jnp.bfloat16))
    send_dy = jnp.where(taken[..., None], cotangent[source_rows], jnp.zeros((), jnp.bfloat16))
    got_x, got_dy = (
        lax.all_to_all(send_x, "shard", split_axis=0, concat_axis=0, tiled=True),
        lax.all_to_all(send_dy, "shard", split_axis=0, concat_axis=0, tiled=True),
    )
    inputs_x = jnp.sum(got_x.astype(jnp.float32), axis=0)
    grad_rows = jnp.sum(got_dy.astype(jnp.float32), axis=0)
    cast_qk = query_key.astype(jnp.bfloat16)
    cast_vg = value_gate.astype(jnp.bfloat16)
    cast_out = output_weight.astype(jnp.bfloat16)
    cast_gu = gate_up.astype(jnp.bfloat16)
    cast_down = down_weight.astype(jnp.bfloat16)
    gathered = (
        lax.all_gather(cast_qk, ("dp", "shard"), axis=1, tiled=True),
        lax.all_gather(cast_vg, ("dp", "shard"), axis=1, tiled=True),
        lax.all_gather(cast_out, ("dp", "shard"), axis=0, tiled=True),
        lax.all_gather(cast_gu, ("dp", "shard"), axis=1, tiled=True),
        lax.all_gather(cast_down, ("dp", "shard"), axis=0, tiled=True),
    )
    block_y, unused_saved = layer_forward(inputs_x, gathered, small_params)
    weights_back = (
        lax.all_gather(cast_qk, ("dp", "shard"), axis=1, tiled=True),
        lax.all_gather(cast_vg, ("dp", "shard"), axis=1, tiled=True),
        lax.all_gather(cast_out, ("dp", "shard"), axis=0, tiled=True),
        lax.all_gather(cast_gu, ("dp", "shard"), axis=1, tiled=True),
        lax.all_gather(cast_down, ("dp", "shard"), axis=0, tiled=True),
    )
    replay_y, saved = layer_forward(inputs_x, weights_back, small_params)
    d_input, big_local, small_local = layer_backward(grad_rows, weights_back, small_params, saved)
    local_qk, local_vg, local_out, local_gu, local_down = big_local
    grad_qk, grad_vg, grad_out, grad_gu, grad_dn = (
        lax.psum_scatter(local_qk, ("dp", "shard"), scatter_dimension=1, tiled=True),
        lax.psum_scatter(local_vg, ("dp", "shard"), scatter_dimension=1, tiled=True),
        lax.psum_scatter(local_out, ("dp", "shard"), scatter_dimension=0, tiled=True),
        lax.psum_scatter(local_gu, ("dp", "shard"), scatter_dimension=1, tiled=True),
        lax.psum_scatter(local_down, ("dp", "shard"), scatter_dimension=0, tiled=True),
    )
    small_grad = lax.psum(small_local, ("dp", "shard"))
    mom_qk = MOMENTUM * momentum_query_key + grad_qk
    mom_vg = MOMENTUM * momentum_value_gate + grad_vg
    mom_out = MOMENTUM * momentum_output + grad_out
    mom_gu = MOMENTUM * momentum_gate_up + grad_gu
    mom_dn = MOMENTUM * momentum_down + grad_dn
    look_qk = (grad_qk + MOMENTUM * mom_qk).astype(jnp.bfloat16)
    look_vg = (grad_vg + MOMENTUM * mom_vg).astype(jnp.bfloat16)
    look_out = (grad_out + MOMENTUM * mom_out).astype(jnp.bfloat16)
    look_gu = (grad_gu + MOMENTUM * mom_gu).astype(jnp.bfloat16)
    look_dn = (grad_dn + MOMENTUM * mom_dn).astype(jnp.bfloat16)
    devices = lax.axis_size(("dp", "shard"))
    position = lax.axis_index(("dp", "shard"))
    spacing = devices // 8
    masters = [
        query_key[0],
        query_key[1],
        value_gate[0],
        value_gate[1],
        output_weight,
        gate_up[0],
        gate_up[1],
        down_weight,
    ]
    pieces = [
        look_qk[0],
        look_qk[1],
        look_vg[0],
        look_vg[1],
        look_out,
        look_gu[0],
        look_gu[1],
        look_dn,
    ]
    full_shapes = [(piece.shape[0] * devices, piece.shape[1]) for piece in pieces]
    pad_rows = max((short_shape(r_count, c_count)[0] for r_count, c_count in full_shapes))
    pad_cols = max((short_shape(r_count, c_count)[1] for r_count, c_count in full_shapes))
    steps_list = []
    widest = max((piece.shape[0] * piece.shape[1] for piece in pieces))
    outgoing = jnp.zeros((devices, widest), jnp.bfloat16)
    for number in range(8):
        flat = pieces[number].reshape(-1)
        outgoing = outgoing.at[number * spacing].set(jnp.pad(flat, (0, widest - flat.shape[0])))
    incoming = lax.all_to_all(outgoing, ("dp", "shard"), split_axis=0, concat_axis=0, tiled=True)
    chosen = jnp.zeros((pad_rows, pad_cols), jnp.bfloat16)
    for number in range(8):
        share_rows, columns = pieces[number].shape
        amount = share_rows * columns
        rebuilt = incoming[:, :amount].reshape(devices * share_rows, columns)
        chosen = jnp.where(
            position == number * spacing, to_padded(rebuilt, pad_rows, pad_cols), chosen
        )
    ortho_own = orthogonalize(chosen)
    returning = jnp.zeros((devices, widest), jnp.bfloat16)
    for number in range(8):
        share_rows, columns = pieces[number].shape
        amount = share_rows * columns
        restored = from_padded(ortho_own, devices * share_rows, columns)
        placed = jnp.pad(restored.reshape(devices, amount), ((0, 0), (0, widest - amount)))
        returning = jnp.where(position == number * spacing, placed, returning)
    arrived = lax.all_to_all(returning, ("dp", "shard"), split_axis=0, concat_axis=0, tiled=True)
    for number in range(8):
        share_rows, columns = pieces[number].shape
        own_part = arrived[number * spacing, : share_rows * columns].reshape(share_rows, columns)
        steps_list.append(muon_step(own_part, masters[number], share_rows * devices, columns))
    step_qk = jnp.stack([steps_list[0], steps_list[1]])
    step_vg = jnp.stack([steps_list[2], steps_list[3]])
    step_out = steps_list[4]
    step_gu = jnp.stack([steps_list[5], steps_list[6]])
    step_dn = steps_list[7]
    new_one = BETA_ONE * moment_one + (1.0 - BETA_ONE) * small_grad
    new_two = BETA_TWO * moment_two + (1.0 - BETA_TWO) * small_grad * small_grad
    small_step = (
        -ADAM_RATE
        * (new_one / (1.0 - BETA_ONE**STEP_COUNT))
        / (jnp.sqrt(new_two / (1.0 - BETA_TWO**STEP_COUNT)) + ADAM_EPS)
    )
    my_start = starts[member]
    my_length = lengths[member]
    targets = (
        jnp.arange(group_size, dtype=jnp.int32)[:, None] * local_rows
        + jnp.arange(local_rows, dtype=jnp.int32)[None, :]
        - my_start
    )
    present = (targets >= 0) & (targets < my_length)
    rows_from = jnp.clip(targets, 0, capacity - 1)
    out_bf = block_y.astype(jnp.bfloat16)
    input_bf = d_input.astype(jnp.bfloat16)
    back_y = jnp.where(present[..., None], out_bf[rows_from], jnp.zeros((), jnp.bfloat16))
    back_dx = jnp.where(present[..., None], input_bf[rows_from], jnp.zeros((), jnp.bfloat16))
    got_y, got_dx = (
        lax.all_to_all(back_y, "shard", split_axis=0, concat_axis=0, tiled=True),
        lax.all_to_all(back_dx, "shard", split_axis=0, concat_axis=0, tiled=True),
    )
    block_out = jnp.sum(got_y.astype(jnp.float32), axis=0).astype(jnp.bfloat16)
    input_grad = jnp.sum(got_dx.astype(jnp.float32), axis=0).astype(jnp.bfloat16)
    return (
        block_out,
        input_grad,
        grad_qk,
        grad_vg,
        grad_out,
        grad_gu,
        grad_dn,
        step_qk,
        step_vg,
        step_out,
        step_gu,
        step_dn,
        mom_qk,
        mom_vg,
        mom_out,
        mom_gu,
        mom_dn,
        small_grad,
        small_step,
        new_one,
        new_two,
    )


def solution(mesh):
    return jax.shard_map(
        body,
        mesh=mesh,
        in_specs=(
            P(("dp", "shard"), None),
            P(("dp", "shard"), None),
            P(None, ("dp", "shard"), None),
            P(None, ("dp", "shard"), None),
            P(("dp", "shard"), None),
            P(None, ("dp", "shard"), None),
            P(("dp", "shard"), None),
            P(),
            P(None, ("dp", "shard"), None),
            P(None, ("dp", "shard"), None),
            P(("dp", "shard"), None),
            P(None, ("dp", "shard"), None),
            P(("dp", "shard"), None),
            P(),
            P(),
            P("dp", None),
        ),
        out_specs=(
            P(("dp", "shard"), None),
            P(("dp", "shard"), None),
            P(None, ("dp", "shard"), None),
            P(None, ("dp", "shard"), None),
            P(("dp", "shard"), None),
            P(None, ("dp", "shard"), None),
            P(("dp", "shard"), None),
            P(None, ("dp", "shard"), None),
            P(None, ("dp", "shard"), None),
            P(("dp", "shard"), None),
            P(None, ("dp", "shard"), None),
            P(("dp", "shard"), None),
            P(None, ("dp", "shard"), None),
            P(None, ("dp", "shard"), None),
            P(("dp", "shard"), None),
            P(None, ("dp", "shard"), None),
            P(("dp", "shard"), None),
            P(),
            P(),
            P(),
            P(),
        ),
        check_vma=False,
    )
```

profile of v0, /device:TPU:31, one launch (start us, length us, event | category | flops | bytes accessed | tf_op | source)
XLA Modules:
  0.0 2288.3 jit_solution(10119291036650976052)
XLA Ops:
  36.9 21.5 all-to-all-done
  58.4 7.2 all-to-all-start.2
  73.8 16.3 all-to-all-done.2
  145.3 9.0 all-gather.8.cloned.1.call-done
  154.3 5.9 convolution_bitcast_fusion.7
  178.6 57.5 %while.82 = (s32[]{:T(128)}, f32[8,128,256]{2,1,0:T(8,128)S(1)}, f32[4,8,64,256]{3,2,1,0:T(8,128)}, f32[4,8,128,256]{3,2,1,0:T(8,128)}, f32[4,8,64]{2,1,0:T(8,12...) while((s32[]{:T(128)}, f32[8,128,256]{2,1,0:T(8,128)S(1)}, ...), condition=%wide.region_13.14_spmd.clone, body=%wide.region_12.13_spmd.clone.sunk | while | flops 706740224 | bytes 12649916 | solution.py:163
  250.9 60.7 %all-gather.12.cloned.1.call-done = bf16[2,1024,2816]{2,1,0:T(8,128)(2,1)} async-done(((bf16[2,32,2816]{2,1,0:T(8,128)(2,1)}), bf16[2,1024,2816]{2,1,0:T(8,128)(2,1)}) %all-gather.12.cloned.1.call-update) | async-done | bytes 11534352 | tf_op jit(solution)/shard_map/all_gather | solution.py:413
  311.6 10.4 convolution_bitcast_fusion.5
  322.0 59.2 %all-gather.14.cloned.1.call-done = bf16[2816,1024]{1,0:T(8,128)(2,1)} async-done(((bf16[88,1024]{1,0:T(8,128)(2,1)}), bf16[2816,1024]{1,0:T(8,128)(2,1)}) %all-gather.14.cloned.1.call-update) | async-done | bytes 5767184 | tf_op jit(solution)/shard_map/all_gather | solution.py:414
  381.2 7.2 multiply_bitcast_fusion
  388.4 9.4 multiply_reduce_fusion.8
  414.8 87.3 %while.83 = (s32[]{:T(128)}, f32[8,128,256]{2,1,0:T(8,128)S(1)}, f32[4,8,64,256]{3,2,1,0:T(8,128)}, f32[4,8,64,128]{3,2,1,0:T(8,128)}, f32[4,8,64,128]{3,2,1,0:T...) while((s32[]{:T(128)}, f32[8,128,256]{2,1,0:T(8,128)S(1)}, ...), condition=%wide.region_22.23_spmd.clone, body=%wide.region_18.22_spmd.clone.sunk | while | flops 1412759552 | bytes 37546716 | solution.py:163
  515.3 9.7 convolution_bitcast_fusion.3
  572.9 34.2 %copy.514 = f32[2,1024,2816]{2,0,1:T(2,128)} copy(f32[2,1024,2816]{1,2,0:T(8,128)} %convolution_bitcast_fusion.3) | data formatting | bytes 46137344 | tf_op jit(solution)/shard_map/nd,snf->sdf/transpose | solution.py:271
  618.5 5.9 multiply_reduce_fusion.4
  640.5 5.6 multiply_reduce_fusion.10
  655.0 13.7 copy.510
  672.7 8.4 convolution_bitcast_fusion.4
  681.1 25.8 %copy.512 = f32[2,1024,2048]{2,0,1:T(2,128)} copy(f32[2,1024,2048]{1,2,0:T(8,128)} %convolution_bitcast_fusion.4) | data formatting | bytes 33554432 | tf_op jit(solution)/shard_map/nd,snc->sdc/transpose | solution.py:301
  707.8 6.0 convolution_bitcast_fusion.10
  720.4 5.7 fusion.237
  727.3 8.7 fusion.139
  736.1 234.9 %all-reduce.53.cloned.1.call-done = f32[2,1024,2816]{2,0,1:T(2,128)} async-done(((f32[2,1024,2816]{2,0,1:T(2,128)}), f32[2,1024,2816]{2,0,1:T(2,128)}) %all-reduce.53.cloned.1.call-update) | async-done | bytes 23068688
  977.1 396.9 %all-reduce.55.cloned.1.call-done = (f32[2,1024,1024]{2,0,1:T(2,128)}, f32[2,1024,2048]{2,0,1:T(2,128)}, f32[35088]{0:T(1024)}) async-done(((f32[2,1024,1024]{2,0,1:T(2,128)}, f32[2,1024,2048]{2,0,1:T(2,128)}, f32[35088]{0:T(1024)}), (f32[2,1024,1024]{2,0,1:T(2,128)}, f32[2,1024,2048]{2,0,1:T(2,128)}, f32[35088]{0:T(1024)})) %all-reduce.55.cloned.1.call-update) | async-done | bytes 25306192
  1386.8 7.9 scatter.29
  1394.7 7.5 scatter.30
  1402.1 7.5 scatter.31
  1409.7 113.0 %reduce-scatter.3.cloned.1.call-done = f32[64,1024]{1,0:T(8,128)} async-done(((f32[2048,1024]{1,0:T(8,128)}), f32[64,1024]{1,0:T(8,128)}) %reduce-scatter.3.cloned.1.call-update) | async-done | bytes 262160 | tf_op jit(solution)/shard_map/reduce_scatter | solution.py:430
  1524.7 7.5 scatter.34
  1532.2 7.5 scatter.35
  1539.7 7.5 scatter.36
  1547.2 131.1 %reduce-scatter.5.cloned.1.call-done = f32[88,1024]{1,0:T(8,128)} async-done(((f32[2816,1024]{1,0:T(8,128)}), f32[88,1024]{1,0:T(8,128)}) %reduce-scatter.5.cloned.1.call-update) | async-done | bytes 360464 | tf_op jit(solution)/shard_map/reduce_scatter | solution.py:432
  1680.3 7.5 scatter.39
  1688.3 8.7 reduce.66
  1697.0 8.2 reshape.1257
  1705.2 6.7 all-to-all-start.4
  1716.8 35.9 %while.81 = (s32[]{:T(128)}, f32[8,128,256]{2,1,0:T(8,128)S(1)}, f32[4,8,64,256]{3,2,1,0:T(8,128)}, f32[4,8,64]{1,2,0:T(8,128)}, f32[4,8,64]{2,1,0:T(8,128)}, /*...) while((s32[]{:T(128)}, f32[8,128,256]{2,1,0:T(8,128)S(1)}, ...), condition=%wide.region_7.8_spmd.clone, body=%wide.region_6.7_spmd.clone.sunk | while | flops 706412544 | bytes 8937175 | solution.py:163
  1776.1 63.8 %all-to-all-done.4 = bf16[32,2,45056]{2,1,0:T(2,128)(2,1)} async-done(((bf16[32,2,45056]{2,1,0:T(2,128)(2,1)}), bf16[32,2,45056]{2,1,0:T(2,128)(2,1)}, u32[]{:S(2)}, u32[]{:S(2)}) %all-to-all-start.4) | async-done | bytes 5767200 | tf_op jit(solution)/shard_map/all_to_all | solution.py:477
  1843.6 21.2 reshape.1258
  1864.7 35.3 %reduce.27 = bf16[32,90112]{1,0:T(8,128)(2,1)} reduce(bf16[32,1,90112]{2,1,0:T(2,128)(2,1)} %reshape.1258, bf16[]{:T(256)} %constant.624), dimensions={1}, to_apply=%all_to_all.54.reduce_sub_computation | reduce | bytes 11534338 | tf_op jit(solution)/shard_map/all_to_all | solution.py:477
  1900.0 10.6 copy.760
  1918.6 5.6 reshape.1141
  1924.2 6.9 reshape.1140
  1931.1 7.3 reshape.1139
  1940.8 6.5 copy.523
  1947.3 8.5 copy.522
  1955.8 12.4 fusion.109
  1968.9 10.6 fusion.293
  1979.5 14.7 add_convert_fusion.1
  1994.3 10.5 fusion.325
  2004.8 14.7 add_convert_fusion
  2019.5 7.0 reshape.1145
  2028.9 8.4 copy.524
  2037.2 6.9 reshape.1144
  2044.2 6.8 slice_bitcast_fusion.16
  2051.0 6.4 copy.525
  2057.4 5.6 reshape.1146
  2073.2 9.3 fusion.115
  2082.5 8.5 reduce.67
  2091.1 8.2 reshape.1259
  2099.3 6.0 all-to-all-start.5
  2114.9 118.4 %all-to-all-done.5 = bf16[32,2,45056]{2,1,0:T(2,128)(2,1)} async-done(((bf16[32,2,45056]{2,1,0:T(2,128)(2,1)}), bf16[32,2,45056]{2,1,0:T(2,128)(2,1)}, u32[]{:S(2)}, u32[]{:S(2)}) %all-to-all-start.5) | async-done | bytes 5767200 | tf_op jit(solution)/shard_map/all_to_all | solution.py:494
  2233.3 21.3 reshape.1260
  2259.2 10.6 copy.759
  (923 shorter events, 534.9 us)
Async XLA Ops:
  7.2 6.5 copy-start
  7.2 6.2 copy-start.197
  7.2 86.0 %all-gather.6.cloned.1.call-start = ((), (), s32[]{:S(2)}) async-start(), calls=%async_computation.8 | async-start | bytes 4325376 | tf_op jit(solution)/shard_map/all_gather | solution.py:410
  9.0 145.4 %all-gather.8.cloned.1.call-start = ((), (), s32[]{:S(2)}) async-start(), calls=%async_computation.9 | async-start | bytes 8650752 | tf_op jit(solution)/shard_map/all_gather | solution.py:411
  10.8 235.3 %all-gather.10.cloned.1.call-start = ((), (), s32[]{:S(2)}) async-start(), calls=%async_computation.10 | async-start | bytes 4325376 | tf_op jit(solution)/shard_map/all_gather | solution.py:412
  12.5 299.1 %all-gather.12.cloned.1.call-start = ((), (), s32[]{:S(2)}) async-start(), calls=%async_computation.11 | async-start | bytes 11894784 | tf_op jit(solution)/shard_map/all_gather | solution.py:413
  13.6 9.5 copy-start.193
  27.2 6.1 copy-start.137
  27.2 31.2 %all-to-all-start = ((bf16[4,256,1024]{2,1,0:T(8,128)(2,1)}), bf16[4,256,1024]{2,1,0:T(8,128)(2,1)}, u32[]{:S(2)}, u32[]{:S(2)}) async-start(bf16[4,256,1024]{2,1,0:T(8,128)(2,1)} %get-tuple-element.1509), calls=%async_computation | async-start | bytes 4194304 | tf_op jit(solution)/shard_map/all_to_all | solution.py:399
  32.6 348.6 %all-gather.14.cloned.1.call-start = ((), (), s32[]{:S(2)}) async-start(), calls=%async_computation.12 | async-start | bytes 5947392 | tf_op jit(solution)/shard_map/all_gather | solution.py:414
  36.1 86.0 %copy-start.138 = (f32[64,64]{0,1:T(8,128)}, f32[64,64]{0,1:T(8,128)S(1)}, u32[]{:S(2)}) copy-start(f32[64,64]{0,1:T(8,128)S(1)} %fusion.250) | copy-start | bytes 49156
  36.2 31.8 %copy-start.195 = (f32[8]{0:T(128)}, f32[8]{0:T(128)S(1)}, u32[]{:S(2)}) copy-start(f32[8]{0:T(128)S(1)} %get-tuple-element.1495) | copy-start | bytes 100
  36.8 31.0 %copy-start.163 = (f32[1024]{0:T(1024)}, f32[1024]{0:T(1024)S(1)}, u32[]{:S(2)}) copy-start(f32[1024]{0:T(1024)S(1)} %get-tuple-element.1490) | copy-start | bytes 12292
  36.8 60.6 %copy-start.165 = (f32[1024]{0:T(1024)}, f32[1024]{0:T(1024)S(1)}, u32[]{:S(2)}) copy-start(f32[1024]{0:T(1024)S(1)} %get-tuple-element.1489) | copy-start | bytes 12292
  36.8 60.6 %copy-start.167 = (f32[1024]{0:T(1024)}, f32[1024]{0:T(1024)S(1)}, u32[]{:S(2)}) copy-start(f32[1024]{0:T(1024)S(1)} %get-tuple-element.1485) | copy-start | bytes 12292
  36.9 60.6 %copy-start.169 = (f32[1024]{0:T(1024)}, f32[1024]{0:T(1024)S(1)}, u32[]{:S(2)}) copy-start(f32[1024]{0:T(1024)S(1)} %get-tuple-element.1482) | copy-start | bytes 12292
  36.9 60.6 %copy-start.171 = (f32[1024]{0:T(1024)}, f32[1024]{0:T(1024)S(1)}, u32[]{:S(2)}) copy-start(f32[1024]{0:T(1024)S(1)} %get-tuple-element.1486) | copy-start | bytes 12292
  36.9 60.6 %copy-start.173 = (f32[1024]{0:T(1024)}, f32[1024]{0:T(1024)S(1)}, u32[]{:S(2)}) copy-start(f32[1024]{0:T(1024)S(1)} %get-tuple-element.1483) | copy-start | bytes 12292
  36.9 60.6 %copy-start.175 = (f32[1024]{0:T(1024)}, f32[1024]{0:T(1024)S(1)}, u32[]{:S(2)}) copy-start(f32[1024]{0:T(1024)S(1)} %get-tuple-element.1487) | copy-start | bytes 12292
  36.9 60.6 %copy-start.177 = (f32[1024]{0:T(1024)}, f32[1024]{0:T(1024)S(1)}, u32[]{:S(2)}) copy-start(f32[1024]{0:T(1024)S(1)} %get-tuple-element.1484) | copy-start | bytes 12292
  36.9 60.6 %copy-start.179 = (f32[1024]{0:T(1024)}, f32[1024]{0:T(1024)S(1)}, u32[]{:S(2)}) copy-start(f32[1024]{0:T(1024)S(1)} %get-tuple-element.1488) | copy-start | bytes 12292
  36.9 478.3 %copy-start.135 = (f32[1024]{0:T(1024)}, f32[1024]{0:T(1024)S(1)}, u32[]{:S(2)}) copy-start(f32[1024]{0:T(1024)S(1)} %get-tuple-element.1481) | copy-start | bytes 12292
  58.4 31.7 %all-to-all-start.2 = ((bf16[4,256,1024]{2,1,0:T(8,128)(2,1)}), bf16[4,256,1024]{2,1,0:T(8,128)(2,1)}, u32[]{:S(2)}, u32[]{:S(2)}) async-start(bf16[4,256,1024]{2,1,0:T(8,128)(2,1)} %get-tuple-element.1508), calls=%async_computation.2 | async-start | bytes 4194304 | tf_op jit(solution)/shard_map/all_to_all | solution.py:400
  65.6 905.4 %all-reduce.53.cloned.1.call-start = ((), (), s32[]{:S(2)}) async-start(), calls=%async_computation.15 | async-start | bytes 46137344
  71.8 24.8 %copy-start.141 = (f32[4,64,8]{1,0,2:T(4,128)}, f32[4,64,8]{1,0,2:T(4,128)S(1)}, u32[]{:S(2)}) copy-start(f32[4,64,8]{1,0,2:T(4,128)S(1)} %reshape.1123) | copy-start | bytes 24580
  71.8 21.4 copy-start.34
  73.2 23.5 %copy-start.181 = (f32[4,8]{1,0:T(4,128)}, f32[4,8]{1,0:T(4,128)S(1)}, u32[]{:S(2)}) copy-start(f32[4,8]{1,0:T(4,128)S(1)} %slice_reduce_fusion.4) | copy-start | bytes 388
  101.9 6.2 copy-start.51
  113.6 8.6 copy-start.20
  116.1 6.1 copy-start.22
  117.3 7.0 copy-start.12
  118.5 7.7 copy-start.14
  120.0 8.2 copy-start.16
  322.0 66.4 %copy-start.62 = (f32[256,1024]{1,0:T(8,128)S(1)}, f32[256,1024]{1,0:T(8,128)}, u32[]{:S(2)}) copy-start(f32[256,1024]{1,0:T(8,128)} %get-tuple-element.1517) | copy-start | bytes 3145732
  388.4 9.5 copy-start.104
  388.4 9.5 copy-start.106
  388.4 9.5 copy-start.88
  502.1 8.0 copy-start.161
  515.3 9.7 copy-start.17
  607.1 766.8 %all-reduce.55.cloned.1.call-start = ((), (), s32[]{:S(2)}) async-start(), calls=%async_computation.16 | async-start | bytes 50618368
  618.5 6.3 copy-start.26
  624.9 8.7 copy-start.152
  625.6 11.5 copy-start.133
  655.0 13.7 copy-start.150
  681.1 26.6 %copy-start.91 = (bf16[1,256,2048]{2,1,0:T(8,128)(2,1)S(1)}, bf16[1,256,2048]{2,1,0:T(8,128)(2,1)}, u32[]{:S(2)}) copy-start(bf16[1,256,2048]{2,1,0:T(8,128)(2,1)} %get-tuple-element.1462) | copy-start | bytes 3145732
  681.1 26.6 %copy-start.103 = (bf16[1,256,2048]{2,1,0:T(8,128)(2,1)S(1)}, bf16[1,256,2048]{2,1,0:T(8,128)(2,1)}, u32[]{:S(2)}) copy-start(bf16[1,256,2048]{2,1,0:T(8,128)(2,1)} %copy-done.102) | copy-start | bytes 3145732
  707.7 6.0 copy-start.119
  719.2 803.5 %reduce-scatter.3.cloned.1.call-start = ((), (), s32[]{:S(2)}) async-start(), calls=%async_computation.13 | async-start | bytes 8650752 | tf_op jit(solution)/shard_map/reduce_scatter | solution.py:430
  726.1 952.2 %reduce-scatter.5.cloned.1.call-start = ((), (), s32[]{:S(2)}) async-start(), calls=%async_computation.14 | async-start | bytes 11894784 | tf_op jit(solution)/shard_map/reduce_scatter | solution.py:432
  736.0 234.9 %copy-start.108 = (f32[2,32,2816]{2,1,0:T(8,128)S(1)}, f32[2,32,2816]{2,1,0:T(8,128)}, u32[]{:S(2)}) copy-start(f32[2,32,2816]{2,1,0:T(8,128)} %param.49) | copy-start | bytes 2162692
  973.9 400.0 %copy-start.130 = (f32[2,32,1024]{2,1,0:T(8,128)S(1)}, f32[2,32,1024]{2,1,0:T(8,128)}, u32[]{:S(2)}) copy-start(f32[2,32,1024]{2,1,0:T(8,128)} %param.46) | copy-start | bytes 786436
  977.1 401.0 %copy-start.115 = (f32[2,32,2048]{2,1,0:T(8,128)S(1)}, f32[2,32,2048]{2,1,0:T(8,128)}, u32[]{:S(2)}) copy-start(f32[2,32,2048]{2,1,0:T(8,128)} %param.47) | copy-start | bytes 1572868
  1402.1 130.1 %copy-start.125 = (bf16[1,32,2816]{2,0,1:T(2,128)(2,1)S(1)}, bf16[1,32,2816]{2,0,1:T(2,128)(2,1)}, u32[]{:S(2)}) copy-start(bf16[1,32,2816]{2,0,1:T(2,128)(2,1)} %get-tuple-element.1478) | copy-start | bytes 540676
  1402.1 137.6 %copy-start.124 = (bf16[1,32,2816]{2,0,1:T(2,128)(2,1)S(1)}, bf16[1,32,2816]{2,0,1:T(2,128)(2,1)}, u32[]{:S(2)}) copy-start(bf16[1,32,2816]{2,0,1:T(2,128)(2,1)} %get-tuple-element.1477) | copy-start | bytes 540676
  1705.2 6.8 copy-start.198
  1705.2 7.3 copy-start.194
  1705.2 134.6 %all-to-all-start.4 = ((bf16[32,2,45056]{2,1,0:T(2,128)(2,1)}), bf16[32,2,45056]{2,1,0:T(2,128)(2,1)}, u32[]{:S(2)}, u32[]{:S(2)}) async-start(bf16[32,2,45056]{2,1,0:T(2,128)(2,1)} %reshape.1257), calls=%async_computation.6 | async-start | bytes 11534336 | tf_op jit(solution)/shard_map/all_to_all | solution.py:477
  1754.7 7.4 slice-start.1
  1839.8 228.9 %all-to-all-start.3 = ((bf16[4,128,1024]{2,1,0:T(8,128)(2,1)}), bf16[4,128,1024]{2,1,0:T(8,128)(2,1)S(1)}, u32[]{:S(2)}, u32[]{:S(2)}) async-start(bf16[4,128,1024]{2,1,0:T(8,128)(2,1)} %get-tuple-element.1510), calls=%async_computation.3 | async-start | bytes 2097152 | tf_op jit(solution)/shard_map/all_to_all | solution.py:526
  1947.3 8.5 copy-start.82
  2019.5 7.0 slice-start
  2068.7 13.8 copy-start.97
  2068.7 30.5 %all-to-all-start.1 = ((bf16[4,128,1024]{2,1,0:T(8,128)(2,1)}), bf16[4,128,1024]{2,1,0:T(8,128)(2,1)}, u32[]{:S(2)}, u32[]{:S(2)}) async-start(bf16[4,128,1024]{2,1,0:T(8,128)(2,1)} %get-tuple-element.1511), calls=%async_computation.1 | async-start | bytes 2097152 | tf_op jit(solution)/shard_map/all_to_all | solution.py:525
  2099.3 134.0 %all-to-all-start.5 = ((bf16[32,2,45056]{2,1,0:T(2,128)(2,1)}), bf16[32,2,45056]{2,1,0:T(2,128)(2,1)}, u32[]{:S(2)}, u32[]{:S(2)}) async-start(bf16[32,2,45056]{2,1,0:T(2,128)(2,1)} %reshape.1259), calls=%async_computation.7 | async-start | bytes 11534336 | tf_op jit(solution)/shard_map/all_to_all | solution.py:494
  (163 other events, 433.2 us)
Sparse Core Ops, SparseCore 0:
  11.6 61.8 all-gather.5
  77.0 77.3 all-gather.7
  157.8 60.5 all-gather.9
  221.9 89.6 all-gather.11
  314.9 66.2 all-gather.13
  607.3 363.6 all-reduce.52
  978.0 395.9 all-reduce.54
  1376.8 145.8 reduce-scatter.2
  1525.6 152.6 reduce-scatter.4
where the time goes:
time: 2300 us; the launch traced here: 2290 us
  waiting for transfers between devices  1220 us (53%)
  local copies, waits for them, and re-layouts  443 us (19%)
  matrix products  378 us (16%)
  other arithmetic  190 us (8%)
  starting transfers between devices  34 us (1%)
    unnamed x11, waiting for transfers between devices  632 us
    unnamed x440, local copies, waits for them, and re-layouts  132 us
    reduce_scatter x1, waiting for transfers between devices, body(): lax.psum_scatter(local_down, ('dp', 'shard'), scatter_dimension=0, tiled=...  131 us
    all_to_all x1, waiting for transfers between devices, body(): lax.all_to_all(returning, ('dp', 'shard'), split_axis=0, concat_axis=0, t...  118 us
    reduce_scatter x1, waiting for transfers between devices, body(): lax.psum_scatter(local_out, ('dp', 'shard'), scatter_dimension=0, tiled=T...  113 us
    all_to_all x1, waiting for transfers between devices, body(): lax.all_to_all(outgoing, ('dp', 'shard'), split_axis=0, concat_axis=0, ti...  63.8 us
    all_gather x1, waiting for transfers between devices, body(): lax.all_gather(cast_gu, ('dp', 'shard'), axis=1, tiled=True)  60.7 us
    all_gather x1, waiting for transfers between devices, body(): lax.all_gather(cast_down, ('dp', 'shard'), axis=0, tiled=True)  59.2 us
  transfers between devices with their start and end apart: 15, of which 11 were waited for; matrix products, arithmetic and copies ran while one was open for 30% of the time, Pallas kernels for 0%

commit v1 on v0

v1 whole, which is shorter than its diff:
```python
import functools
import math

import jax
import jax.numpy as jnp
from jax import lax
from jax.experimental import pallas as pl
from jax.experimental.pallas import tpu as pltpu
from jax.sharding import PartitionSpec as P

DK=128; DV=256; KCONV=4; CH=128
f32=jnp.float32; bf16=jnp.bfloat16
HI=lax.Precision.HIGHEST
GATE_EPS=1e-5; UNIT_EPS=1e-6

def _split(a):
    h=a.astype(bf16)
    return h,(a-h.astype(f32)).astype(bf16)

def dot(a,b,ca,cb,passes=3):
    dn=(((ca,),(cb,)),((),()))
    if passes==6:
        return lax.dot_general(a,b,dn,precision=HI,preferred_element_type=f32)
    if passes==1:
        return lax.dot_general(a.astype(bf16),b.astype(bf16),dn,preferred_element_type=f32)
    ah,al=_split(a); bh,bl=_split(b)
    g=functools.partial(lax.dot_general,dimension_numbers=dn,preferred_element_type=f32)
    return g(ah,bh)+(g(ah,bl)+g(al,bh))

def softplus(x): return jnp.maximum(x,0.0)+jnp.log1p(jnp.exp(-jnp.abs(x)))
def sigmoid(x): return lax.logistic(x)

def iota2(n,ax): return lax.broadcasted_iota(jnp.int32,(n,n),ax)

def inverse(A,p):
    n=A[0].shape[0]
    ri=iota2(n,0); ci=iota2(n,1)
    eye=(ri==ci).astype(f32)
    same=lambda b:(ri//b)==(ci//b)
    pw=[jnp.where(same(16),a,0.0) for a in A]
    X=[eye-q for q in pw]
    for _ in range(3):
        pw=[dot(q,q,1,0,p) for q in pw]
        X=[x+dot(x,q,1,0,p) for x,q in zip(X,pw)]
    b=16
    while b<n:
        m=jnp.logical_and(same(2*b),jnp.logical_not(same(b)))
        off=[jnp.where(m,a,0.0) for a in A]
        t=[dot(o,x,1,0,p) for o,x in zip(off,X)]
        X=[x-dot(x,q,1,0,p) for x,q in zip(X,t)]
        b*=2
    return X

def conv_pre(u,taps,info):
    s=taps[3:4]*u
    for k in (1,2,3):
        s=s+taps[3-k:4-k]*(pltpu.roll(u,k,0)*info[:,k:k+1])
    return s

def l2(u):
    return lax.rsqrt(jnp.sum(u*u,axis=-1,keepdims=True)+UNIT_EPS)

def acts(raw,taps,info,nh):
    out=[]
    kq=nh*DK
    for h in range(nh):
        d={}
        for nm,off,w in (("q",h*DK,DK),("k",kq+h*DK,DK),("v",2*kq+h*DV,DV)):
            pre=conv_pre(raw[:,off:off+w],taps[:,off:off+w],info)
            act=pre*sigmoid(pre)
            d[nm+"pre"]=pre; d[nm]=act
        rq=l2(d["q"])*(DK**-0.5); rk=l2(d["k"])
        d["rq"]=rq; d["rk"]=rk
        d["qn"]=d["q"]*rq; d["kn"]=d["k"]*rk
        out.append(d)
    return out

def decays(small,vec,nh):
    z=small+vec[1:2]
    ld=-vec[0:1]*softplus(z)
    beta=sigmoid(small)
    return z,ld,beta

def chunk_terms(ld,segc,segr,R,nh):
    n=CH
    ri=iota2(n,0); ci=iota2(n,1)
    low=(ri>=ci)
    L=low.astype(f32)
    out=[]
    for c in range(R//n):
        sl=slice(c*n,(c+1)*n)
        ldc=ld[sl]
        cc=dot(L,ldc,1,0,6)
        cr=dot(ldc,L,0,1,6)
        sc=segc[sl]; sr=segr[:,sl]
        M=jnp.logical_and(low,sc==sr)
        prev=segc[c*n-1:c*n] if c else None
        last=segc[(c+1)*n-1:(c+1)*n]
        heads=[]
        for h in range(nh):
            col=cc[:,h:h+1]; row=cr[h:h+1,:]
            R_=jnp.where(M,jnp.exp(jnp.where(M,col-row,0.0)),0.0)
            end=cc[n-1:n,h:h+1]
            t=jnp.where(sc==last,jnp.exp(end-col),0.0)
            if c:
                e=jnp.where(sc==prev,jnp.exp(col),0.0)
                g=jnp.where(last==prev,jnp.exp(end),0.0)
            else:
                e=jnp.zeros_like(col); g=jnp.zeros_like(end)
            heads.append((R_,e,t,g))
        out.append(heads)
    return out

def mixer_fwd(raw,small,taps,vec,gain,info,segr,nh,P):
    R=raw.shape[0]; nc=R//CH; n=CH
    segc=info[:,0:1]
    a=acts(raw,taps,info,nh)
    z,ld,beta=decays(small,vec,nh)
    terms=chunk_terms(ld,segc,segr,R,nh)
    ri=iota2(n,0); ci=iota2(n,1)
    strict=ri>ci
    idx=[(h,c) for c in range(nc) for h in range(nh)]
    sl=lambda c:slice(c*n,(c+1)*n)
    A=[];Pm=[]
    for h,c in idx:
        K=a[h]["kn"][sl(c)]; Q=a[h]["qn"][sl(c)]
        R_=terms[c][h][0]
        b=beta[sl(c),nh+h:nh+h+1]
        A.append(jnp.where(strict,b*R_*dot(K,K,1,1,P["kk"]),0.0))
        Pm.append(dot(Q,K,1,1,P["qk"])*R_)
    X=inverse(A,P["inv"])
    U0=[];W=[]
    for i,(h,c) in enumerate(idx):
        b=beta[sl(c),nh+h:nh+h+1]; e=terms[c][h][1]
        U0.append(dot(X[i],b*a[h]["v"][sl(c)],1,0,P["u"]))
        W.append(dot(X[i],(b*e)*a[h]["kn"][sl(c)],1,0,P["u"]) if c else None)
    S=[None]*nh
    S0s={};Us={};O={}
    for i,(h,c) in enumerate(idx):
        R_,e,t,g=terms[c][h]
        K=a[h]["kn"][sl(c)]; Q=a[h]["qn"][sl(c)]
        S0=S[h]
        U=U0[i] if c==0 else U0[i]-dot(W[i],S0,1,0,P["s"])
        o=dot(Pm[i],U,1,0,P["o"])
        if c: o=o+dot(e*Q,S0,1,0,P["o"])
        up=dot(t*K,U,0,0,P["s"])
        S[h]=up if c==0 else g*S0+up
        S0s[h,c]=S0; Us[h,c]=U; O[h,c]=o
    off=2*nh*DK+nh*DV
    gated={}
    for h,c in idx:
        o=O[h,c]
        r=lax.rsqrt(jnp.mean(o*o,axis=-1,keepdims=True)+GATE_EPS)
        gt=raw[sl(c),off+h*DV:off+(h+1)*DV]
        gated[h,c]=o*r*gain*(gt*sigmoid(gt))
    return gated,O,Us,S0s,{(h,c):X[i] for i,(h,c) in enumerate(idx)}

def mixer_bwd(raw,small,taps,vec,gain,info,segr,dgated,O,Us,S0s,X,nh,P):
    R=raw.shape[0]; nc=R//CH; n=CH
    segc=info[:,0:1]
    a=acts(raw,taps,info,nh)
    z,ld,beta=decays(small,vec,nh)
    terms=chunk_terms(ld,segc,segr,R,nh)
    ri=iota2(n,0); ci=iota2(n,1)
    strict=ri>ci
    U_=(ri<=ci).astype(f32)
    idx=[(h,c) for c in range(nc) for h in range(nh)]
    sl=lambda c:slice(c*n,(c+1)*n)
    off=2*nh*DK+nh*DV
    dO={};dgate={};ggain=None
    for h,c in idx:
        o=O[h,c]
        r=lax.rsqrt(jnp.mean(o*o,axis=-1,keepdims=True)+GATE_EPS)
        gt=raw[sl(c),off+h*DV:off+(h+1)*DV]
        s=sigmoid(gt); sg=gt*s
        dg=dgated[h,c]
        nrm=o*r
        dgate[h,c]=dg*nrm*gain*(s*(1.0+gt*(1.0-s)))
        dsn=dg*sg
        part=jnp.sum(dsn*nrm,axis=0,keepdims=True)
        ggain=part if ggain is None else ggain+part
        dn=dsn*gain
        dO[h,c]=r*dn-nrm*(r*jnp.mean(nrm*dn,axis=-1,keepdims=True))
    Pm={};dU0={};KK={};QK={}
    for h,c in idx:
        K=a[h]["kn"][sl(c)]; Q=a[h]["qn"][sl(c)]
        KK[h,c]=dot(K,K,1,1,P["kk"]); QK[h,c]=dot(Q,K,1,1,P["qk"])
        Pm[h,c]=QK[h,c]*terms[c][h][0]
        dU0[h,c]=dot(Pm[h,c],dO[h,c],0,0,P["u"])
    dS=[None]*nh
    dS1s={};Ys={}
    for c in reversed(range(nc)):
        for h in range(nh):
            R_,e,t,g=terms[c][h]
            K=a[h]["kn"][sl(c)]; Q=a[h]["qn"][sl(c)]
            b=beta[sl(c),nh+h:nh+h+1]
            dS1=dS[h]
            dS1s[h,c]=dS1
            dU=dU0[h,c]
            if dS1 is not None: dU=dU+dot(t*K,dS1,1,0,P["s"])
            Y=dot(X[h,c],dU,0,0,P["s"])
            Ys[h,c]=Y
            if c:
                d0=dot(e*Q,dO[h,c],0,0,P["s"])-dot((b*e)*K,Y,0,0,P["s"])
                dS[h]=d0 if dS1 is None else g*dS1+d0
    dQ={};dK={};dV={};dbeta={};dld={}
    ones_r=jnp.ones((8,n),f32)
    for h,c in idx:
        R_,e,t,g=terms[c][h]
        K=a[h]["kn"][sl(c)]; Q=a[h]["qn"][sl(c)]; V=a[h]["v"][sl(c)]
        b=beta[sl(c),nh+h:nh+h+1]
        Y=Ys[h,c]; U=Us[h,c]; dS1=dS1s[h,c]; S0=S0s[h,c]
        dA=jnp.where(strict,-dot(Y,U,1,1,P["g"]),0.0)
        dP=dot(dO[h,c],U,1,1,P["g"])
        H=dP*R_
        Gr=dA*R_
        G=b*Gr
        dq=dot(H,K,1,0,P["g"])
        dk=dot(G,K,1,0,P["g"])+dot(G,K,0,0,P["g"])+dot(H,Q,0,0,P["g"])
        dV[h,c]=b*Y
        db=jnp.sum(Y*V,axis=-1,keepdims=True)+jnp.sum(Gr*KK[h,c],axis=-1,keepdims=True)
        Z=H*QK[h,c]+G*KK[h,c]
        dc=jnp.sum(Z,axis=-1,keepdims=True)-jnp.sum(Z.T,axis=-1,keepdims=True)
        last=(lax.broadcasted_iota(jnp.int32,(n,1),0)==n-1).astype(f32)
        if c:
            YS=dot(Y,S0,1,1,P["g"]); OS=dot(dO[h,c],S0,1,1,P["g"])
            dq=dq+e*OS
            dk=dk-(b*e)*YS
            ks=jnp.sum(YS*K,axis=-1,keepdims=True)
            qs=jnp.sum(OS*Q,axis=-1,keepdims=True)
            db=db-e*ks
            dc=dc+e*(qs-b*ks)
        if dS1 is not None:
            US=dot(U,dS1,1,1,P["g"])
            dk=dk+t*US
            tt=t*jnp.sum(US*K,axis=-1,keepdims=True)
            dc=dc-tt
            tot=jnp.sum(tt,axis=0,keepdims=True)
            if c:
                tot=tot+g*jnp.sum(jnp.sum(dS1*S0,axis=-1,keepdims=True),axis=0,keepdims=True)
            dc=dc+last*tot
        dQ[h,c]=dq; dK[h,c]=dk; dbeta[h,c]=db
        dld[h,c]=dc
    lane=lax.broadcasted_iota(jnp.int32,(n,128),1)
    dsm=[]
    for c in range(nc):
        acc_d=jnp.zeros((n,128),f32); acc_b=jnp.zeros((n,128),f32)
        for h in range(nh):
            acc_d=acc_d+jnp.where(lane==h,dld[h,c],0.0)
            acc_b=acc_b+jnp.where(lane==nh+h,dbeta[h,c],0.0)
        acc_d=dot(U_,acc_d,1,0,6)
        dsm.append((acc_d,acc_b))
    dldf=jnp.concatenate([x[0] for x in dsm],axis=0)
    dbf=jnp.concatenate([x[1] for x in dsm],axis=0)
    dz=-dldf*vec[0:1]*sigmoid(z)
    dsmall=dz+dbf*beta*(1.0-beta)
    g_dt=jnp.sum(dz,axis=0,keepdims=True)
    g_al=jnp.sum(dldf*ld,axis=0,keepdims=True)
    draw={};gt=[None]*0
    tapg=[[None]*0 for _ in range(4)]
    cols=[]
    for nm in ("q","k","v"):
        for h in range(nh):
            d=a[h]
            w=DV if nm=="v" else DK
            coff={"q":h*DK,"k":nh*DK+h*DK,"v":2*nh*DK+h*DV}[nm]
            dy=jnp.concatenate([{"q":dQ,"k":dK,"v":dV}[nm][h,c] for c in range(nc)],axis=0)
            if nm!="v":
                rho=d["r"+nm]; y=d[nm+"n"]
                if nm=="q":
                    dy=rho*dy-(y*(DK**0.5))*(l2(d["q"])*jnp.sum((y*(DK**0.5))*dy,axis=-1,keepdims=True)*(DK**-0.5))
                else:
                    dy=rho*(dy-y*jnp.sum(y*dy,axis=-1,keepdims=True))
            pre=d[nm+"pre"]; s=sigmoid(pre)
            dp=dy*(s*(1.0+pre*(1.0-s)))
            u=raw[:,coff:coff+w]; tp=taps[:,coff:coff+w]
            du=tp[3:4]*dp
            tg=[None]*4
            tg[3]=jnp.sum(dp*u,axis=0,keepdims=True)
            for k in (1,2,3):
                su=pltpu.roll(dp,dp.shape[0]-k,0)*info[:,3+k:4+k]
                du=du+tp[3-k:4-k]*su
                tg[3-k]=jnp.sum(su*u,axis=0,keepdims=True)
            cols.append((nm,h,du,tg))
    return cols,dgate,dsmall,g_dt,g_al,ggain

def m1_kernel(nh,P,raw_ref,small_ref,taps_ref,vec_ref,gain_ref,info_ref,segr_ref,gated_ref,o_ref,u_ref,s_ref,x_ref):
    gated,O,U,S0,X=mixer_fwd(raw_ref[...],small_ref[...],taps_ref[...],vec_ref[...],gain_ref[0:1],info_ref[...],segr_ref[0:1],nh,P)
    n=CH
    for (h,c) in gated:
        r=slice(c*n,(c+1)*n); co=slice(h*DV,(h+1)*DV)
        gated_ref[r,co]=gated[h,c].astype(bf16)
        o_ref[r,co]=O[h,c]; u_ref[r,co]=U[h,c]
        x_ref[c*nh+h]=X[h,c]
        s_ref[c*nh+h]=S0[h,c] if c else jnp.zeros((DK,DV),f32)

def m1(raw,small,taps,vec,gain,info,segr,P):
    R=raw.shape[0]; nh=raw.shape[1]//(2*DK+2*DV); nb=nh*R//CH
    vm=pl.BlockSpec(memory_space=pltpu.VMEM)
    return pl.pallas_call(functools.partial(m1_kernel,nh,P),
      out_shape=[jax.ShapeDtypeStruct((R,nh*DV),bf16),jax.ShapeDtypeStruct((R,nh*DV),f32),jax.ShapeDtypeStruct((R,nh*DV),f32),
                 jax.ShapeDtypeStruct((nb,DK,DV),f32),jax.ShapeDtypeStruct((nb,CH,CH),f32)],
      in_specs=[vm]*7,out_specs=[vm]*5,
      compiler_params=pltpu.CompilerParams(vmem_limit_bytes=56<<20),name="mixer_forward")(raw,small,taps,vec,gain,info,segr)

def m2_kernel(nh,P,raw_ref,small_ref,taps_ref,vec_ref,gain_ref,info_ref,segr_ref,dg_ref,o_ref,u_ref,s_ref,x_ref,
              draw_ref,dsmall_ref,gt_ref,gv_ref,gg_ref):
    n=CH; R=raw_ref.shape[0]; nc=R//n
    g=lambda ref:{(h,c):ref[c*n:(c+1)*n,h*DV:(h+1)*DV] for h in range(nh) for c in range(nc)}
    b=lambda ref:{(h,c):ref[c*nh+h] for h in range(nh) for c in range(nc)}
    cols,dgate,dsmall,g_dt,g_al,gg=mixer_bwd(raw_ref[...],small_ref[...],taps_ref[...],vec_ref[...],gain_ref[0:1],info_ref[...],segr_ref[0:1],
       g(dg_ref),g(o_ref),g(u_ref),b(s_ref),b(x_ref),nh,P)
    gt_ref[...]=jnp.zeros_like(gt_ref)
    for nm,h,du,tg in cols:
        w=DV if nm=="v" else DK
        co={"q":h*DK,"k":nh*DK+h*DK,"v":2*nh*DK+h*DV}[nm]
        draw_ref[:,co:co+w]=du.astype(bf16)
        for i in range(4): gt_ref[i:i+1,co:co+w]=tg[i]
    off=2*nh*DK+nh*DV
    for h,c in dgate: draw_ref[c*n:(c+1)*n,off+h*DV:off+(h+1)*DV]=dgate[h,c].astype(bf16)
    dsmall_ref[...]=dsmall
    gv_ref[...]=jnp.zeros_like(gv_ref)
    gv_ref[0:1]=g_al; gv_ref[1:2]=g_dt
    gg_ref[...]=jnp.zeros_like(gg_ref)
    gg_ref[0:1]=gg

def m2(raw,small,taps,vec,gain,info,segr,dgated,O,U,S,X,P):
    R=raw.shape[0]; nh=raw.shape[1]//(2*DK+2*DV); nb=nh*R//CH
    vm=pl.BlockSpec(memory_space=pltpu.VMEM)
    return pl.pallas_call(functools.partial(m2_kernel,nh,P),
      out_shape=[jax.ShapeDtypeStruct((R,raw.shape[1]),bf16),jax.ShapeDtypeStruct((R,128),f32),jax.ShapeDtypeStruct((8,nh*(2*DK+DV)),f32),
                 jax.ShapeDtypeStruct((8,128),f32),jax.ShapeDtypeStruct((8,DV),f32)],
      in_specs=[vm]*12,out_specs=[vm]*5,
      compiler_params=pltpu.CompilerParams(vmem_limit_bytes=56<<20),name="mixer_backward")(raw,small,taps,vec,gain,info,segr,dgated,O,U,S,X)


f32=jnp.float32; bf16=jnp.bfloat16
MESH=pl.DeviceIdType.MESH
ANY=pl.BlockSpec(memory_space=pl.ANY)
VM=pl.BlockSpec(memory_space=pltpu.VMEM)

def place():
    d=lax.axis_index("dp"); s=lax.axis_index("shard")
    return d,s,d//2,d%2

def greet(peers):
    bar=pltpu.get_barrier_semaphore()
    for p in peers:
        pl.semaphore_signal(bar,inc=1,device_id=p,device_id_type=MESH)
    pl.semaphore_wait(bar,len(peers))

def remote(src,dst,ss,rs,dev):
    return pltpu.make_async_remote_copy(src_ref=src,dst_ref=dst,send_sem=ss,recv_sem=rs,device_id=dev,device_id_type=MESH)

def gather_kernel(n_dp,n_s,ncol,nrow,nact,order,W,*refs):
    n=ncol+nrow+nact
    ins=refs[:n]; outs=refs[n:2*n]
    s0,r0,s1,r1,sa,ra,lsem=refs[2*n:]
    d,s,hi,lo=place()
    n_hi=n_dp//2
    np_=ncol+nrow
    me=d*n_s+s
    td=me%n_dp; ts=me//n_dp
    fd=(s*n_dp+d)//n_s; fs=(s*n_dp+d)%n_s
    zs=[((hi+j)%n_hi)*2+lo for j in range(1,n_hi)]
    xd=hi*2+(1-lo)
    grp=[(d,(s+j)%n_s) for j in range(1,n_s)]
    bar=pltpu.get_barrier_semaphore()
    peers=grp+[(z,s) for z in zs]+[(xd,s)]
    moved=jnp.logical_or(td!=d,ts!=s)
    for p in peers:
        pl.semaphore_signal(bar,inc=1,device_id=p,device_id_type=MESH)
    @pl.when(moved)
    def _():
        pl.semaphore_signal(bar,inc=1,device_id=(td,ts),device_id_type=MESH)
        pl.semaphore_signal(bar,inc=1,device_id=(fd,fs),device_id_type=MESH)
    @pl.when(moved)
    def _():
        pl.semaphore_wait(bar,len(peers)+2)
    @pl.when(jnp.logical_not(moved))
    def _():
        pl.semaphore_wait(bar,len(peers))
    sends=[]
    local=[]
    for k in range(nact):
        src=ins[np_+k]; dst=outs[np_+k]
        c=pltpu.make_async_copy(src,dst.at[s],lsem.at[np_+k]); c.start(); local.append(c)
        for j,p in enumerate(grp):
            c=remote(src,dst.at[s],sa.at[k,j],ra.at[k,j],p); c.start(); sends.append(c)
    col={}
    def phase0(k):
        if k<ncol:
            c=pltpu.make_async_copy(ins[k].at[s],outs[k].at[d,s],lsem.at[k]); c.start()
            col[k]=[c]
            for j,p in enumerate(grp):
                c=remote(ins[k].at[p[1]],outs[k].at[d,s],s0.at[k,j],r0.at[k,j],p); c.start(); col[k].append(c)
        else:
            @pl.when(moved)
            def _():
                remote(ins[k],outs[k].at[td],s0.at[k,0],r0.at[k,0],(td,ts)).start()
            @pl.when(jnp.logical_not(moved))
            def _():
                pltpu.make_async_copy(ins[k],outs[k].at[d],r0.at[k,0]).start()
    def ready(k):
        if k<ncol:
            for c in col[k]: c.wait()
        else:
            pltpu.make_async_copy(ins[k],outs[k].at[d],r0.at[k,0]).wait()
            @pl.when(moved)
            def _():
                remote(ins[k],outs[k].at[td],s0.at[k,0],r0.at[k,0],(td,ts)).wait_send()
    pieces=[]
    for k,_,_ in order:
        if k not in pieces: pieces.append(k)
    for k in pieces: phase0(k)
    def blk(i,src):
        k,a,m=order[i]
        return outs[k].at[src,a:a+m] if m else outs[k].at[src]
    def first(i):
        own=blk(i,d)
        for j,z in enumerate(zs):
            remote(own,own,s1.at[i,j],r1.at[i,j],(z,s)).start()
        remote(own,own,s1.at[i,n_hi-1],r1.at[i,n_hi-1],(xd,s)).start()
    def second(i):
        for j in range(1,n_hi):
            b=blk(i,((hi-j)%n_hi)*2+lo)
            remote(b,b,s1.at[i,j-1],r1.at[i,j-1],(xd,s)).wait()
            remote(b,b,s1.at[i,n_hi-1+j],r1.at[i,n_hi-1+j],(xd,s)).start()
    def third(i):
        for j in range(n_hi):
            b=blk(i,((hi-j)%n_hi)*2+(1-lo))
            remote(b,b,s1.at[i,n_hi-1+j],r1.at[i,n_hi-1+j],(xd,s)).wait()
    done=set()
    nch=len(order)
    for i in range(nch+W+1):
        if i<nch:
            k=order[i][0]
            if k not in done:
                ready(k); done.add(k)
            first(i)
        if 0<=i-W<nch: second(i-W)
        if 0<=i-W-1<nch: third(i-W-1)
    for k in range(nact): local[k].wait()
    for c in sends: c.wait()

def gather(cols,rows,acts,n_dp,n_s,cid,order,W=1):
    pieces=list(cols)+list(rows); np_=len(pieces); n_hi=n_dp//2
    shapes=[jax.ShapeDtypeStruct((n_dp,)+x.shape,x.dtype) for x in pieces]+[jax.ShapeDtypeStruct((n_s,)+x.shape,x.dtype) for x in acts]
    D=pltpu.SemaphoreType.DMA
    na=max(len(acts),1); nch=len(order)
    return pl.pallas_call(functools.partial(gather_kernel,n_dp,n_s,len(cols),len(rows),len(acts),order,W),
        out_shape=shapes,in_specs=[ANY]*(np_+len(acts)),out_specs=[ANY]*(np_+len(acts)),
        scratch_shapes=[D((np_,n_s)),D((np_,n_s)),D((nch,2*n_hi)),D((nch,2*n_hi)),D((na,n_s)),D((na,n_s)),D((np_+na,))],
        compiler_params=pltpu.CompilerParams(collective_id=cid,has_side_effects=True),name="gather_weights")(*pieces,*acts)

NORM_EPS=1e-6
D_=pltpu.SemaphoreType.DMA
def ring(n_s):
    d,s,_,_=place()
    return [(d,(s+j)%n_s) for j in range(1,n_s)]

def push_parts(n_s,part,land,ss,rs):
    cs=[]
    for j,p in enumerate(ring(n_s)):
        c=remote(part.at[p[1]],land.at[j],ss.at[j],rs.at[j],p); c.start(); cs.append(c)
    return cs

def push_all(n_s,out,ss,rs):
    _,s,_,_=place()
    cs=[]
    for j,p in enumerate(ring(n_s)):
        c=remote(out.at[s],out.at[s],ss.at[j],rs.at[j],p); c.start(); cs.append(c)
    return cs

def add_up(n_s,part,land):
    _,s,_,_=place()
    t=part[s].astype(f32)
    for j in range(n_s-1): t=t+land[j].astype(f32)
    return t

def norm_back(u,g,dn):
    w=u.shape[-1]
    r=lax.rsqrt(jnp.mean(u*u,axis=-1,keepdims=True)+NORM_EPS)
    gd=g*dn
    du=r*gd-u*(r*r*r*(jnp.sum(u*gd,axis=-1,keepdims=True)/w))
    return du,jnp.sum(u*r*dn,axis=0,keepdims=True)

def mid_kernel(n_s,part,x,gain,middle,gathered,land,s0,r0,s1,r1):
    _,s,_,_=place()
    greet(ring(n_s))
    a=push_parts(n_s,part,land,s0,r0)
    for c in a: c.wait()
    m=x[...].astype(f32)+add_up(n_s,part,land)
    middle[...]=m
    r=lax.rsqrt(jnp.mean(m*m,axis=-1,keepdims=True)+NORM_EPS)
    gathered[s]=(m*r*gain[0:1]).astype(bf16)
    for c in push_all(n_s,gathered,s1,r1): c.wait()

def mid(part,x,gain,n_s,cid):
    rows,w=x.shape
    return pl.pallas_call(functools.partial(mid_kernel,n_s),
        out_shape=[jax.ShapeDtypeStruct((rows,w),f32),jax.ShapeDtypeStruct((n_s,rows,w),bf16)],
        in_specs=[VM]*3,out_specs=[VM]*2,
        scratch_shapes=[pltpu.VMEM((n_s-1,rows,w),bf16)]+[D_((n_s,))]*4,
        compiler_params=pltpu.CompilerParams(collective_id=cid,has_side_effects=True,vmem_limit_bytes=40<<20),name="branch_sum")(part,x,gain)

def ffn_kernel(n_s,ypart,dpart,middle,dy,gain,out,dmid,gathered,dgain,yland,dland,s0,r0,s1,r1,s2,r2):
    _,s,_,_=place()
    greet(ring(n_s))
    b=push_parts(n_s,dpart,dland,s1,r1)
    for c in b: c.wait()
    a=push_parts(n_s,ypart,yland,s0,r0)
    m=middle[...]
    du,dg=norm_back(m,gain[0:1],add_up(n_s,dpart,dland))
    dm=dy[...].astype(f32)+du
    dmid[...]=dm
    dgain[...]=jnp.broadcast_to(dg,dgain.shape)
    gathered[s]=dm.astype(bf16)
    g=push_all(n_s,gathered,s2,r2)
    for c in a: c.wait()
    out[...]=(m+add_up(n_s,ypart,yland)).astype(bf16)
    for c in g: c.wait()

def ffn(ypart,dpart,middle,dy,gain,n_s,cid):
    rows,w=middle.shape
    return pl.pallas_call(functools.partial(ffn_kernel,n_s),
        out_shape=[jax.ShapeDtypeStruct((rows,w),bf16),jax.ShapeDtypeStruct((rows,w),f32),jax.ShapeDtypeStruct((n_s,rows,w),bf16),
                   jax.ShapeDtypeStruct((8,w),f32)],
        in_specs=[VM]*5,out_specs=[VM]*4,
        scratch_shapes=[pltpu.VMEM((n_s-1,rows,w),bf16)]*2+[D_((n_s,))]*6,
        compiler_params=pltpu.CompilerParams(collective_id=cid,has_side_effects=True,vmem_limit_bytes=40<<20),name="block_sum")(ypart,dpart,middle,dy,gain)

def end_kernel(n_s,part,x,dmid,gain,out,dgain,land,s0,r0):
    greet(ring(n_s))
    for c in push_parts(n_s,part,land,s0,r0): c.wait()
    du,dg=norm_back(x[...].astype(f32),gain[0:1],add_up(n_s,part,land))
    out[...]=(dmid[...]+du).astype(bf16)
    dgain[...]=jnp.broadcast_to(dg,dgain.shape)

def end(part,x,dmid,gain,n_s,cid):
    rows,w=x.shape
    return pl.pallas_call(functools.partial(end_kernel,n_s),
        out_shape=[jax.ShapeDtypeStruct((rows,w),bf16),jax.ShapeDtypeStruct((8,w),f32)],
        in_specs=[VM]*4,out_specs=[VM]*2,
        scratch_shapes=[pltpu.VMEM((n_s-1,rows,w),bf16)]+[D_((n_s,))]*2,
        compiler_params=pltpu.CompilerParams(collective_id=cid,has_side_effects=True,vmem_limit_bytes=40<<20),name="input_sum")(part,x,dmid,gain)

def scatter_kernel(n_dp,n_s,ncol,nrow,W,*refs):
    n=ncol+nrow
    g=refs[:n]; outs=refs[n:2*n]
    xl=refs[2*n:3*n]; zb=refs[3*n:4*n]; zl=refs[4*n:5*n]; fin=refs[5*n:6*n]
    sx,rx,sz,rz,sf,rf,lsem=refs[6*n:]
    d,s,hi,lo=place()
    n_hi=n_dp//2
    me=s*n_dp+d
    td=me//n_s; ts=me%n_s
    own=d*n_s+s
    fd=own%n_dp; fs=own//n_dp
    moved=jnp.logical_or(td!=d,ts!=s)
    zs=[((hi+j)%n_hi)*2+lo for j in range(1,n_hi)]
    xd=hi*2+(1-lo)
    grp=ring(n_s)
    bar=pltpu.get_barrier_semaphore()
    peers=grp+[(z,s) for z in zs]+[(xd,s)]
    for p in peers:
        pl.semaphore_signal(bar,inc=1,device_id=p,device_id_type=MESH)
    @pl.when(moved)
    def _():
        pl.semaphore_signal(bar,inc=1,device_id=(td,ts),device_id_type=MESH)
        pl.semaphore_signal(bar,inc=1,device_id=(fd,fs),device_id_type=MESH)
    @pl.when(moved)
    def _():
        pl.semaphore_wait(bar,len(peers)+2)
    @pl.when(jnp.logical_not(moved))
    def _():
        pl.semaphore_wait(bar,len(peers))
    order=[(k,j) for k in range(n) for j in list(range(1,n_hi))+[0]]
    def xc(i):
        k,j=order[i]; z=(hi+j)%n_hi
        return remote(g[k].at[z*2+1-lo],xl[k].at[z],sx.at[k,j],rx.at[k,j],(xd,s))
    def zc(k,j):
        return remote(zb[k].at[j-1],zl[k].at[j-1],sz.at[k,j],rz.at[k,j],(((hi+j)%n_hi)*2+lo,s))
    fc={}
    nch=len(order)
    for i in range(nch+W):
        if i<nch: xc(i).start()
        if i>=W:
            k,j=order[i-W]; z=(hi+j)%n_hi
            xc(i-W).wait()
            t=g[k][z*2+lo].astype(f32)+xl[k][z].astype(f32)
            if j:
                zb[k][j-1]=t.astype(bf16); zc(k,j).start()
            else:
                for jj in range(1,n_hi):
                    zc(k,jj).wait()
                    t=t+zl[k][jj-1].astype(f32)
                t=t.astype(bf16)
                if k<ncol:
                    rows=t.shape[0]//n_s
                    fin[k][...]=t.reshape(n_s,rows,t.shape[1])
                    c=pltpu.make_async_copy(fin[k].at[s],outs[k].at[s],lsem.at[k]); c.start()
                    fc[k]=[c]
                    for jj,p in enumerate(grp):
                        c=remote(fin[k].at[p[1]],outs[k].at[s],sf.at[k,jj],rf.at[k,jj],p); c.start(); fc[k].append(c)
                else:
                    fin[k][...]=t
                    @pl.when(moved)
                    def _():
                        remote(fin[k],outs[k],sf.at[k,0],rf.at[k,0],(td,ts)).start()
                    @pl.when(jnp.logical_not(moved))
                    def _():
                        pltpu.make_async_copy(fin[k],outs[k],rf.at[k,0]).start()
    for k in range(n):
        if k<ncol:
            for c in fc[k]: c.wait()
        else:
            pltpu.make_async_copy(fin[k],outs[k],rf.at[k,0]).wait()
            @pl.when(moved)
            def _():
                remote(fin[k],outs[k],sf.at[k,0],rf.at[k,0],(td,ts)).wait_send()

def scatter(cols,rows,n_dp,n_s,cid,W=2):
    ps=list(cols)+list(rows); n=len(ps); nc=len(cols); n_hi=n_dp//2
    oshape=lambda k,x:(n_s,x.shape[1]//n_s,x.shape[2]) if k<nc else x.shape[1:]
    outs=[jax.ShapeDtypeStruct(oshape(k,x),bf16) for k,x in enumerate(ps)]
    V=pltpu.VMEM
    sc=[V((n_hi,)+x.shape[1:],bf16) for x in ps]+[V((n_hi-1,)+x.shape[1:],bf16) for x in ps]*2+[V(oshape(k,x),bf16) for k,x in enumerate(ps)]
    return pl.pallas_call(functools.partial(scatter_kernel,n_dp,n_s,nc,len(rows),W),
        out_shape=outs,in_specs=[VM]*n,out_specs=[VM]*n,
        scratch_shapes=sc+[D_((n,n_hi))]*4+[D_((n,n_s))]*2+[D_((n,))],
        compiler_params=pltpu.CompilerParams(collective_id=cid,has_side_effects=True,vmem_limit_bytes=60<<20),name="scatter_gradients")(*ps)


f32=jnp.float32; bf16=jnp.bfloat16
CA,CB,CC=3.4445,-4.775,2.0315
def dg(a,b,ca,cb): return lax.dot_general(a,b,(((ca,),(cb,)),((),())),preferred_element_type=f32)
TB=256
def ns_wide(x,y,g,p,cols,iters=2,tm=256,tn=512):
    r=g.shape[0]
    cs=slice(0,cols)
    def sq(i,a):
        v=x[pl.ds(i*TB,TB),cs].astype(f32)
        return a+jnp.sum(v*v,axis=0,keepdims=True)
    t=lax.fori_loop(0,r//TB,sq,jnp.zeros((1,cols),f32))
    inv=1.0/(jnp.sqrt(jnp.sum(t,axis=1,keepdims=True))+1e-7)
    def sc(i,_):
        x[pl.ds(i*TB,TB),cs]=(x[pl.ds(i*TB,TB),cs].astype(f32)*inv).astype(bf16)
        return 0
    lax.fori_loop(0,r//TB,sc,0)
    a,b=x,y
    for _ in range(iters):
        def gram(i,_):
            ri=pl.ds(pl.multiple_of(i*tm,tm),tm)
            g[ri,:]=dg(a[ri,cs],a[:,cs],1,1).astype(bf16)
            return 0
        lax.fori_loop(0,r//tm,gram,0)
        def poly(i,_):
            ri=pl.ds(pl.multiple_of(i*tm,tm),tm)
            p[ri,:]=(CB*g[ri,:].astype(f32)+CC*dg(g[ri,:],g[...],1,0)).astype(bf16)
            return 0
        lax.fori_loop(0,r//tm,poly,0)
        def nxt(i,_):
            ri=pl.ds(pl.multiple_of(i*tm,tm),tm)
            b[ri,cs]=(CA*a[ri,cs].astype(f32)+dg(p[ri,:],a[:,cs],1,0)).astype(bf16)
            return 0
        lax.fori_loop(0,r//tm,nxt,0)
        a,b=b,a
def ns_tall(x,y,g,p,n=None,iters=2,tm=256):
    n=n or x.shape[0]; r=x.shape[1]
    def sq(i,a):
        v=x[pl.ds(i*TB,TB),:].astype(f32)
        return a+jnp.sum(v*v,axis=0,keepdims=True)
    t=lax.fori_loop(0,n//TB,sq,jnp.zeros((1,r),f32))
    inv=1.0/(jnp.sqrt(jnp.sum(t,axis=1,keepdims=True))+1e-7)
    def sc(i,_):
        x[pl.ds(i*TB,TB),:]=(x[pl.ds(i*TB,TB),:].astype(f32)*inv).astype(bf16)
        return 0
    lax.fori_loop(0,n//TB,sc,0)
    a,b=x,y
    for _ in range(iters):
        for j in range(r//tm):
            cj=slice(j*tm,(j+1)*tm)
            g[cj,:]=dg(a[0:n,cj],a[0:n,:],0,0).astype(bf16)
        def poly(i,_):
            ri=pl.ds(pl.multiple_of(i*tm,tm),tm)
            p[ri,:]=(CB*g[ri,:].astype(f32)+CC*dg(g[ri,:],g[...],1,0)).astype(bf16)
            return 0
        lax.fori_loop(0,r//tm,poly,0)
        def nxt(i,_):
            ri=pl.ds(pl.multiple_of(i*tm,tm),tm)
            b[ri,:]=(CA*a[ri,:].astype(f32)+dg(a[ri,:],p[...],1,0)).astype(bf16)
            return 0
        lax.fori_loop(0,n//tm,nxt,0)
        a,b=b,a


def muon_owner(i,n_dp):
    base=n_dp//2-2
    d,s=((2,0),(3,0),(1,2),(3,2),(2,2),(0,0),(1,0),(0,2))[i]
    return base+d,s

def muon_kernel(n_dp,n_s,kinds,*refs):
    n=len(kinds)
    ins=refs[:n]; outs=refs[n:2*n]
    wide,wide2,tall,tall2,g,p,rin,sin,rout,sout,lsem=refs[2*n:]
    d,s,_,_=place()
    nd=n_dp*n_s
    me=d*n_s+s
    own=[muon_owner(i,n_dp) for i in range(n)]
    base=n_dp//2-2
    is_owner=lambda dd,ss: jnp.logical_and(jnp.logical_and(dd>=base,dd<base+4),ss%2==0)
    mine=is_owner(d,s)
    bar=pltpu.get_barrier_semaphore()
    for o in own:
        @pl.when(jnp.logical_or(d!=o[0],s!=o[1]))
        def _():
            pl.semaphore_signal(bar,inc=1,device_id=o,device_id_type=MESH)
    @pl.when(mine)
    def _():
        def greet_one(q,_):
            dd=q//n_s; ss=q%n_s
            @pl.when(jnp.logical_not(is_owner(dd,ss)))
            def _():
                pl.semaphore_signal(bar,inc=1,device_id=(dd,ss),device_id_type=MESH)
            return 0
        lax.fori_loop(0,nd,greet_one,0)
        pl.semaphore_wait(bar,nd-1)
    @pl.when(jnp.logical_not(mine))
    def _():
        pl.semaphore_wait(bar,n)
    def slot(buf,i,q):
        t,rows,cols=kinds[i]
        ds=pl.ds(pl.multiple_of(q*rows,rows),rows)
        return buf.at[ds] if t else buf.at[ds,pl.ds(0,cols)]
    for i in range(n):
        t,rows,cols=kinds[i]
        dst=slot(tall if t else wide,i,me)
        there=jnp.logical_and(d==own[i][0],s==own[i][1])
        @pl.when(there)
        def _():
            pltpu.make_async_copy(ins[i],dst,rin.at[0]).start()
        @pl.when(jnp.logical_not(there))
        def _():
            remote(ins[i],dst,sin.at[i],rin.at[0],own[i]).start()
    for i in range(n):
        t,rows,cols=kinds[i]
        there=jnp.logical_and(d==own[i][0],s==own[i][1])
        @pl.when(there)
        def _():
            buf=tall if t else wide
            full=buf.at[pl.ds(0,rows*nd)] if t else buf.at[:,pl.ds(0,cols)]
            pltpu.make_async_copy(full,full,rin.at[0]).wait()
            if t: ns_tall(tall,tall2,g,p,n=rows*nd)
            else: ns_wide(wide,wide2,g,p,cols,tm=512 if cols>1024 else 256)
            def send(q,_):
                src=slot(buf,i,q)
                @pl.when(q==me)
                def _():
                    pltpu.make_async_copy(src,outs[i],rout.at[i]).start()
                @pl.when(q!=me)
                def _():
                    remote(src,outs[i],sout.at[0],rout.at[i],(q//n_s,q%n_s)).start()
                return 0
            lax.fori_loop(0,nd,send,0)
            part=buf.at[pl.ds(0,rows*(nd-1))] if t else buf.at[pl.ds(0,rows*(nd-1)),pl.ds(0,cols)]
            pltpu.make_async_copy(part,part,sout.at[0]).wait()
    for i in range(n):
        there=jnp.logical_and(d==own[i][0],s==own[i][1])
        @pl.when(jnp.logical_not(there))
        def _():
            pltpu.make_async_copy(ins[i],ins[i],sin.at[i]).wait()
        pltpu.make_async_copy(ins[i],outs[i],rout.at[i]).wait()

def muon(looks,n_dp,n_s,cid):
    nd=n_dp*n_s
    kinds=[]
    for x in looks:
        r,c=x.shape
        kinds.append((r*nd>c,r,c))
    r=min(min(k[1]*nd,k[2]) for k in kinds)
    wc=max(k[2] for k in kinds if not k[0]); tr=max(k[1]*nd for k in kinds if k[0])
    V=pltpu.VMEM
    return pl.pallas_call(functools.partial(muon_kernel,n_dp,n_s,tuple(kinds)),
        out_shape=[jax.ShapeDtypeStruct(x.shape,bf16) for x in looks],in_specs=[VM]*8,out_specs=[VM]*8,
        scratch_shapes=[V((r,wc),bf16)]*2+[V((tr,r),bf16)]*2+[V((r,r),bf16)]*2+[D_((1,)),D_((8,)),D_((8,)),D_((1,)),D_((1,))],
        compiler_params=pltpu.CompilerParams(collective_id=cid,has_side_effects=True,vmem_limit_bytes=60<<20),name="muon")(*looks)


D = 1024
H = 8
STEP_COUNT = 10
MOMENTUM = 0.95
MUON_RATE = 0.1
MUON_DECAY = 0.01
ADAM_RATE = 0.05
BETA_ONE = 0.9
BETA_TWO = 0.95
ADAM_EPS = 1e-08
PASSES = dict(kk=3, qk=3, inv=3, u=3, s=3, o=3, g=3)


def unpack(packed):
    layouts = [(D, H), (D, H), (KCONV, H * DK), (KCONV, H * DK), (KCONV, H * DV), (D,), (D,), (DV,), (H,), (H,)]
    pieces = []
    offset = 0
    for layout in layouts:
        amount = math.prod(layout)
        pieces.append(packed[offset : offset + amount].reshape(layout))
        offset = offset + amount
    return pieces


def mm(a, b, ca, cb, kind=f32):
    return lax.dot_general(
        a, b, (((ca,), (cb,)), ((), ())), preferred_element_type=f32
    ).astype(kind)


def row_facts(lengths, rows):
    count = lengths.shape[0]
    ends = jnp.sum(jnp.where(jnp.arange(count)[:, None] >= jnp.arange(count)[None, :], lengths[None, :], 0), axis=1)
    pos = jnp.arange(rows, dtype=jnp.int32)

    def number(p):
        seg = jnp.sum((p[:, None] >= ends[None, :]).astype(jnp.int32), axis=1)
        return jnp.where(p < 0, -1, seg).astype(f32)

    seg = number(pos)
    cols = [seg]
    for k in (1, 2, 3):
        cols.append((number(pos - k) == seg).astype(f32))
    for k in (1, 2, 3):
        cols.append((number(pos + k) == seg).astype(f32))
    info = jnp.pad(jnp.stack(cols, axis=1), ((0, 0), (0, 128 - len(cols))))
    return info, jnp.broadcast_to(seg[None, :], (8, rows))


def top(rows, array):
    return jnp.pad(array, ((0, rows - array.shape[0]), (0, 0)))


def by_member(parts, n_s):
    split = [p.reshape(p.shape[0], n_s, p.shape[1] // n_s) for p in parts]
    return jnp.swapaxes(jnp.concatenate(split, axis=2), 0, 1)


def whole_rows(piece, widths):
    out = []
    at = 0
    for w in widths:
        p = jnp.swapaxes(piece[:, :, at : at + w], 0, 1)
        out.append(p.reshape(p.shape[0], -1))
        at += w
    return out


def body(
    n_dp,
    n_s,
    tokens,
    cotangent,
    query_key,
    value_gate,
    output_weight,
    gate_up,
    down_weight,
    small_params,
    momentum_query_key,
    momentum_value_gate,
    momentum_output,
    momentum_gate_up,
    momentum_down,
    moment_one,
    moment_two,
    seq_lengths,
):
    member = lax.axis_index("shard")
    nh = H // n_s
    local = tokens.shape[0]
    rows = local * n_s
    ff = gate_up.shape[2] // n_s
    (w_decay, w_beta, conv_query, conv_keys, conv_value, gain_one, gain_two, gain_out, a_log, dt_bias) = unpack(
        small_params
    )

    def mine(array, axis, size):
        return lax.dynamic_slice_in_dim(array, member * size, size, axis)

    def put(array, axis, full):
        shape = list(array.shape)
        shape[axis] = full
        return lax.dynamic_update_slice_in_dim(
            jnp.zeros(shape, array.dtype), array, member * array.shape[axis], axis
        )

    info, segr = row_facts(seq_lengths[0], rows)
    w_small = jnp.concatenate([mine(w_decay, 1, nh), mine(w_beta, 1, nh)], axis=1)
    w_small = jnp.pad(w_small, ((0, 0), (0, 128 - 2 * nh))).astype(bf16)
    taps = jnp.concatenate(
        [mine(conv_query, 1, nh * DK), mine(conv_keys, 1, nh * DK), mine(conv_value, 1, nh * DV)], axis=1
    )
    taps = top(8, taps)
    vec = jnp.stack([jnp.exp(mine(a_log, 0, nh)), mine(dt_bias, 0, nh)])
    vec = top(8, jnp.pad(vec, ((0, 0), (0, 128 - nh))))
    gain_o = top(8, gain_out[None])
    gain_1 = top(8, gain_one[None])
    gain_2 = top(8, gain_two[None])

    x = tokens.astype(f32)
    normed_own = (x * lax.rsqrt(jnp.mean(x * x, axis=-1, keepdims=True) + NORM_EPS) * gain_one).astype(bf16)
    cast = [
        by_member([query_key[0].astype(bf16), query_key[1].astype(bf16), value_gate[0].astype(bf16), value_gate[1].astype(bf16)], n_s),
        by_member([gate_up[0].astype(bf16), gate_up[1].astype(bf16)], n_s),
        output_weight.astype(bf16),
        down_weight.astype(bf16),
    ]
    order = [(0, i, 1) for i in range(n_s)] + [(2, 0, 0)] + [(1, i, 1) for i in range(n_s)] + [(3, 0, 0)]
    w_in, w_gu, w_out, w_dn, normed, dy = gather(
        cast[:2], cast[2:], [normed_own, cotangent], n_dp, n_s, 0, tuple(order)
    )
    w_in = w_in.reshape(D, -1)
    w_gu = w_gu.reshape(D, -1)
    w_out = w_out.reshape(-1, D)
    w_dn = w_dn.reshape(-1, D)
    normed = normed.reshape(rows, D)
    dy = dy.reshape(rows, D)

    raw = mm(normed, w_in, 1, 0)
    raw_small = mm(normed, w_small, 1, 0)
    gated, mixed, updates, states, inverses = m1(raw, raw_small, taps, vec, gain_o, info, segr, PASSES)
    part = mm(gated, w_out, 1, 0, bf16).reshape(n_s, local, D)
    middle, normed_two = mid(part, tokens, gain_2, n_s, 1)
    normed_two = normed_two.reshape(rows, D)
    gu = mm(normed_two, w_gu, 1, 0)
    gate = gu[:, :ff]
    upper = gu[:, ff:]
    sig = jax.nn.sigmoid(gate)
    hidden = (gate * sig * upper).astype(bf16)
    y_part = mm(hidden, w_dn, 1, 0, bf16).reshape(n_s, local, D)
    d_hidden = mm(dy, w_dn, 1, 1)
    d_gate = (d_hidden * upper * sig * (1.0 + gate * (1.0 - sig))).astype(bf16)
    d_upper = (d_hidden * (gate * sig)).astype(bf16)
    d_gu = jnp.concatenate([d_gate, d_upper], axis=1)
    d_part = mm(d_gu, w_gu, 1, 1, bf16).reshape(n_s, local, D)
    block_out, d_middle, d_branch, d_gain_two = ffn(y_part, d_part, middle, cotangent, gain_2, n_s, 2)
    d_branch = d_branch.reshape(rows, D)
    part_dn = mm(hidden, dy, 0, 0, bf16)
    part_gu = mm(normed_two, d_gu, 0, 0, bf16)
    part_out = mm(gated, d_branch, 0, 0, bf16)
    d_gated = mm(d_branch, w_out, 1, 1)
    d_raw, d_small, g_taps, g_vec, g_gain = m2(
        raw, raw_small, taps, vec, gain_o, info, segr, d_gated, mixed, updates, states, inverses, PASSES
    )
    d_small = d_small.astype(bf16)
    part_in = mm(normed, d_raw, 0, 0, bf16)
    part_small = mm(normed, d_small, 0, 0)
    d_part_one = (mm(d_raw, w_in, 1, 1) + mm(d_small, w_small, 1, 1)).astype(bf16).reshape(n_s, local, D)
    input_grad, d_gain_one = end(d_part_one, tokens, d_middle, gain_1, n_s, 3)

    kq = nh * DK
    small_local = jnp.concatenate(
        [
            put(part_small[:, :nh], 1, H).reshape(-1),
            put(part_small[:, nh : 2 * nh], 1, H).reshape(-1),
            put(g_taps[:KCONV, :kq], 1, H * DK).reshape(-1),
            put(g_taps[:KCONV, kq : 2 * kq], 1, H * DK).reshape(-1),
            put(g_taps[:KCONV, 2 * kq :], 1, H * DV).reshape(-1),
            d_gain_one[0],
            d_gain_two[0],
            g_gain[0],
            put(g_vec[0, :nh], 0, H),
            put(g_vec[1, :nh], 0, H),
        ]
    )
    small_grad = lax.psum(small_local, ("dp", "shard"))

    g_in, g_gu, grad_out, grad_dn = scatter(
        [part_in.reshape(n_dp, -1, part_in.shape[1]), part_gu.reshape(n_dp, -1, part_gu.shape[1])],
        [part_out.reshape(n_dp, -1, D), part_dn.reshape(n_dp, -1, D)],
        n_dp,
        n_s,
        4,
    )
    grads = [p.astype(f32) for p in whole_rows(g_in, [kq, kq, nh * DV, nh * DV])]
    grads += [grad_out.astype(f32)]
    grads += [p.astype(f32) for p in whole_rows(g_gu, [ff, ff])]
    grads += [grad_dn.astype(f32)]
    masters = [query_key[0], query_key[1], value_gate[0], value_gate[1], output_weight, gate_up[0], gate_up[1], down_weight]
    momenta = [
        momentum_query_key[0],
        momentum_query_key[1],
        momentum_value_gate[0],
        momentum_value_gate[1],
        momentum_output,
        momentum_gate_up[0],
        momentum_gate_up[1],
        momentum_down,
    ]
    moms = [MOMENTUM * m + g for m, g in zip(momenta, grads)]
    looks = [(g + MOMENTUM * m).astype(bf16) for m, g in zip(moms, grads)]
    devices = n_dp * n_s
    pads = []
    for look in looks:
        r_count, c_count = look.shape
        tall = r_count * devices > c_count
        pads.append(top(-(-r_count // 16) * 16, look) if tall else look)
    orthos = muon(pads, n_dp, n_s, 5)
    steps = []
    for master, ortho in zip(masters, orthos):
        r_count, c_count = master.shape
        scale = 0.2 * math.sqrt(max(r_count * devices, c_count))
        steps.append(-MUON_RATE * (scale * ortho[:r_count].astype(f32) + MUON_DECAY * master))
    new_one = BETA_ONE * moment_one + (1.0 - BETA_ONE) * small_grad
    new_two = BETA_TWO * moment_two + (1.0 - BETA_TWO) * small_grad * small_grad
    small_step = (
        -ADAM_RATE
        * (new_one / (1.0 - BETA_ONE**STEP_COUNT))
        / (jnp.sqrt(new_two / (1.0 - BETA_TWO**STEP_COUNT)) + ADAM_EPS)
    )

    def bundle(a):
        return (jnp.stack(a[0:2]), jnp.stack(a[2:4]), a[4], jnp.stack(a[5:7]), a[7])

    return (
        (block_out, input_grad)
        + bundle(grads)
        + bundle(steps)
        + bundle(moms)
        + (small_grad, small_step, new_one, new_two)
    )


def solution(mesh):
    cols = P(None, ("dp", "shard"), None)
    rows = P(("dp", "shard"), None)
    weights = (cols, cols, rows, cols, rows)
    return jax.shard_map(
        functools.partial(body, mesh.shape["dp"], mesh.shape["shard"]),
        mesh=mesh,
        in_specs=(rows, rows) + weights + (P(),) + weights + (P(), P(), P("dp", None)),
        out_specs=(rows, rows) + weights * 3 + (P(),) * 4,
        check_vma=False,
    )
```

time: 2300 us -> 644 us (0.28)
  waiting for transfers between devices: 1220 us -> 0.02 us
  Pallas kernels: 0 us -> 518 us
  local copies, waits for them, and re-layouts: 443 us -> 40.7 us
  matrix products: 378 us -> 35.8 us
  other arithmetic: 190 us -> 29.8 us
  starting transfers between devices: 34 us -> 0.04 us
    unnamed x11 -> x1, waiting for transfers between devices: 632 us -> 0.02 us
    pallas_call x0 -> x8, Pallas kernels: none -> 518 us  [the longest x1 143 us: gather(): pl.pallas_call(functools.partial(gather_kernel, n_dp, n_s, len(cols), len...]
    dot_general x133 -> x15, matrix products: 378 us -> 35.8 us  [mm(): lax.dot_general(a, b, (((ca,), (cb,)), ((), ())), preferred_element_type=...]
    reduce_scatter x2 -> x0, waiting for transfers between devices: 244 us -> none  [the longest x1 131 us: body(): lax.psum_scatter(local_down, ('dp', 'shard'), scatter_dimension=0, tiled=...]
    all_to_all x6 -> x0, waiting for transfers between devices: 220 us -> none  [the longest x1 118 us: body(): lax.all_to_all(returning, ('dp', 'shard'), split_axis=0, concat_axis=0, t...]
    all_gather x5 -> x0, waiting for transfers between devices: 129 us -> none  [the longest x1 60.7 us: body(): lax.all_gather(cast_gu, ('dp', 'shard'), axis=1, tiled=True)]
    unnamed x440 -> x112, local copies, waits for them, and re-layouts: 132 us -> 3.91 us
    transpose x11 -> x0, local copies, waits for them, and re-layouts: 100 us -> none  [the longest x1 34.2 us: layer_backward(): jnp.einsum('nd,snf->sdf', normed_two, d_gate_upper, preferred_element_typ...]
  transfers between devices with their start and end apart: 15 -> 1, of which waited for: 11 -> 0; matrix products, arithmetic and copies ran while one was open for 30% -> 8% of each run, Pallas kernels for 0% -> 41%
where the time goes in v1:
time: 644 us; the launch traced here: 640 us
  Pallas kernels  518 us (80%)
  local copies, waits for them, and re-layouts  40.7 us (6%)
  matrix products  35.8 us (6%)
  other arithmetic  29.8 us (5%)
  between operations  15.2 us (2%)
    pallas_call x1, Pallas kernels, gather(): pl.pallas_call(functools.partial(gather_kernel, n_dp, n_s, len(cols), len...  143 us
    pallas_call x1, Pallas kernels, muon(): pl.pallas_call(functools.partial(muon_kernel, n_dp, n_s, tuple(kinds)), o...  140 us
    pallas_call x1, Pallas kernels, scatter(): pl.pallas_call(functools.partial(scatter_kernel, n_dp, n_s, nc, len(rows)...  125 us
    pallas_call x1, Pallas kernels, ffn(): pl.pallas_call(functools.partial(ffn_kernel, n_s), out_shape=[jax.ShapeDt...  37.5 us
    dot_general x15, matrix products, mm(): lax.dot_general(a, b, (((ca,), (cb,)), ((), ())), preferred_element_type=...  35.8 us
    pallas_call x1, Pallas kernels, mid(): pl.pallas_call(functools.partial(mid_kernel, n_s), out_shape=[jax.ShapeDt...  28 us
    pallas_call x1, Pallas kernels, m2(): pl.pallas_call(functools.partial(m2_kernel, nh, P), out_shape=[jax.ShapeD...  19.4 us
    pallas_call x1, Pallas kernels, end(): pl.pallas_call(functools.partial(end_kernel, n_s), out_shape=[jax.ShapeDt...  14.2 us
  transfers between devices with their start and end apart: 1, of which 0 were waited for; matrix products, arithmetic and copies ran while one was open for 8% of the time, Pallas kernels for 41%

profile of v1, /device:TPU:31, one launch (start us, length us, event | category | flops | bytes accessed | tf_op | source)
XLA Modules:
  0.0 640.0 jit_solution(12158995206084358488)
XLA Ops:
  7.3 0.8 fusion.74
  9.6 0.8 fusion.72
  16.1 0.9 maximum_bitcast_fusion.1.refs_1_
  16.9 0.8 fusion.3.refs_4_
  18.5 142.7 %gather_weights.1 = (bf16[8,4,32,1536]{3,2,1,0:T(8,128)(2,1)}, bf16[8,4,32,1408]{3,2,1,0:T(8,128)(2,1)}, bf16[8,64,1024]{2,1,0:T(8,128)(2,1)}, bf16[8,88,1024]{2...) custom-call(bf16[4,32,1536]{2,1,0:T(8,128)(2,1)} %maximum_bitcast_fusion.refs_0_, ...), custom_call_target="tpu_custom_call" | custom-call | tf_op jit(solution)/shard_map/gather_weights/pallas_call | solution.py:451
  161.3 5.8 fusion.75.raw_ref
  167.0 1.1 fusion.31.small_ref
  170.7 11.6 %mixer_forward.1 = (bf16[512,512]{1,0:T(8,128)(2,1)}, f32[512,512]{1,0:T(8,128)}, f32[512,512]{1,0:T(8,128)}, f32[8,128,256]{2,1,0:T(8,128)}, f32[8,128,128]{2,1,0:T(8,128)}) custom-call(f32[512,1536]{1,0:T(8,128)} %fusion.75.raw_ref, f32[512,128]{1,0:T(8,128)} %fusion.31.small_ref, f32[8,1024]{1,0:T(8,128)} %select_maximum_fusion.taps_ref, ...), custom_call_target="tpu_custom_call" | custom-call | tf_op jit(solution)/shard_map/mixer_forward/pallas_call | solution.py:300
  182.3 1.9 convolution_convert_fusion.6
  184.3 28.0 %branch_sum.1 = (f32[128,1024]{1,0:T(8,128)S(1)}, bf16[4,128,1024]{2,1,0:T(8,128)(2,1)S(1)}) custom-call(bf16[4,128,1024]{2,1,0:T(8,128)(2,1)S(1)} %bitcast.197, bf16[128,1024]{1,0:T(8,128)(2,1)S(1)} %copy-done, f32[8,1024]{1,0:T(8,128)S(1)} %pad.42.gain), custom_call_target="tpu_custom_call" | custom-call | tf_op jit(solution)/shard_map/branch_sum/pallas_call | solution.py:501
  212.3 2.0 fusion.76
  214.3 1.4 multiply_convert_fusion.1
  215.7 1.0 convolution_convert_fusion.4
  217.1 1.8 convolution_convert_fusion.3
  219.0 37.5 %block_sum.1 = (bf16[128,1024]{1,0:T(8,128)(2,1)S(1)}, f32[128,1024]{1,0:T(8,128)S(1)}, bf16[4,128,1024]{2,1,0:T(8,128)(2,1)S(1)}, f32[8,1024]{1,0:T(8,128)S(1)}) custom-call(bf16[4,128,1024]{2,1,0:T(8,128)(2,1)S(1)} %bitcast.198, bf16[4,128,1024]{2,1,0:T(8,128)(2,1)S(1)} %bitcast.199, f32[128,1024]{1,0:T(8,128)S(1)} %get-tuple-element.65.middle, ...), custom_call_target="tpu_custom_call" | custom-call | tf_op jit(solution)/shard_map/block_sum/pallas_call | solution.py:526
  256.5 1.7 fusion.77.dg_ref
  258.2 19.4 %mixer_backward.1 = (bf16[512,1536]{1,0:T(8,128)(2,1)}, f32[512,128]{1,0:T(8,128)}, f32[8,1024]{1,0:T(8,128)}, f32[8,128]{1,0:T(8,128)}, f32[8,256]{1,0:T(8,128)}) custom-call(f32[512,1536]{1,0:T(8,128)} %fusion.75.raw_ref, f32[512,128]{1,0:T(8,128)} %fusion.31.small_ref, f32[8,1024]{1,0:T(8,128)} %select_maximum_fusion.taps_ref, f32[8,128]{1,0:T(8,128)} %pad.39.vec_ref, ...), custom_call_target="tpu_custom_call" | custom-call | tf_op jit(solution)/shard_map/mixer_backward/pallas_call | solution.py:330
  277.6 1.3 fusion.49
  279.0 1.0 copy.165
  280.0 0.8 broadcast.327.clone
  280.8 3.4 dynamic_update_slice.21
  284.2 1.3 reshape.508
  285.5 1.0 copy.166
  286.5 0.8 broadcast.327.clone.1
  287.3 3.4 dynamic_update_slice.22
  290.7 1.3 reshape.509
  292.0 4.2 fusion.78
  296.7 14.2 %input_sum.1 = (bf16[128,1024]{1,0:T(8,128)(2,1)S(1)}, f32[8,1024]{1,0:T(8,128)S(1)}) custom-call(bf16[4,128,1024]{2,1,0:T(8,128)(2,1)S(1)} %bitcast.196, bf16[128,1024]{1,0:T(8,128)(2,1)S(1)} %copy-done, f32[128,1024]{1,0:T(8,128)S(1)} %get-tuple-element.74.dmid, f32[8,1024]{1,0:T(8,128)S(1)} %pad.43.gain), custom_call_target="tpu_custom_call" | custom-call | tf_op jit(solution)/shard_map/input_sum/pallas_call | solution.py:542
  311.0 0.8 bitcast_dynamic-update-slice_fusion
  311.8 0.9 bitcast_dynamic-update-slice_fusion.1
  314.2 2.8 convolution_convert_fusion.5
  317.0 4.9 convolution_convert_fusion
  321.9 2.1 convolution_convert_fusion.2
  324.0 3.5 convolution_convert_fusion.1
  327.5 124.8 %scatter_gradients.1 = (bf16[4,32,1536]{2,1,0:T(8,128)(2,1)}, bf16[4,32,1408]{2,1,0:T(8,128)(2,1)}, bf16[64,1024]{1,0:T(8,128)(2,1)}, bf16[88,1024]{1,0:T(8,128)(2,1)}) custom-call(bf16[8,128,1536]{2,1,0:T(8,128)(2,1)} %bitcast.204, bf16[8,128,1408]{2,1,0:T(8,128)(2,1)} %bitcast.205, bf16[8,64,1024]{2,1,0:T(8,128)(2,1)} %bitcast.213, ...), custom_call_target="tpu_custom_call" | custom-call | tf_op jit(solution)/shard_map/scatter_gradients/pallas_call | solution.py:628
  452.3 2.0 convert_bitcast_fusion.2
  454.3 1.7 convert_bitcast_fusion.6
  457.7 0.9 pad_maximum_fusion.3
  458.6 0.8 fusion.16
  459.4 0.9 copy.155
  460.3 1.1 reshape.515
  461.5 0.9 copy.156
  462.3 1.1 reshape.516
  463.5 0.8 pad_maximum_fusion.6
  464.3 0.8 fusion.29
  465.2 1.0 copy.153
  466.3 1.6 copy.154
  467.9 1.0 reshape.514
  469.6 1.7 fusion.47
  471.3 1.0 copy.172
  472.4 1.0 copy.170
  473.3 0.9 copy.171
  474.3 0.8 fusion.12
  476.6 1.0 add_convert_fusion.1
  478.2 0.9 add_convert_fusion.2
  479.1 140.2 %muon.1 = (bf16[32,1024]{1,0:T(8,128)(2,1)}, bf16[32,1024]{1,0:T(8,128)(2,1)}, bf16[32,2048]{1,0:T(8,128)(2,1)}, bf16[32,2048]{1,0:T(8,128)(2,1)}, bf16[64,1024]...) custom-call(bf16[32,1024]{1,0:T(8,128)(2,1)} %get-tuple-element.145.refs_0_, ...), custom_call_target="tpu_custom_call" | custom-call | tf_op jit(solution)/shard_map/muon/pallas_call | solution.py:783
  619.4 1.8 add_multiply_fusion
  621.3 1.7 add_multiply_fusion.1
  622.9 0.9 pad_maximum_fusion.5
  623.8 0.8 pad_maximum_fusion.8
  625.6 0.9 pad_maximum_fusion.4
  626.6 0.8 pad_maximum_fusion.7
  628.2 1.7 add_divide_fusion.1
  631.4 1.6 copy.198
  (198 shorter events, 20.6 us)
Async XLA Ops:
  7.2 5.5 copy-start.9
  7.2 621.0 %all-reduce.11.cloned.1.call-start = ((), (), s32[]{:S(2)}) async-start(), calls=%async_computation | async-start | bytes 286720 | tf_op jit(solution)/shard_map/psum | solution.py:975
  9.6 3.4 copy-start.23
  11.8 1.3 copy-start.4
  12.7 1.0 copy-start
  12.8 1.1 copy-start.6
  12.9 1.7 copy-start.18
  13.0 2.3 slice-start
  161.3 5.8 copy-start.11
  167.0 1.8 slice-start.1
  168.2 14.2 %copy-start.46 = (bf16[8,64,1024]{2,1,0:T(8,128)(2,1)S(1)}, bf16[8,64,1024]{2,1,0:T(8,128)(2,1)}, u32[]{:S(2)}) copy-start(bf16[8,64,1024]{2,1,0:T(8,128)(2,1)} %get-tuple-element.60) | copy-start | bytes 3145732
  182.3 29.9 %copy-start.41 = (bf16[8,4,32,1408]{3,2,1,0:T(8,128)(2,1)S(1)}, bf16[8,4,32,1408]{3,2,1,0:T(8,128)(2,1)}, u32[]{:S(2)}) copy-start(bf16[8,4,32,1408]{3,2,1,0:T(8,128)(2,1)} %get-tuple-element.62) | copy-start | bytes 8650756
  212.3 2.0 copy-start.43
  212.3 2.0 copy-start.44
  215.7 1.0 copy-start.48
  215.7 1.2 copy-start.50
  215.7 1.4 copy-start.51
  217.1 1.8 copy-start.1
  219.0 37.5 %copy-start.47 = (bf16[8,64,1024]{2,1,0:T(8,128)(2,1)S(1)}, bf16[8,64,1024]{2,1,0:T(8,128)(2,1)}, u32[]{:S(2)}) copy-start(bf16[8,64,1024]{2,1,0:T(8,128)(2,1)} %get-tuple-element.60) | copy-start | bytes 3145732
  258.2 19.4 %copy-start.12 = (bf16[4,128,1024]{2,1,0:T(8,128)(2,1)S(1)}, bf16[4,128,1024]{2,1,0:T(8,128)(2,1)}, u32[]{:S(2)}) copy-start(bf16[4,128,1024]{2,1,0:T(8,128)(2,1)} %get-tuple-element.57) | copy-start | bytes 3145732
  292.0 4.2 copy-start.22
  296.3 14.7 %copy-start.40 = (f32[8,1024]{1,0:T(8,128)S(1)}, f32[8,1024]{1,0:T(8,128)}, u32[]{:S(2)}) copy-start(f32[8,1024]{1,0:T(8,128)} %get-tuple-element.88) | copy-start | bytes 98308
  317.0 5.0 copy-start.45
  317.0 5.0 copy-start.49
  321.9 2.1 copy-start.13
  321.9 2.1 copy-start.42
  452.3 3.7 copy-start.27
  456.6 2.0 copy-start.2
  457.7 1.8 copy-start.17
  457.7 3.8 copy-start.16
  459.4 4.9 copy-start.3
  465.1 7.1 %copy-start.15 = (f32[4,4,8,512]{3,2,1,0:T(8,128)S(1)}, f32[4,4,8,512]{3,2,1,0:T(8,128)}, u32[]{:S(2)}) copy-start(f32[4,4,8,512]{3,2,1,0:T(8,128)} %get-tuple-element.130) | copy-start | bytes 786436
  472.3 3.6 copy-start.14
  472.3 4.2 copy-start.28
  472.3 4.2 copy-start.32
  475.1 3.1 copy-start.29
  475.1 3.1 copy-start.37
  476.6 142.8 %copy-start.7 = (f32[88,1024]{1,0:T(8,128)S(1)}, f32[88,1024]{1,0:T(8,128)}, u32[]{:S(2)}) copy-start(f32[88,1024]{1,0:T(8,128)} %param.22) | copy-start | bytes 1081348
  476.6 144.7 %copy-start.19 = (f32[64,1024]{1,0:T(8,128)S(1)}, f32[64,1024]{1,0:T(8,128)}, u32[]{:S(2)}) copy-start(f32[64,1024]{1,0:T(8,128)} %param.20) | copy-start | bytes 786436
  477.5 145.4 %copy-start.8 = (f32[1,32,2816]{2,1,0:T(8,128)S(1)}, f32[1,32,2816]{2,1,0:T(8,128)}, u32[]{:S(2)}) copy-start(f32[1,32,2816]{2,1,0:T(8,128)} %get-tuple-element.113) | copy-start | bytes 1081348
  479.1 144.7 %copy-start.20 = (f32[1,32,2048]{2,1,0:T(8,128)S(1)}, f32[1,32,2048]{2,1,0:T(8,128)}, u32[]{:S(2)}) copy-start(f32[1,32,2048]{2,1,0:T(8,128)} %get-tuple-element.122) | copy-start | bytes 786436
  479.1 144.7 %copy-start.21 = (f32[1,32,2048]{2,1,0:T(8,128)S(1)}, f32[1,32,2048]{2,1,0:T(8,128)}, u32[]{:S(2)}) copy-start(f32[1,32,2048]{2,1,0:T(8,128)} %get-tuple-element.123) | copy-start | bytes 786436
  619.4 5.3 copy-start.25
  619.4 5.3 copy-start.26
  619.4 6.0 copy-start.5
  619.4 6.0 copy-start.30
  619.4 6.0 copy-start.31
  624.7 1.8 copy-start.10
  624.7 1.8 copy-start.35
  624.7 1.8 copy-start.36
  625.5 1.9 copy-start.24
  625.6 1.9 copy-start.38
  625.6 1.9 copy-start.39
  626.5 1.8 copy-start.33
  626.5 1.8 copy-start.34
Sparse Core Ops, SparseCore 0:
  314.3 157.4 all-reduce.10

commit v2 on v1

--- a/solution.py
+++ b/solution.py
@@ -155,38 +155,47 @@
         gated[h,c]=o*r*gain*(gt*sigmoid(gt))
     return gated,O,Us,S0s,{(h,c):X[i] for i,(h,c) in enumerate(idx)}
 
-def mixer_bwd(raw,small,taps,vec,gain,info,segr,dgated,O,Us,S0s,X,nh,P):
-    R=raw.shape[0]; nc=R//CH; n=CH
+def gate_back(raw_ref,gain,dgated_ref,o_ref,nh,emit):
+    R=raw_ref.shape[0]; nc=R//CH; n=CH
+    off=2*nh*DK+nh*DV
+    dO={};ggain=None
+    for c in range(nc):
+        for h in range(nh):
+            r_=slice(c*n,(c+1)*n); co=slice(h*DV,(h+1)*DV)
+            o=o_ref[r_,co]
+            r=lax.rsqrt(jnp.mean(o*o,axis=-1,keepdims=True)+GATE_EPS)
+            gt=raw_ref[r_,off+h*DV:off+(h+1)*DV]
+            s=sigmoid(gt); sg=gt*s
+            dg=dgated_ref[r_,co]
+            nrm=o*r
+            emit(h,c,dg*nrm*gain*(s*(1.0+gt*(1.0-s))))
+            dsn=dg*sg
+            part=jnp.sum(dsn*nrm,axis=0,keepdims=True)
+            ggain=part if ggain is None else ggain+part
+            dn=dsn*gain
+            dO[h,c]=r*dn-nrm*(r*jnp.mean(nrm*dn,axis=-1,keepdims=True))
+    return dO,ggain
+
+def mixer_bwd(raw_ref,small_ref,taps_ref,vec_ref,info_ref,segr_ref,dO,u_ref,s_ref,x_ref,nh,P,result):
+    R=raw_ref.shape[0]; nc=R//CH; n=CH
+    raw=raw_ref; taps=taps_ref[...]; vec=vec_ref[...]; info=info_ref[...]
     segc=info[:,0:1]
     a=acts(raw,taps,info,nh)
-    z,ld,beta=decays(small,vec,nh)
-    terms=chunk_terms(ld,segc,segr,R,nh)
+    z,ld,beta=decays(small_ref[...],vec,nh)
+    yield
+    terms=chunk_terms(ld,segc,segr_ref[0:1],R,nh)
     ri=iota2(n,0); ci=iota2(n,1)
     strict=ri>ci
     U_=(ri<=ci).astype(f32)
-    idx=[(h,c) for c in range(nc) for h in range(nh)]
+    idx=[(h,c) for c in reversed(range(nc)) for h in range(nh)]
     sl=lambda c:slice(c*n,(c+1)*n)
-    off=2*nh*DK+nh*DV
-    dO={};dgate={};ggain=None
-    for h,c in idx:
-        o=O[h,c]
-        r=lax.rsqrt(jnp.mean(o*o,axis=-1,keepdims=True)+GATE_EPS)
-        gt=raw[sl(c),off+h*DV:off+(h+1)*DV]
-        s=sigmoid(gt); sg=gt*s
-        dg=dgated[h,c]
-        nrm=o*r
-        dgate[h,c]=dg*nrm*gain*(s*(1.0+gt*(1.0-s)))
-        dsn=dg*sg
-        part=jnp.sum(dsn*nrm,axis=0,keepdims=True)
-        ggain=part if ggain is None else ggain+part
-        dn=dsn*gain
-        dO[h,c]=r*dn-nrm*(r*jnp.mean(nrm*dn,axis=-1,keepdims=True))
-    Pm={};dU0={};KK={};QK={}
+    yield
+    dU0={};KK={};QK={}
     for h,c in idx:
         K=a[h]["kn"][sl(c)]; Q=a[h]["qn"][sl(c)]
         KK[h,c]=dot(K,K,1,1,P["kk"]); QK[h,c]=dot(Q,K,1,1,P["qk"])
-        Pm[h,c]=QK[h,c]*terms[c][h][0]
-        dU0[h,c]=dot(Pm[h,c],dO[h,c],0,0,P["u"])
+        dU0[h,c]=dot(QK[h,c]*terms[c][h][0],dO[h,c],0,0,P["u"])
+    yield
     dS=[None]*nh
     dS1s={};Ys={}
     for c in reversed(range(nc)):
@@ -198,18 +207,18 @@
             dS1s[h,c]=dS1
             dU=dU0[h,c]
             if dS1 is not None: dU=dU+dot(t*K,dS1,1,0,P["s"])
-            Y=dot(X[h,c],dU,0,0,P["s"])
+            Y=dot(x_ref[c*nh+h],dU,0,0,P["s"])
             Ys[h,c]=Y
             if c:
                 d0=dot(e*Q,dO[h,c],0,0,P["s"])-dot((b*e)*K,Y,0,0,P["s"])
                 dS[h]=d0 if dS1 is None else g*dS1+d0
+        yield
     dQ={};dK={};dV={};dbeta={};dld={}
-    ones_r=jnp.ones((8,n),f32)
     for h,c in idx:
         R_,e,t,g=terms[c][h]
         K=a[h]["kn"][sl(c)]; Q=a[h]["qn"][sl(c)]; V=a[h]["v"][sl(c)]
         b=beta[sl(c),nh+h:nh+h+1]
-        Y=Ys[h,c]; U=Us[h,c]; dS1=dS1s[h,c]; S0=S0s[h,c]
+        Y=Ys[h,c]; U=u_ref[sl(c),h*DV:(h+1)*DV]; dS1=dS1s[h,c]
         dA=jnp.where(strict,-dot(Y,U,1,1,P["g"]),0.0)
         dP=dot(dO[h,c],U,1,1,P["g"])
         H=dP*R_
@@ -223,6 +232,7 @@
         dc=jnp.sum(Z,axis=-1,keepdims=True)-jnp.sum(Z.T,axis=-1,keepdims=True)
         last=(lax.broadcasted_iota(jnp.int32,(n,1),0)==n-1).astype(f32)
         if c:
+            S0=s_ref[c*nh+h]
             YS=dot(Y,S0,1,1,P["g"]); OS=dot(dO[h,c],S0,1,1,P["g"])
             dq=dq+e*OS
             dk=dk-(b*e)*YS
@@ -241,6 +251,7 @@
             dc=dc+last*tot
         dQ[h,c]=dq; dK[h,c]=dk; dbeta[h,c]=db
         dld[h,c]=dc
+        if h==nh-1: yield
     lane=lax.broadcasted_iota(jnp.int32,(n,128),1)
     dsm=[]
     for c in range(nc):
@@ -256,9 +267,7 @@
     dsmall=dz+dbf*beta*(1.0-beta)
     g_dt=jnp.sum(dz,axis=0,keepdims=True)
     g_al=jnp.sum(dldf*ld,axis=0,keepdims=True)
-    draw={};gt=[None]*0
-    tapg=[[None]*0 for _ in range(4)]
-    cols=[]
+    result.append((dsmall,g_dt,g_al))
     for nm in ("q","k","v"):
         for h in range(nh):
             d=a[h]
@@ -266,11 +275,9 @@
             coff={"q":h*DK,"k":nh*DK+h*DK,"v":2*nh*DK+h*DV}[nm]
             dy=jnp.concatenate([{"q":dQ,"k":dK,"v":dV}[nm][h,c] for c in range(nc)],axis=0)
             if nm!="v":
-                rho=d["r"+nm]; y=d[nm+"n"]
-                if nm=="q":
-                    dy=rho*dy-(y*(DK**0.5))*(l2(d["q"])*jnp.sum((y*(DK**0.5))*dy,axis=-1,keepdims=True)*(DK**-0.5))
-                else:
-                    dy=rho*(dy-y*jnp.sum(y*dy,axis=-1,keepdims=True))
+                y=d[nm+"n"]
+                if nm=="q": y=y*(DK**0.5)
+                dy=d["r"+nm]*(dy-y*jnp.sum(y*dy,axis=-1,keepdims=True))
             pre=d[nm+"pre"]; s=sigmoid(pre)
             dp=dy*(s*(1.0+pre*(1.0-s)))
             u=raw[:,coff:coff+w]; tp=taps[:,coff:coff+w]
@@ -281,8 +288,8 @@
                 su=pltpu.roll(dp,dp.shape[0]-k,0)*info[:,3+k:4+k]
                 du=du+tp[3-k:4-k]*su
                 tg[3-k]=jnp.sum(su*u,axis=0,keepdims=True)
-            cols.append((nm,h,du,tg))
-    return cols,dgate,dsmall,g_dt,g_al,ggain
+            result.append((coff,w,du,tg))
+        yield
 
 def m1_kernel(nh,P,raw_ref,small_ref,taps_ref,vec_ref,gain_ref,info_ref,segr_ref,gated_ref,o_ref,u_ref,s_ref,x_ref):
     gated,O,U,S0,X=mixer_fwd(raw_ref[...],small_ref[...],taps_ref[...],vec_ref[...],gain_ref[0:1],info_ref[...],segr_ref[0:1],nh,P)
@@ -302,36 +309,6 @@
                  jax.ShapeDtypeStruct((nb,DK,DV),f32),jax.ShapeDtypeStruct((nb,CH,CH),f32)],
       in_specs=[vm]*7,out_specs=[vm]*5,
       compiler_params=pltpu.CompilerParams(vmem_limit_bytes=56<<20),name="mixer_forward")(raw,small,taps,vec,gain,info,segr)
-
-def m2_kernel(nh,P,raw_ref,small_ref,taps_ref,vec_ref,gain_ref,info_ref,segr_ref,dg_ref,o_ref,u_ref,s_ref,x_ref,
-              draw_ref,dsmall_ref,gt_ref,gv_ref,gg_ref):
-    n=CH; R=raw_ref.shape[0]; nc=R//n
-    g=lambda ref:{(h,c):ref[c*n:(c+1)*n,h*DV:(h+1)*DV] for h in range(nh) for c in range(nc)}
-    b=lambda ref:{(h,c):ref[c*nh+h] for h in range(nh) for c in range(nc)}
-    cols,dgate,dsmall,g_dt,g_al,gg=mixer_bwd(raw_ref[...],small_ref[...],taps_ref[...],vec_ref[...],gain_ref[0:1],info_ref[...],segr_ref[0:1],
-       g(dg_ref),g(o_ref),g(u_ref),b(s_ref),b(x_ref),nh,P)
-    gt_ref[...]=jnp.zeros_like(gt_ref)
-    for nm,h,du,tg in cols:
-        w=DV if nm=="v" else DK
-        co={"q":h*DK,"k":nh*DK+h*DK,"v":2*nh*DK+h*DV}[nm]
-        draw_ref[:,co:co+w]=du.astype(bf16)
-        for i in range(4): gt_ref[i:i+1,co:co+w]=tg[i]
-    off=2*nh*DK+nh*DV
-    for h,c in dgate: draw_ref[c*n:(c+1)*n,off+h*DV:off+(h+1)*DV]=dgate[h,c].astype(bf16)
-    dsmall_ref[...]=dsmall
-    gv_ref[...]=jnp.zeros_like(gv_ref)
-    gv_ref[0:1]=g_al; gv_ref[1:2]=g_dt
-    gg_ref[...]=jnp.zeros_like(gg_ref)
-    gg_ref[0:1]=gg
-
-def m2(raw,small,taps,vec,gain,info,segr,dgated,O,U,S,X,P):
-    R=raw.shape[0]; nh=raw.shape[1]//(2*DK+2*DV); nb=nh*R//CH
-    vm=pl.BlockSpec(memory_space=pltpu.VMEM)
-    return pl.pallas_call(functools.partial(m2_kernel,nh,P),
-      out_shape=[jax.ShapeDtypeStruct((R,raw.shape[1]),bf16),jax.ShapeDtypeStruct((R,128),f32),jax.ShapeDtypeStruct((8,nh*(2*DK+DV)),f32),
-                 jax.ShapeDtypeStruct((8,128),f32),jax.ShapeDtypeStruct((8,DV),f32)],
-      in_specs=[vm]*12,out_specs=[vm]*5,
-      compiler_params=pltpu.CompilerParams(vmem_limit_bytes=56<<20),name="mixer_backward")(raw,small,taps,vec,gain,info,segr,dgated,O,U,S,X)
 
 
 f32=jnp.float32; bf16=jnp.bfloat16
@@ -504,132 +481,6 @@
         scratch_shapes=[pltpu.VMEM((n_s-1,rows,w),bf16)]+[D_((n_s,))]*4,
         compiler_params=pltpu.CompilerParams(collective_id=cid,has_side_effects=True,vmem_limit_bytes=40<<20),name="branch_sum")(part,x,gain)
 
-def ffn_kernel(n_s,ypart,dpart,middle,dy,gain,out,dmid,gathered,dgain,yland,dland,s0,r0,s1,r1,s2,r2):
-    _,s,_,_=place()
-    greet(ring(n_s))
-    b=push_parts(n_s,dpart,dland,s1,r1)
-    for c in b: c.wait()
-    a=push_parts(n_s,ypart,yland,s0,r0)
-    m=middle[...]
-    du,dg=norm_back(m,gain[0:1],add_up(n_s,dpart,dland))
-    dm=dy[...].astype(f32)+du
-    dmid[...]=dm
-    dgain[...]=jnp.broadcast_to(dg,dgain.shape)
-    gathered[s]=dm.astype(bf16)
-    g=push_all(n_s,gathered,s2,r2)
-    for c in a: c.wait()
-    out[...]=(m+add_up(n_s,ypart,yland)).astype(bf16)
-    for c in g: c.wait()
-
-def ffn(ypart,dpart,middle,dy,gain,n_s,cid):
-    rows,w=middle.shape
-    return pl.pallas_call(functools.partial(ffn_kernel,n_s),
-        out_shape=[jax.ShapeDtypeStruct((rows,w),bf16),jax.ShapeDtypeStruct((rows,w),f32),jax.ShapeDtypeStruct((n_s,rows,w),bf16),
-                   jax.ShapeDtypeStruct((8,w),f32)],
-        in_specs=[VM]*5,out_specs=[VM]*4,
-        scratch_shapes=[pltpu.VMEM((n_s-1,rows,w),bf16)]*2+[D_((n_s,))]*6,
-        compiler_params=pltpu.CompilerParams(collective_id=cid,has_side_effects=True,vmem_limit_bytes=40<<20),name="block_sum")(ypart,dpart,middle,dy,gain)
-
-def end_kernel(n_s,part,x,dmid,gain,out,dgain,land,s0,r0):
-    greet(ring(n_s))
-    for c in push_parts(n_s,part,land,s0,r0): c.wait()
-    du,dg=norm_back(x[...].astype(f32),gain[0:1],add_up(n_s,part,land))
-    out[...]=(dmid[...]+du).astype(bf16)
-    dgain[...]=jnp.broadcast_to(dg,dgain.shape)
-
-def end(part,x,dmid,gain,n_s,cid):
-    rows,w=x.shape
-    return pl.pallas_call(functools.partial(end_kernel,n_s),
-        out_shape=[jax.ShapeDtypeStruct((rows,w),bf16),jax.ShapeDtypeStruct((8,w),f32)],
-        in_specs=[VM]*4,out_specs=[VM]*2,
-        scratch_shapes=[pltpu.VMEM((n_s-1,rows,w),bf16)]+[D_((n_s,))]*2,
-        compiler_params=pltpu.CompilerParams(collective_id=cid,has_side_effects=True,vmem_limit_bytes=40<<20),name="input_sum")(part,x,dmid,gain)
-
-def scatter_kernel(n_dp,n_s,ncol,nrow,W,*refs):
-    n=ncol+nrow
-    g=refs[:n]; outs=refs[n:2*n]
-    xl=refs[2*n:3*n]; zb=refs[3*n:4*n]; zl=refs[4*n:5*n]; fin=refs[5*n:6*n]
-    sx,rx,sz,rz,sf,rf,lsem=refs[6*n:]
-    d,s,hi,lo=place()
-    n_hi=n_dp//2
-    me=s*n_dp+d
-    td=me//n_s; ts=me%n_s
-    own=d*n_s+s
-    fd=own%n_dp; fs=own//n_dp
-    moved=jnp.logical_or(td!=d,ts!=s)
-    zs=[((hi+j)%n_hi)*2+lo for j in range(1,n_hi)]
-    xd=hi*2+(1-lo)
-    grp=ring(n_s)
-    bar=pltpu.get_barrier_semaphore()
-    peers=grp+[(z,s) for z in zs]+[(xd,s)]
-    for p in peers:
-        pl.semaphore_signal(bar,inc=1,device_id=p,device_id_type=MESH)
-    @pl.when(moved)
-    def _():
-        pl.semaphore_signal(bar,inc=1,device_id=(td,ts),device_id_type=MESH)
-        pl.semaphore_signal(bar,inc=1,device_id=(fd,fs),device_id_type=MESH)
-    @pl.when(moved)
-    def _():
-        pl.semaphore_wait(bar,len(peers)+2)
-    @pl.when(jnp.logical_not(moved))
-    def _():
-        pl.semaphore_wait(bar,len(peers))
-    order=[(k,j) for k in range(n) for j in list(range(1,n_hi))+[0]]
-    def xc(i):
-        k,j=order[i]; z=(hi+j)%n_hi
-        return remote(g[k].at[z*2+1-lo],xl[k].at[z],sx.at[k,j],rx.at[k,j],(xd,s))
-    def zc(k,j):
-        return remote(zb[k].at[j-1],zl[k].at[j-1],sz.at[k,j],rz.at[k,j],(((hi+j)%n_hi)*2+lo,s))
-    fc={}
-    nch=len(order)
-    for i in range(nch+W):
-        if i<nch: xc(i).start()
-        if i>=W:
-            k,j=order[i-W]; z=(hi+j)%n_hi
-            xc(i-W).wait()
-            t=g[k][z*2+lo].astype(f32)+xl[k][z].astype(f32)
-            if j:
-                zb[k][j-1]=t.astype(bf16); zc(k,j).start()
-            else:
-                for jj in range(1,n_hi):
-                    zc(k,jj).wait()
-                    t=t+zl[k][jj-1].astype(f32)
-                t=t.astype(bf16)
-                if k<ncol:
-                    rows=t.shape[0]//n_s
-                    fin[k][...]=t.reshape(n_s,rows,t.shape[1])
-                    c=pltpu.make_async_copy(fin[k].at[s],outs[k].at[s],lsem.at[k]); c.start()
-                    fc[k]=[c]
-                    for jj,p in enumerate(grp):
-                        c=remote(fin[k].at[p[1]],outs[k].at[s],sf.at[k,jj],rf.at[k,jj],p); c.start(); fc[k].append(c)
-                else:
-                    fin[k][...]=t
-                    @pl.when(moved)
-                    def _():
-                        remote(fin[k],outs[k],sf.at[k,0],rf.at[k,0],(td,ts)).start()
-                    @pl.when(jnp.logical_not(moved))
-                    def _():
-                        pltpu.make_async_copy(fin[k],outs[k],rf.at[k,0]).start()
-    for k in range(n):
-        if k<ncol:
-            for c in fc[k]: c.wait()
-        else:
-            pltpu.make_async_copy(fin[k],outs[k],rf.at[k,0]).wait()
-            @pl.when(moved)
-            def _():
-                remote(fin[k],outs[k],sf.at[k,0],rf.at[k,0],(td,ts)).wait_send()
-
-def scatter(cols,rows,n_dp,n_s,cid,W=2):
-    ps=list(cols)+list(rows); n=len(ps); nc=len(cols); n_hi=n_dp//2
-    oshape=lambda k,x:(n_s,x.shape[1]//n_s,x.shape[2]) if k<nc else x.shape[1:]
-    outs=[jax.ShapeDtypeStruct(oshape(k,x),bf16) for k,x in enumerate(ps)]
-    V=pltpu.VMEM
-    sc=[V((n_hi,)+x.shape[1:],bf16) for x in ps]+[V((n_hi-1,)+x.shape[1:],bf16) for x in ps]*2+[V(oshape(k,x),bf16) for k,x in enumerate(ps)]
-    return pl.pallas_call(functools.partial(scatter_kernel,n_dp,n_s,nc,len(rows),W),
-        out_shape=outs,in_specs=[VM]*n,out_specs=[VM]*n,
-        scratch_shapes=sc+[D_((n,n_hi))]*4+[D_((n,n_s))]*2+[D_((n,))],
-        compiler_params=pltpu.CompilerParams(collective_id=cid,has_side_effects=True,vmem_limit_bytes=60<<20),name="scatter_gradients")(*ps)
-
 
 f32=jnp.float32; bf16=jnp.bfloat16
 CA,CB,CC=3.4445,-4.775,2.0315
@@ -786,6 +637,182 @@
         compiler_params=pltpu.CompilerParams(collective_id=cid,has_side_effects=True,vmem_limit_bytes=60<<20),name="muon")(*looks)
 
 
+class Reducer:
+    def __init__(self,n_dp,n_s,pieces,sems,W):
+        self.n_s=n_s; self.n_hi=n_dp//2; self.p=pieces; self.W=W
+        self.sx,self.rx,self.sz,self.rz,self.sf,self.rf,self.lsem=sems
+        d,s,hi,lo=place()
+        self.s=s; self.hi=hi; self.lo=lo
+        me=s*n_dp+d
+        self.td=me//n_s; self.ts=me%n_s
+        own=d*n_s+s
+        self.fd=own%n_dp; self.fs=own//n_dp
+        self.moved=jnp.logical_or(self.td!=d,self.ts!=s)
+        self.xd=(hi*2+(1-lo),s)
+        self.zd=lambda j:(((hi+j)%self.n_hi)*2+lo,s)
+        self.grp=ring(n_s)
+        self.q=[]; self.ns=0; self.nh=0; self.late=[]; self.fc={}
+    def greet(self):
+        bar=pltpu.get_barrier_semaphore()
+        peers=self.grp+[self.zd(j) for j in range(1,self.n_hi)]+[self.xd]
+        for p in peers: pl.semaphore_signal(bar,inc=1,device_id=p,device_id_type=MESH)
+        @pl.when(self.moved)
+        def _():
+            pl.semaphore_signal(bar,inc=1,device_id=(self.td,self.ts),device_id_type=MESH)
+            pl.semaphore_signal(bar,inc=1,device_id=(self.fd,self.fs),device_id_type=MESH)
+            pl.semaphore_wait(bar,len(peers)+2)
+        @pl.when(jnp.logical_not(self.moved))
+        def _():
+            pl.semaphore_wait(bar,len(peers))
+    def xc(self,k,j):
+        z=(self.hi+j)%self.n_hi; p=self.p[k]
+        return remote(p["g"].at[z*2+1-self.lo],p["xl"].at[j],self.sx.at[k,j],self.rx.at[k,j],self.xd)
+    def xw(self,k,j):
+        return self.xc(k,j)
+    def zc(self,k,j):
+        p=self.p[k]
+        return remote(p["zb"].at[j-1],p["zl"].at[j-1],self.sz.at[k,j],self.rz.at[k,j],self.zd(j))
+    def add(self,k):
+        self.q+=[(k,j) for j in list(range(1,self.n_hi))+[0]]
+    def handle(self,k,j):
+        p=self.p[k]; z=(self.hi+j)%self.n_hi
+        self.xw(k,j).wait()
+        t=p["g"][z*2+self.lo].astype(f32)+p["xl"][j].astype(f32)
+        if j:
+            p["zb"][j-1]=t.astype(bf16); self.zc(k,j).start()
+        else:
+            p["own"][...]=t
+            self.late.append([k,2])
+    def finish(self,k):
+        p=self.p[k]; t=p["own"][...]
+        for j in range(1,self.n_hi):
+            self.zc(k,j).wait()
+            t=t+p["zl"][j-1].astype(f32)
+        t=t.astype(bf16)
+        fin,out=p["fin"],p["out"]
+        if p["col"]:
+            rows=t.shape[0]//self.n_s
+            fin[...]=t.reshape(self.n_s,rows,t.shape[1])
+            c=pltpu.make_async_copy(fin.at[self.s],out.at[self.s],self.lsem.at[k]); c.start()
+            self.fc[k]=[c]
+            for j,q in enumerate(self.grp):
+                c=remote(fin.at[q[1]],out.at[self.s],self.sf.at[k,j],self.rf.at[k,j],q); c.start(); self.fc[k].append(c)
+        else:
+            fin[...]=t
+            @pl.when(self.moved)
+            def _():
+                remote(fin,out,self.sf.at[k,0],self.rf.at[k,0],(self.td,self.ts)).start()
+            @pl.when(jnp.logical_not(self.moved))
+            def _():
+                pltpu.make_async_copy(fin,out,self.rf.at[k,0]).start()
+    def tick(self,times=1):
+        for _ in range(times):
+            if self.ns<len(self.q):
+                self.xc(*self.q[self.ns]).start(); self.ns+=1
+                if self.ns-self.nh>self.W:
+                    self.handle(*self.q[self.nh]); self.nh+=1
+            elif self.nh<self.ns:
+                self.handle(*self.q[self.nh]); self.nh+=1
+            for e in list(self.late):
+                e[1]-=1
+                if e[1]<0:
+                    self.late.remove(e); self.finish(e[0])
+    def drain(self):
+        while self.nh<len(self.q) or self.late: self.tick()
+        for k,p in enumerate(self.p):
+            if p["col"]:
+                for c in self.fc[k]: c.wait()
+            else:
+                pltpu.make_async_copy(p["fin"],p["out"],self.rf.at[k,0]).wait()
+                @pl.when(self.moved)
+                def _():
+                    remote(p["fin"],p["out"],self.sf.at[k,0],self.rf.at[k,0],(self.td,self.ts)).wait_send()
+
+def dotb(a,b,ca,cb): return lax.dot_general(a,b,(((ca,),(cb,)),((),())),preferred_element_type=f32)
+
+def back_kernel(n_dp,n_s,nh,P,W,*refs):
+    (gu_ref,dn_ref,ypart,dpart,middle,dy,x_ref,gain2,gain1,w_out,w_in,w_sm,raw,small,taps,vec,gain,info,segr,normed,gated,o_ref,u_ref,s_ref,xi_ref,
+     out_gu,out_dn,out_out,out_g,out_q,bout,igrad,psm,gtaps,gvec,ggain,dg1,dg2,
+     yland,dland,eland,gath,dgt,draw,dsb,epart,dmid,
+     p_out,p_g,p_q)=refs[:50]
+    rest=refs[50:]
+    xl=rest[0:5]; zb=rest[5:10]; zl=rest[10:15]; own=rest[15:20]; fin=rest[20:25]
+    sems=rest[25:32]; ss,rs=rest[32:34]
+    gs=(gu_ref,dn_ref,p_out,p_g,p_q); outs=(out_gu,out_dn,out_out,out_g,out_q)
+    pieces=[dict(g=gs[k],xl=xl[k],zb=zb[k],zl=zl[k],own=own[k],fin=fin[k],out=outs[k],col=k in (0,3,4)) for k in range(5)]
+    E=Reducer(n_dp,n_s,pieces,sems,W)
+    s=E.s
+    E.greet()
+    b=push_parts(n_s,dpart,dland,ss.at[0],rs.at[0])
+    E.add(0); E.add(1)
+    E.tick(2)
+    for c in b: c.wait()
+    m=middle[...]
+    du,dg=norm_back(m,gain2[0:1],add_up(n_s,dpart,dland))
+    dm=dy[...].astype(f32)+du
+    dmid[...]=dm
+    dg2[...]=jnp.broadcast_to(dg,dg2.shape)
+    gath[s]=dm.astype(bf16)
+    g=push_all(n_s,gath,ss.at[1],rs.at[1])
+    E.tick(1)
+    for c in g: c.wait()
+    a=push_parts(n_s,ypart,yland,ss.at[2],rs.at[2])
+    rows=raw.shape[0]; D=gath.shape[2]
+    dbr=gath[...].reshape(rows,D)
+    dgt[...]=dotb(dbr,w_out[...],1,1)
+    E.tick(1)
+    p_out[...]=dotb(gated[...],dbr,0,0).astype(bf16).reshape(p_out.shape)
+    E.add(2)
+    n=CH; off=2*nh*DK+nh*DV
+    def emit(h,c,v): draw[c*n:(c+1)*n,off+h*DV:off+(h+1)*DV]=v.astype(bf16)
+    dO,gg=gate_back(raw,gain[0:1],dgt,o_ref,nh,emit)
+    ggain[...]=jnp.broadcast_to(gg,ggain.shape)
+    E.tick(1)
+    p_g[...]=dotb(normed[...],draw[:,off:],0,0).astype(bf16).reshape(p_g.shape)
+    E.add(3)
+    res=[]
+    for _ in mixer_bwd(raw,small,taps,vec,info,segr,dO,u_ref,s_ref,xi_ref,nh,P,res):
+        E.tick(1)
+    dsmall,g_dt,g_al=res[0]
+    gtaps[...]=jnp.zeros_like(gtaps); gvec[...]=jnp.zeros_like(gvec)
+    for coff,w,dcol,tg in res[1:]:
+        draw[:,coff:coff+w]=dcol.astype(bf16)
+        for i in range(4): gtaps[i:i+1,coff:coff+w]=tg[i]
+    gvec[0:1]=g_al; gvec[1:2]=g_dt
+    dsb[...]=dsmall.astype(bf16)
+    p_q[...]=dotb(normed[...],draw[:,:off],0,0).astype(bf16).reshape(p_q.shape)
+    E.add(4)
+    E.tick(2)
+    epart[...]=(dotb(draw[...],w_in[...],1,1)+dotb(dsb[...],w_sm[...],1,1)).astype(bf16).reshape(epart.shape)
+    e=push_parts(n_s,epart,eland,ss.at[3],rs.at[3])
+    for c in a: c.wait()
+    bout[...]=(middle[...]+add_up(n_s,ypart,yland)).astype(bf16)
+    psm[...]=dotb(normed[...],dsb[...],0,0)
+    E.tick(2)
+    for c in e: c.wait()
+    du,dg=norm_back(x_ref[...].astype(f32),gain1[0:1],add_up(n_s,epart,eland))
+    igrad[...]=(dmid[...]+du).astype(bf16)
+    dg1[...]=jnp.broadcast_to(dg,dg1.shape)
+    E.drain()
+
+def back(part_gu,part_dn,ypart,dpart,middle,dy,x,gain2,gain1,w_out,w_in,w_sm,raw,small,taps,vec,gain,info,segr,normed,gated,O,U,S,X,n_dp,n_s,P,cid,W=2):
+    ins=[part_gu,part_dn,ypart,dpart,middle,dy,x,gain2,gain1,w_out,w_in,w_sm,raw,small,taps,vec,gain,info,segr,normed,gated,O,U,S,X]
+    local,D=x.shape; rows=local*n_s; nh=raw.shape[1]//(2*DK+2*DV); n_hi=n_dp//2
+    off=2*nh*DK+nh*DV
+    shp=[part_gu.shape,part_dn.shape,(n_dp,w_out.shape[0]//n_dp,D),(n_dp,D//n_dp,nh*DV),(n_dp,D//n_dp,off)]
+    col=(0,3,4)
+    osh=[(n_s,q[1]//n_s,q[2]) if k in col else q[1:] for k,q in enumerate(shp)]
+    S_=jax.ShapeDtypeStruct; V=pltpu.VMEM
+    outs=[S_(q,bf16) for q in osh]+[S_((local,D),bf16),S_((local,D),bf16),S_((D,128),f32),S_((8,off),f32),S_((8,128),f32),S_((8,DV),f32),S_((8,D),f32),S_((8,D),f32)]
+    sc=[V((n_s-1,local,D),bf16)]*3+[V((n_s,local,D),bf16),V((rows,nh*DV),f32),V((rows,raw.shape[1]),bf16),V((rows,128),bf16),V((n_s,local,D),bf16),V((local,D),f32)]
+    sc+=[V(shp[k],bf16) for k in (2,3,4)]
+    sc+=[V((n_hi,)+q[1:],bf16) for q in shp]+[V((n_hi-1,)+q[1:],bf16) for q in shp]*2+[V(q[1:],f32) for q in shp]+[V(q,bf16) for q in osh]
+    sc+=[D_((5,n_hi))]*4+[D_((5,n_s))]*2+[D_((5,))]+[D_((4,n_s))]*2
+    return pl.pallas_call(functools.partial(back_kernel,n_dp,n_s,nh,P,W),
+        out_shape=outs,in_specs=[VM]*len(ins),out_specs=[VM]*len(outs),scratch_shapes=sc,
+        compiler_params=pltpu.CompilerParams(collective_id=cid,has_side_effects=True,vmem_limit_bytes=63<<20),name="backward")(*ins)
+
+
 D = 1024
 H = 8
 STEP_COUNT = 10
@@ -942,21 +969,39 @@
     d_upper = (d_hidden * (gate * sig)).astype(bf16)
     d_gu = jnp.concatenate([d_gate, d_upper], axis=1)
     d_part = mm(d_gu, w_gu, 1, 1, bf16).reshape(n_s, local, D)
-    block_out, d_middle, d_branch, d_gain_two = ffn(y_part, d_part, middle, cotangent, gain_2, n_s, 2)
-    d_branch = d_branch.reshape(rows, D)
     part_dn = mm(hidden, dy, 0, 0, bf16)
     part_gu = mm(normed_two, d_gu, 0, 0, bf16)
-    part_out = mm(gated, d_branch, 0, 0, bf16)
-    d_gated = mm(d_branch, w_out, 1, 1)
-    d_raw, d_small, g_taps, g_vec, g_gain = m2(
-        raw, raw_small, taps, vec, gain_o, info, segr, d_gated, mixed, updates, states, inverses, PASSES
+    (g_gu, grad_dn, grad_out, g_gate, g_qkv, block_out, input_grad, part_small, g_taps, g_vec, g_gain, d_gain_one, d_gain_two) = back(
+        part_gu.reshape(n_dp, -1, part_gu.shape[1]),
+        part_dn.reshape(n_dp, -1, D),
+        y_part,
+        d_part,
+        middle,
+        cotangent,
+        tokens,
+        gain_2,
+        gain_1,
+        w_out,
+        w_in,
+        w_small,
+        raw,
+        raw_small,
+        taps,
+        vec,
+        gain_o,
+        info,
+        segr,
+        normed,
+        gated,
+        mixed,
+        updates,
+        states,
+        inverses,
+        n_dp,
+        n_s,
+        PASSES,
+        2,
     )
-    d_small = d_small.astype(bf16)
-    part_in = mm(normed, d_raw, 0, 0, bf16)
-    part_small = mm(normed, d_small, 0, 0)
-    d_part_one = (mm(d_raw, w_in, 1, 1) + mm(d_small, w_small, 1, 1)).astype(bf16).reshape(n_s, local, D)
-    input_grad, d_gain_one = end(d_part_one, tokens, d_middle, gain_1, n_s, 3)
-
     kq = nh * DK
     small_local = jnp.concatenate(
         [
@@ -974,14 +1019,8 @@
     )
     small_grad = lax.psum(small_local, ("dp", "shard"))
 
-    g_in, g_gu, grad_out, grad_dn = scatter(
-        [part_in.reshape(n_dp, -1, part_in.shape[1]), part_gu.reshape(n_dp, -1, part_gu.shape[1])],
-        [part_out.reshape(n_dp, -1, D), part_dn.reshape(n_dp, -1, D)],
-        n_dp,
-        n_s,
-        4,
-    )
-    grads = [p.astype(f32) for p in whole_rows(g_in, [kq, kq, nh * DV, nh * DV])]
+    grads = [p.astype(f32) for p in whole_rows(g_qkv, [kq, kq, nh * DV])]
+    grads += [p.astype(f32) for p in whole_rows(g_gate, [nh * DV])]
     grads += [grad_out.astype(f32)]
     grads += [p.astype(f32) for p in whole_rows(g_gu, [ff, ff])]
     grads += [grad_dn.astype(f32)]

time: 644 us -> 574 us (0.89)
  Pallas kernels: 518 us -> 469 us
  matrix products: 35.8 us -> 23.6 us
    pallas_call x4 -> x1, Pallas kernels: 196 us -> 154 us  [back(): pl.pallas_call(functools.partial(back_kernel, n_dp, n_s, nh, P, W), out_s...]
    dot_general x15 -> x9, matrix products: 35.8 us -> 23.6 us  [mm(): lax.dot_general(a, b, (((ca,), (cb,)), ((), ())), preferred_element_type=...]
    pallas_call x1, Pallas kernels: 140 us -> 133 us  [muon(): pl.pallas_call(functools.partial(muon_kernel, n_dp, n_s, tuple(kinds)), o...]
  transfers between devices with their start and end apart: 1 -> 1, of which waited for: 0 -> 0; matrix products, arithmetic and copies ran while one was open for 8% -> 5% of each run, Pallas kernels for 41% -> 23%
where the time goes in v2:
time: 574 us; the launch traced here: 570 us
  Pallas kernels  469 us (82%)
  local copies, waits for them, and re-layouts  35 us (6%)
  other arithmetic  27.7 us (5%)
  matrix products  23.6 us (4%)
  between operations  15.1 us (3%)
    pallas_call x1, Pallas kernels, back(): pl.pallas_call(functools.partial(back_kernel, n_dp, n_s, nh, P, W), out_s...  154 us
    pallas_call x1, Pallas kernels, gather(): pl.pallas_call(functools.partial(gather_kernel, n_dp, n_s, len(cols), len...  143 us
    pallas_call x1, Pallas kernels, muon(): pl.pallas_call(functools.partial(muon_kernel, n_dp, n_s, tuple(kinds)), o...  133 us
    pallas_call x1, Pallas kernels, mid(): pl.pallas_call(functools.partial(mid_kernel, n_s), out_shape=[jax.ShapeDt...  28 us
    dot_general x9, matrix products, mm(): lax.dot_general(a, b, (((ca,), (cb,)), ((), ())), preferred_element_type=...  23.6 us
    pallas_call x1, Pallas kernels, m1(): pl.pallas_call(functools.partial(m1_kernel, nh, P), out_shape=[jax.ShapeD...  11.7 us
  transfers between devices with their start and end apart: 1, of which 0 were waited for; matrix products, arithmetic and copies ran while one was open for 5% of the time, Pallas kernels for 23%

profile of v2, /device:TPU:31, one launch (start us, length us, event | category | flops | bytes accessed | tf_op | source)
XLA Modules:
  0.0 570.4 jit_solution(13757577353299322854)
XLA Ops:
  7.3 0.8 fusion.60
  8.1 0.7 fusion.57
  8.8 0.7 fusion.59
  9.5 0.8 fusion.58
  10.3 0.8 select_reduce_fusion
  12.1 1.1 fusion.55
  14.6 0.7 convert_element_type.483.refs_3_
  16.4 0.9 maximum_bitcast_fusion.1.refs_1_
  17.3 0.8 fusion.3.refs_4_
  18.1 0.8 maximum_bitcast_fusion.refs_0_
  18.9 142.7 %gather_weights.1 = (bf16[8,4,32,1536]{3,2,1,0:T(8,128)(2,1)}, bf16[8,4,32,1408]{3,2,1,0:T(8,128)(2,1)}, bf16[8,64,1024]{2,1,0:T(8,128)(2,1)}, bf16[8,88,1024]{2...) custom-call(bf16[4,32,1536]{2,1,0:T(8,128)(2,1)} %maximum_bitcast_fusion.refs_0_, ...), custom_call_target="tpu_custom_call" | custom-call | tf_op jit(solution)/shard_map/gather_weights/pallas_call | solution.py:428
  161.6 2.5 fusion.62.small_ref.refs_13_
  164.1 5.4 fusion.61.raw_ref.refs_12_
  169.4 0.7 pad.41.info_ref.refs_17_
  172.7 11.7 %mixer_forward.1 = (bf16[512,512]{1,0:T(8,128)(2,1)}, f32[512,512]{1,0:T(8,128)}, f32[512,512]{1,0:T(8,128)}, f32[8,128,256]{2,1,0:T(8,128)}, f32[8,128,128]{2,1,0:T(8,128)}) custom-call(f32[512,1536]{1,0:T(8,128)} %fusion.61.raw_ref.refs_12_, f32[512,128]{1,0:T(8,128)} %fusion.62.small_ref.refs_13_, f32[8,1024]{1,0:T(8,128)} %select_maximum_fusion.taps_ref.refs_14_, ...), custom_call_target="tpu_custom_call" | custom-call | tf_op jit(solution)/shard_map/mixer_forward/pallas_call | solution.py:307
  184.4 1.9 convolution_convert_fusion.4
  186.3 28.0 %branch_sum.1 = (f32[128,1024]{1,0:T(8,128)S(1)}, bf16[4,128,1024]{2,1,0:T(8,128)(2,1)S(1)}) custom-call(bf16[4,128,1024]{2,1,0:T(8,128)(2,1)S(1)} %bitcast.184, bf16[128,1024]{1,0:T(8,128)(2,1)S(1)} %copy-done, f32[8,1024]{1,0:T(8,128)S(1)} %pad.42.gain.refs_7_), custom_call_target="tpu_custom_call" | custom-call | tf_op jit(solution)/shard_map/branch_sum/pallas_call | solution.py:478
  214.4 2.0 fusion.63
  216.4 1.5 multiply_convert_fusion.2
  217.9 2.0 convolution_convert_fusion.3
  219.9 2.0 convolution_convert_fusion.1
  222.0 2.9 convolution_convert_fusion.2
  224.9 3.5 convolution_convert_fusion
  229.0 153.8 %backward.1 = (bf16[4,32,1408]{2,1,0:T(8,128)(2,1)}, bf16[88,1024]{1,0:T(8,128)(2,1)}, bf16[64,1024]{1,0:T(8,128)(2,1)}, bf16[4,32,512]{2,1,0:T(8,128)(2,1)}, bf...) custom-call(bf16[8,128,1408]{2,1,0:T(8,128)(2,1)} %bitcast.192, ...), custom_call_target="tpu_custom_call" | custom-call | tf_op jit(solution)/shard_map/backward/pallas_call | solution.py:811
  382.8 1.4 fusion.54
  384.2 3.1 dynamic_update_slice.21
  387.6 3.1 dynamic_update_slice.22
  391.1 0.8 bitcast_dynamic-update-slice_fusion
  391.8 0.9 bitcast_dynamic-update-slice_fusion.1
  392.8 0.8 slice.177
  393.5 0.8 slice.178
  394.3 0.7 slice.179
  395.0 0.7 concatenate.24
  395.8 0.8 convert_bitcast_fusion.4
  396.6 0.8 convert_bitcast_fusion.6
  399.1 0.9 pad_maximum_fusion.3
  400.0 0.8 fusion.16
  401.4 0.7 convert_bitcast_fusion.2
  402.1 0.9 copy.126
  403.0 1.1 reshape.500
  404.1 0.8 pad_maximum_fusion.6
  404.9 0.8 fusion.29
  406.0 1.6 copy.124
  407.6 1.0 reshape.498
  408.6 0.7 pad_maximum_fusion.9
  410.0 1.0 copy.138
  411.0 1.0 copy.139
  412.0 0.9 copy.136
  413.0 0.8 fusion.12
  413.8 0.8 fusion.25
  415.3 1.0 add_convert_fusion
  416.9 0.9 add_convert_fusion.1
  417.8 132.8 %muon.1 = (bf16[32,1024]{1,0:T(8,128)(2,1)}, bf16[32,1024]{1,0:T(8,128)(2,1)}, bf16[32,2048]{1,0:T(8,128)(2,1)}, bf16[32,2048]{1,0:T(8,128)(2,1)}, bf16[64,1024]...) custom-call(bf16[32,1024]{1,0:T(8,128)(2,1)} %get-tuple-element.135.refs_0_, ...), custom_call_target="tpu_custom_call" | custom-call | tf_op jit(solution)/shard_map/muon/pallas_call | solution.py:634
  550.7 1.8 add_multiply_fusion
  552.4 1.7 add_multiply_fusion.1
  554.2 0.9 pad_maximum_fusion.5
  555.1 0.8 pad_maximum_fusion.8
  555.9 0.7 pad_maximum_fusion.11
  556.8 0.9 pad_maximum_fusion.4
  557.9 0.8 pad_maximum_fusion.7
  558.8 0.7 pad_maximum_fusion.10
  559.5 1.8 add_divide_fusion.1
  561.3 0.7 copy.162
  562.0 0.7 copy.163
  (175 shorter events, 12.7 us)
Async XLA Ops:
  7.2 6.2 %copy-start.19 = (f32[2,32,1024]{2,1,0:T(8,128)S(1)}, f32[2,32,1024]{2,1,0:T(8,128)}, u32[]{:S(2)}) copy-start(f32[2,32,1024]{2,1,0:T(8,128)} %param.18) | copy-start | bytes 786436
  7.2 552.3 %all-reduce.11.cloned.1.call-start = ((), (), s32[]{:S(2)}) async-start(), calls=%async_computation | async-start | bytes 286720 | tf_op jit(solution)/shard_map/psum | solution.py:1020
  11.5 2.1 copy-start.7
  13.5 1.0 copy-start
  13.5 1.0 copy-start.9
  13.6 1.6 copy-start.14
  13.7 2.3 slice-start
  16.4 145.2 %copy-start.5 = (bf16[1024,128]{1,0:T(8,128)(2,1)}, bf16[1024,128]{1,0:T(8,128)(2,1)S(1)}, u32[]{:S(2)}) copy-start(bf16[1024,128]{1,0:T(8,128)(2,1)S(1)} %fusion.18.refs_11_) | copy-start | bytes 786436
  161.6 2.5 copy-start.3
  164.1 6.8 %slice-start.1 = ((f32[35088]{0:T(1024)}), f32[256]{0:T(256)S(1)}, s32[]{:S(2)}) async-start(f32[35088]{0:T(1024)} %param.23), calls=%async_computation.2 | async-start | bytes 2048 | tf_op jit(solution)/shard_map/slice | solution.py:835
  172.7 11.7 %copy-start.12 = (bf16[8,64,1024]{2,1,0:T(8,128)(2,1)S(1)}, bf16[8,64,1024]{2,1,0:T(8,128)(2,1)}, u32[]{:S(2)}) copy-start(bf16[8,64,1024]{2,1,0:T(8,128)(2,1)} %get-tuple-element.58) | copy-start | bytes 3145732
  184.4 30.0 %copy-start.43 = (bf16[8,4,32,1408]{3,2,1,0:T(8,128)(2,1)S(1)}, bf16[8,4,32,1408]{3,2,1,0:T(8,128)(2,1)}, u32[]{:S(2)}) copy-start(bf16[8,4,32,1408]{3,2,1,0:T(8,128)(2,1)} %get-tuple-element.62) | copy-start | bytes 8650756
  186.3 30.0 %copy-start.2 = (f32[8,1024]{1,0:T(8,128)}, f32[8,1024]{1,0:T(8,128)S(1)}, u32[]{:S(2)}) copy-start(f32[8,1024]{1,0:T(8,128)S(1)} %pad.42.gain.refs_7_) | copy-start | bytes 98308
  214.3 2.0 copy-start.1
  214.4 2.0 copy-start.44
  214.4 2.0 copy-start.45
  387.3 3.7 copy-start.42
  387.5 8.2 %copy-start.27 = (bf16[4,32,1024]{2,1,0:T(8,128)(2,1)S(1)}, bf16[4,32,1024]{2,1,0:T(8,128)(2,1)}, u32[]{:S(2)}) copy-start(bf16[4,32,1024]{2,1,0:T(8,128)(2,1)} %get-tuple-element.70) | copy-start | bytes 786436
  390.7 6.8 %copy-start.25 = (bf16[4,32,1408]{2,1,0:T(8,128)(2,1)S(1)}, bf16[4,32,1408]{2,1,0:T(8,128)(2,1)}, u32[]{:S(2)}) copy-start(bf16[4,32,1408]{2,1,0:T(8,128)(2,1)} %get-tuple-element.73) | copy-start | bytes 1081348
  398.6 1.4 copy-start.4
  400.0 1.0 copy-start.16
  400.0 1.3 copy-start.36
  401.3 3.6 copy-start.6
  404.1 1.7 copy-start.23
  405.8 3.6 copy-start.13
  407.6 5.3 copy-start.22
  412.9 2.3 copy-start.26
  412.9 2.3 copy-start.33
  414.6 2.4 copy-start.30
  414.6 2.4 copy-start.39
  416.9 135.5 %copy-start.15 = (f32[64,1024]{1,0:T(8,128)S(1)}, f32[64,1024]{1,0:T(8,128)}, u32[]{:S(2)}) copy-start(f32[64,1024]{1,0:T(8,128)} %param.20) | copy-start | bytes 786436
  417.8 136.3 %copy-start.10 = (f32[1,32,2816]{2,1,0:T(8,128)S(1)}, f32[1,32,2816]{2,1,0:T(8,128)}, u32[]{:S(2)}) copy-start(f32[1,32,2816]{2,1,0:T(8,128)} %get-tuple-element.109) | copy-start | bytes 1081348
  550.6 4.4 copy-start.17
  550.6 4.4 copy-start.18
  552.4 3.5 copy-start.24
  554.1 2.5 copy-start.8
  554.1 2.5 copy-start.31
  554.1 2.5 copy-start.32
  556.6 1.1 copy-start.11
  556.6 1.1 copy-start.37
  556.7 1.1 copy-start.38
  557.7 1.0 copy-start.20
  557.7 1.0 copy-start.40
  557.7 1.0 copy-start.41
  557.9 1.7 copy-start.34
  557.9 1.7 copy-start.35
  557.9 3.4 copy-start.29
  558.7 3.3 copy-start.28
  559.5 3.2 copy-start.21
Sparse Core Ops, SparseCore 0:
  395.9 148.1 all-reduce.10

commit v3 on v2

--- a/solution.py
+++ b/solution.py
@@ -111,12 +111,14 @@
         out.append(heads)
     return out
 
-def mixer_fwd(raw,small,taps,vec,gain,info,segr,nh,P):
-    R=raw.shape[0]; nc=R//CH; n=CH
+def mixer_fwd(raw_ref,small_ref,taps_ref,vec_ref,gain_ref,info_ref,segr_ref,gated_ref,o_ref,u_ref,s_ref,x_ref,nh,P):
+    R=raw_ref.shape[0]; nc=R//CH; n=CH
+    info=info_ref[...]; gain=gain_ref[0:1]
     segc=info[:,0:1]
-    a=acts(raw,taps,info,nh)
-    z,ld,beta=decays(small,vec,nh)
-    terms=chunk_terms(ld,segc,segr,R,nh)
+    a=acts(raw_ref,taps_ref[...],info,nh)
+    z,ld,beta=decays(small_ref[...],vec_ref[...],nh)
+    yield
+    terms=chunk_terms(ld,segc,segr_ref[0:1],R,nh)
     ri=iota2(n,0); ci=iota2(n,1)
     strict=ri>ci
     idx=[(h,c) for c in range(nc) for h in range(nh)]
@@ -128,14 +130,18 @@
         b=beta[sl(c),nh+h:nh+h+1]
         A.append(jnp.where(strict,b*R_*dot(K,K,1,1,P["kk"]),0.0))
         Pm.append(dot(Q,K,1,1,P["qk"])*R_)
+    yield
     X=inverse(A,P["inv"])
+    for i in range(len(idx)): x_ref[i]=X[i]
+    yield
     U0=[];W=[]
     for i,(h,c) in enumerate(idx):
         b=beta[sl(c),nh+h:nh+h+1]; e=terms[c][h][1]
         U0.append(dot(X[i],b*a[h]["v"][sl(c)],1,0,P["u"]))
         W.append(dot(X[i],(b*e)*a[h]["kn"][sl(c)],1,0,P["u"]) if c else None)
+    yield
     S=[None]*nh
-    S0s={};Us={};O={}
+    off=2*nh*DK+nh*DV
     for i,(h,c) in enumerate(idx):
         R_,e,t,g=terms[c][h]
         K=a[h]["kn"][sl(c)]; Q=a[h]["qn"][sl(c)]
@@ -145,15 +151,13 @@
         if c: o=o+dot(e*Q,S0,1,0,P["o"])
         up=dot(t*K,U,0,0,P["s"])
         S[h]=up if c==0 else g*S0+up
-        S0s[h,c]=S0; Us[h,c]=U; O[h,c]=o
-    off=2*nh*DK+nh*DV
-    gated={}
-    for h,c in idx:
-        o=O[h,c]
+        co=slice(h*DV,(h+1)*DV)
+        s_ref[i]=S0 if c else jnp.zeros((DK,DV),f32)
+        u_ref[sl(c),co]=U; o_ref[sl(c),co]=o
         r=lax.rsqrt(jnp.mean(o*o,axis=-1,keepdims=True)+GATE_EPS)
-        gt=raw[sl(c),off+h*DV:off+(h+1)*DV]
-        gated[h,c]=o*r*gain*(gt*sigmoid(gt))
-    return gated,O,Us,S0s,{(h,c):X[i] for i,(h,c) in enumerate(idx)}
+        gt=raw_ref[sl(c),off+h*DV:off+(h+1)*DV]
+        gated_ref[sl(c),co]=(o*r*gain*(gt*sigmoid(gt))).astype(bf16)
+        if h==nh-1 and c==1: yield
 
 def gate_back(raw_ref,gain,dgated_ref,o_ref,nh,emit):
     R=raw_ref.shape[0]; nc=R//CH; n=CH
@@ -291,25 +295,6 @@
             result.append((coff,w,du,tg))
         yield
 
-def m1_kernel(nh,P,raw_ref,small_ref,taps_ref,vec_ref,gain_ref,info_ref,segr_ref,gated_ref,o_ref,u_ref,s_ref,x_ref):
-    gated,O,U,S0,X=mixer_fwd(raw_ref[...],small_ref[...],taps_ref[...],vec_ref[...],gain_ref[0:1],info_ref[...],segr_ref[0:1],nh,P)
-    n=CH
-    for (h,c) in gated:
-        r=slice(c*n,(c+1)*n); co=slice(h*DV,(h+1)*DV)
-        gated_ref[r,co]=gated[h,c].astype(bf16)
-        o_ref[r,co]=O[h,c]; u_ref[r,co]=U[h,c]
-        x_ref[c*nh+h]=X[h,c]
-        s_ref[c*nh+h]=S0[h,c] if c else jnp.zeros((DK,DV),f32)
-
-def m1(raw,small,taps,vec,gain,info,segr,P):
-    R=raw.shape[0]; nh=raw.shape[1]//(2*DK+2*DV); nb=nh*R//CH
-    vm=pl.BlockSpec(memory_space=pltpu.VMEM)
-    return pl.pallas_call(functools.partial(m1_kernel,nh,P),
-      out_shape=[jax.ShapeDtypeStruct((R,nh*DV),bf16),jax.ShapeDtypeStruct((R,nh*DV),f32),jax.ShapeDtypeStruct((R,nh*DV),f32),
-                 jax.ShapeDtypeStruct((nb,DK,DV),f32),jax.ShapeDtypeStruct((nb,CH,CH),f32)],
-      in_specs=[vm]*7,out_specs=[vm]*5,
-      compiler_params=pltpu.CompilerParams(vmem_limit_bytes=56<<20),name="mixer_forward")(raw,small,taps,vec,gain,info,segr)
-
 
 f32=jnp.float32; bf16=jnp.bfloat16
 MESH=pl.DeviceIdType.MESH
@@ -328,107 +313,6 @@
 
 def remote(src,dst,ss,rs,dev):
     return pltpu.make_async_remote_copy(src_ref=src,dst_ref=dst,send_sem=ss,recv_sem=rs,device_id=dev,device_id_type=MESH)
-
-def gather_kernel(n_dp,n_s,ncol,nrow,nact,order,W,*refs):
-    n=ncol+nrow+nact
-    ins=refs[:n]; outs=refs[n:2*n]
-    s0,r0,s1,r1,sa,ra,lsem=refs[2*n:]
-    d,s,hi,lo=place()
-    n_hi=n_dp//2
-    np_=ncol+nrow
-    me=d*n_s+s
-    td=me%n_dp; ts=me//n_dp
-    fd=(s*n_dp+d)//n_s; fs=(s*n_dp+d)%n_s
-    zs=[((hi+j)%n_hi)*2+lo for j in range(1,n_hi)]
-    xd=hi*2+(1-lo)
-    grp=[(d,(s+j)%n_s) for j in range(1,n_s)]
-    bar=pltpu.get_barrier_semaphore()
-    peers=grp+[(z,s) for z in zs]+[(xd,s)]
-    moved=jnp.logical_or(td!=d,ts!=s)
-    for p in peers:
-        pl.semaphore_signal(bar,inc=1,device_id=p,device_id_type=MESH)
-    @pl.when(moved)
-    def _():
-        pl.semaphore_signal(bar,inc=1,device_id=(td,ts),device_id_type=MESH)
-        pl.semaphore_signal(bar,inc=1,device_id=(fd,fs),device_id_type=MESH)
-    @pl.when(moved)
-    def _():
-        pl.semaphore_wait(bar,len(peers)+2)
-    @pl.when(jnp.logical_not(moved))
-    def _():
-        pl.semaphore_wait(bar,len(peers))
-    sends=[]
-    local=[]
-    for k in range(nact):
-        src=ins[np_+k]; dst=outs[np_+k]
-        c=pltpu.make_async_copy(src,dst.at[s],lsem.at[np_+k]); c.start(); local.append(c)
-        for j,p in enumerate(grp):
-            c=remote(src,dst.at[s],sa.at[k,j],ra.at[k,j],p); c.start(); sends.append(c)
-    col={}
-    def phase0(k):
-        if k<ncol:
-            c=pltpu.make_async_copy(ins[k].at[s],outs[k].at[d,s],lsem.at[k]); c.start()
-            col[k]=[c]
-            for j,p in enumerate(grp):
-                c=remote(ins[k].at[p[1]],outs[k].at[d,s],s0.at[k,j],r0.at[k,j],p); c.start(); col[k].append(c)
-        else:
-            @pl.when(moved)
-            def _():
-                remote(ins[k],outs[k].at[td],s0.at[k,0],r0.at[k,0],(td,ts)).start()
-            @pl.when(jnp.logical_not(moved))
-            def _():
-                pltpu.make_async_copy(ins[k],outs[k].at[d],r0.at[k,0]).start()
-    def ready(k):
-        if k<ncol:
-            for c in col[k]: c.wait()
-        else:
-            pltpu.make_async_copy(ins[k],outs[k].at[d],r0.at[k,0]).wait()
-            @pl.when(moved)
-            def _():
-                remote(ins[k],outs[k].at[td],s0.at[k,0],r0.at[k,0],(td,ts)).wait_send()
-    pieces=[]
-    for k,_,_ in order:
-        if k not in pieces: pieces.append(k)
-    for k in pieces: phase0(k)
-    def blk(i,src):
-        k,a,m=order[i]
-        return outs[k].at[src,a:a+m] if m else outs[k].at[src]
-    def first(i):
-        own=blk(i,d)
-        for j,z in enumerate(zs):
-            remote(own,own,s1.at[i,j],r1.at[i,j],(z,s)).start()
-        remote(own,own,s1.at[i,n_hi-1],r1.at[i,n_hi-1],(xd,s)).start()
-    def second(i):
-        for j in range(1,n_hi):
-            b=blk(i,((hi-j)%n_hi)*2+lo)
-            remote(b,b,s1.at[i,j-1],r1.at[i,j-1],(xd,s)).wait()
-            remote(b,b,s1.at[i,n_hi-1+j],r1.at[i,n_hi-1+j],(xd,s)).start()
-    def third(i):
-        for j in range(n_hi):
-            b=blk(i,((hi-j)%n_hi)*2+(1-lo))
-            remote(b,b,s1.at[i,n_hi-1+j],r1.at[i,n_hi-1+j],(xd,s)).wait()
-    done=set()
-    nch=len(order)
-    for i in range(nch+W+1):
-        if i<nch:
-            k=order[i][0]
-            if k not in done:
-                ready(k); done.add(k)
-            first(i)
-        if 0<=i-W<nch: second(i-W)
-        if 0<=i-W-1<nch: third(i-W-1)
-    for k in range(nact): local[k].wait()
-    for c in sends: c.wait()
-
-def gather(cols,rows,acts,n_dp,n_s,cid,order,W=1):
-    pieces=list(cols)+list(rows); np_=len(pieces); n_hi=n_dp//2
-    shapes=[jax.ShapeDtypeStruct((n_dp,)+x.shape,x.dtype) for x in pieces]+[jax.ShapeDtypeStruct((n_s,)+x.shape,x.dtype) for x in acts]
-    D=pltpu.SemaphoreType.DMA
-    na=max(len(acts),1); nch=len(order)
-    return pl.pallas_call(functools.partial(gather_kernel,n_dp,n_s,len(cols),len(rows),len(acts),order,W),
-        out_shape=shapes,in_specs=[ANY]*(np_+len(acts)),out_specs=[ANY]*(np_+len(acts)),
-        scratch_shapes=[D((np_,n_s)),D((np_,n_s)),D((nch,2*n_hi)),D((nch,2*n_hi)),D((na,n_s)),D((na,n_s)),D((np_+na,))],
-        compiler_params=pltpu.CompilerParams(collective_id=cid,has_side_effects=True),name="gather_weights")(*pieces,*acts)
 
 NORM_EPS=1e-6
 D_=pltpu.SemaphoreType.DMA
@@ -461,25 +345,6 @@
     gd=g*dn
     du=r*gd-u*(r*r*r*(jnp.sum(u*gd,axis=-1,keepdims=True)/w))
     return du,jnp.sum(u*r*dn,axis=0,keepdims=True)
-
-def mid_kernel(n_s,part,x,gain,middle,gathered,land,s0,r0,s1,r1):
-    _,s,_,_=place()
-    greet(ring(n_s))
-    a=push_parts(n_s,part,land,s0,r0)
-    for c in a: c.wait()
-    m=x[...].astype(f32)+add_up(n_s,part,land)
-    middle[...]=m
-    r=lax.rsqrt(jnp.mean(m*m,axis=-1,keepdims=True)+NORM_EPS)
-    gathered[s]=(m*r*gain[0:1]).astype(bf16)
-    for c in push_all(n_s,gathered,s1,r1): c.wait()
-
-def mid(part,x,gain,n_s,cid):
-    rows,w=x.shape
-    return pl.pallas_call(functools.partial(mid_kernel,n_s),
-        out_shape=[jax.ShapeDtypeStruct((rows,w),f32),jax.ShapeDtypeStruct((n_s,rows,w),bf16)],
-        in_specs=[VM]*3,out_specs=[VM]*2,
-        scratch_shapes=[pltpu.VMEM((n_s-1,rows,w),bf16)]+[D_((n_s,))]*4,
-        compiler_params=pltpu.CompilerParams(collective_id=cid,has_side_effects=True,vmem_limit_bytes=40<<20),name="branch_sum")(part,x,gain)
 
 
 f32=jnp.float32; bf16=jnp.bfloat16
@@ -635,6 +500,139 @@
         out_shape=[jax.ShapeDtypeStruct(x.shape,bf16) for x in looks],in_specs=[VM]*8,out_specs=[VM]*8,
         scratch_shapes=[V((r,wc),bf16)]*2+[V((tr,r),bf16)]*2+[V((r,r),bf16)]*2+[D_((1,)),D_((8,)),D_((8,)),D_((1,)),D_((1,))],
         compiler_params=pltpu.CompilerParams(collective_id=cid,has_side_effects=True,vmem_limit_bytes=60<<20),name="muon")(*looks)
+
+
+class Gatherer:
+    def __init__(self,n_dp,n_s,ins,outs,ncol,sems,order):
+        self.n_dp=n_dp; self.n_s=n_s; self.n_hi=n_dp//2; self.ins=ins; self.outs=outs; self.ncol=ncol; self.order=order
+        self.s0,self.r0,self.s1,self.r1,self.lsem=sems
+        d,s,hi,lo=place()
+        self.d=d; self.s=s; self.hi=hi; self.lo=lo
+        me=d*n_s+s
+        self.td=me%n_dp; self.ts=me//n_dp
+        self.fd=(s*n_dp+d)//n_s; self.fs=(s*n_dp+d)%n_s
+        self.moved=jnp.logical_or(self.td!=d,self.ts!=s)
+        self.zs=[((hi+j)%self.n_hi)*2+lo for j in range(1,self.n_hi)]
+        self.xd=(hi*2+(1-lo),s)
+        self.grp=ring(n_s)
+        self.col={}; self.done=set(); self.i=0
+    def greet(self):
+        bar=pltpu.get_barrier_semaphore()
+        peers=self.grp+[(z,self.s) for z in self.zs]+[self.xd]
+        for p in peers: pl.semaphore_signal(bar,inc=1,device_id=p,device_id_type=MESH)
+        @pl.when(self.moved)
+        def _():
+            pl.semaphore_signal(bar,inc=1,device_id=(self.td,self.ts),device_id_type=MESH)
+            pl.semaphore_signal(bar,inc=1,device_id=(self.fd,self.fs),device_id_type=MESH)
+            pl.semaphore_wait(bar,len(peers)+2)
+        @pl.when(jnp.logical_not(self.moved))
+        def _():
+            pl.semaphore_wait(bar,len(peers))
+    def phase0(self,k):
+        src,dst=self.ins[k],self.outs[k]
+        if k<self.ncol:
+            c=pltpu.make_async_copy(src.at[self.s],dst.at[self.d,self.s],self.lsem.at[k]); c.start()
+            self.col[k]=[c]
+            for j,p in enumerate(self.grp):
+                c=remote(src.at[p[1]],dst.at[self.d,self.s],self.s0.at[k,j],self.r0.at[k,j],p); c.start(); self.col[k].append(c)
+        else:
+            @pl.when(self.moved)
+            def _():
+                remote(src,dst.at[self.td],self.s0.at[k,0],self.r0.at[k,0],(self.td,self.ts)).start()
+            @pl.when(jnp.logical_not(self.moved))
+            def _():
+                pltpu.make_async_copy(src,dst.at[self.d],self.r0.at[k,0]).start()
+    def ready(self,k):
+        if k in self.done: return
+        self.done.add(k)
+        if k<self.ncol:
+            for c in self.col[k]: c.wait()
+        else:
+            src,dst=self.ins[k],self.outs[k]
+            pltpu.make_async_copy(src,dst.at[self.d],self.r0.at[k,0]).wait()
+            @pl.when(self.moved)
+            def _():
+                remote(src,dst.at[self.td],self.s0.at[k,0],self.r0.at[k,0],(self.td,self.ts)).wait_send()
+    def blk(self,i,src):
+        k,a,m=self.order[i]
+        return self.outs[k].at[src,a:a+m] if m else self.outs[k].at[src]
+    def go(self,i,j,b,dev):
+        return remote(b,b,self.s1.at[i,j],self.r1.at[i,j],dev)
+    def tick(self,times=1):
+        n=len(self.order); nh=self.n_hi
+        for _ in range(times):
+            i=self.i; self.i+=1
+            if i<n:
+                self.ready(self.order[i][0])
+                own=self.blk(i,self.d)
+                for j,z in enumerate(self.zs): self.go(i,j,own,(z,self.s)).start()
+                self.go(i,nh-1,own,self.xd).start()
+            if 0<=i-1<n:
+                for j in range(1,nh):
+                    b=self.blk(i-1,((self.hi-j)%nh)*2+self.lo)
+                    self.go(i-1,j-1,b,self.xd).wait()
+                    self.go(i-1,nh-1+j,b,self.xd).start()
+            if 0<=i-2<n:
+                for j in range(nh):
+                    self.go(i-2,nh-1+j,self.blk(i-2,((self.hi-j)%nh)*2+(1-self.lo)),self.xd).wait()
+    def after(self,i):
+        while self.i<i+3: self.tick()
+    def drain(self):
+        self.after(len(self.order)-1)
+
+def dotb(a,b,ca,cb): return lax.dot_general(a,b,(((ca,),(cb,)),((),())),preferred_element_type=f32)
+
+def fore_kernel(n_dp,n_s,nh,P,order,last_in,last_out,*refs):
+    (c_in,c_gu,c_out,c_dn,nown,dyown,x_ref,gain2,w_sm,taps,vec,gain,info,segr,
+     g_in,g_gu,g_out,g_dn,normed,dy,raw,small,gated,o_ref,u_ref,s_ref,xi_ref,middle,gath,
+     part,land)=refs[:31]
+    sems=refs[31:36]; ss,rs,ls=refs[36:39]
+    E=Gatherer(n_dp,n_s,[c_in,c_gu,c_out,c_dn],[g_in,g_gu,g_out,g_dn],2,sems,order)
+    s=E.s
+    E.greet()
+    normed[s]=nown[...]
+    a=push_all(n_s,normed,ss.at[0],rs.at[0])
+    for k in (0,2,1,3): E.phase0(k)
+    E.tick(2)
+    dy[s]=dyown[...]
+    b=push_all(n_s,dy,ss.at[1],rs.at[1])
+    for c in a: c.wait()
+    local,D=x_ref.shape; rows=local*n_s
+    nrm=normed[...].reshape(rows,D)
+    small[...]=dotb(nrm,w_sm[...],1,0)
+    E.after(last_in)
+    raw[...]=dotb(nrm,g_in[...].reshape(D,raw.shape[1]),1,0)
+    E.tick()
+    for i,_ in enumerate(mixer_fwd(raw,small,taps,vec,gain,info,segr,gated,o_ref,u_ref,s_ref,xi_ref,nh,P)):
+        if i%2==0: E.tick()
+    E.after(last_out)
+    part[...]=dotb(gated[...],g_out[...].reshape(nh*DV,D),1,0).astype(bf16).reshape(part.shape)
+    c1=push_parts(n_s,part,land,ss.at[2],rs.at[2])
+    E.tick()
+    for c in c1: c.wait()
+    m=x_ref[...].astype(f32)+add_up(n_s,part,land)
+    middle[...]=m
+    r=lax.rsqrt(jnp.mean(m*m,axis=-1,keepdims=True)+NORM_EPS)
+    gath[s]=(m*r*gain2[0:1]).astype(bf16)
+    c2=push_all(n_s,gath,ss.at[3],rs.at[3])
+    E.drain()
+    for c in c2: c.wait()
+    for c in b: c.wait()
+
+def fore(cols,rws,nown,dyown,x,gain2,w_sm,taps,vec,gain,info,segr,n_dp,n_s,P,cid):
+    ins=list(cols)+list(rws)+[nown,dyown,x,gain2,w_sm,taps,vec,gain,info,segr]
+    local,D=x.shape; rows=local*n_s; n_hi=n_dp//2
+    nh=rws[0].shape[0]*n_dp//DV; wid=nh*(2*DK+2*DV); nb=nh*rows//CH
+    order=tuple([(0,i,1) for i in range(n_s)]+[(2,0,0)]+[(1,i,1) for i in range(n_s)]+[(3,0,0)])
+    S_=jax.ShapeDtypeStruct; V=pltpu.VMEM
+    ps=list(cols)+list(rws)
+    outs=[S_((n_dp,)+q.shape,bf16) for q in ps]+[S_((n_s,local,D),bf16)]*2+[S_((rows,wid),f32),S_((rows,128),f32),S_((rows,nh*DV),bf16),S_((rows,nh*DV),f32),S_((rows,nh*DV),f32),
+          S_((nb,DK,DV),f32),S_((nb,CH,CH),f32),S_((local,D),f32),S_((n_s,local,D),bf16)]
+    sc=[V((n_s,local,D),bf16),V((n_s-1,local,D),bf16)]
+    sc+=[D_((4,n_s))]*2+[D_((len(order),2*n_hi))]*2+[D_((4,))]+[D_((4,n_s))]*2+[D_((2,))]
+    return pl.pallas_call(functools.partial(fore_kernel,n_dp,n_s,nh,P,order,n_s-1,n_s),
+        out_shape=outs,in_specs=[VM]*len(ins),out_specs=[VM]*len(outs),scratch_shapes=sc,
+        compiler_params=pltpu.CompilerParams(collective_id=cid,has_side_effects=True,vmem_limit_bytes=63<<20),name="forward")(*ins)
 
 
 class Reducer:
@@ -941,9 +939,8 @@
         output_weight.astype(bf16),
         down_weight.astype(bf16),
     ]
-    order = [(0, i, 1) for i in range(n_s)] + [(2, 0, 0)] + [(1, i, 1) for i in range(n_s)] + [(3, 0, 0)]
-    w_in, w_gu, w_out, w_dn, normed, dy = gather(
-        cast[:2], cast[2:], [normed_own, cotangent], n_dp, n_s, 0, tuple(order)
+    (w_in, w_gu, w_out, w_dn, normed, dy, raw, raw_small, gated, mixed, updates, states, inverses, middle, normed_two) = fore(
+        cast[:2], cast[2:], normed_own, cotangent, tokens, gain_2, w_small, taps, vec, gain_o, info, segr, n_dp, n_s, PASSES, 0
     )
     w_in = w_in.reshape(D, -1)
     w_gu = w_gu.reshape(D, -1)
@@ -951,12 +948,6 @@
     w_dn = w_dn.reshape(-1, D)
     normed = normed.reshape(rows, D)
     dy = dy.reshape(rows, D)
-
-    raw = mm(normed, w_in, 1, 0)
-    raw_small = mm(normed, w_small, 1, 0)
-    gated, mixed, updates, states, inverses = m1(raw, raw_small, taps, vec, gain_o, info, segr, PASSES)
-    part = mm(gated, w_out, 1, 0, bf16).reshape(n_s, local, D)
-    middle, normed_two = mid(part, tokens, gain_2, n_s, 1)
     normed_two = normed_two.reshape(rows, D)
     gu = mm(normed_two, w_gu, 1, 0)
     gate = gu[:, :ff]

time: 574 us -> 537 us (0.936)
  Pallas kernels: 469 us -> 437 us
  matrix products: 23.6 us -> 15.9 us
    pallas_call x3 -> x1, Pallas kernels: 182 us -> 146 us  [fore(): pl.pallas_call(functools.partial(fore_kernel, n_dp, n_s, nh, P, order, n_...]
    dot_general x9 -> x6, matrix products: 23.6 us -> 15.9 us  [mm(): lax.dot_general(a, b, (((ca,), (cb,)), ((), ())), preferred_element_type=...]
  transfers between devices with their start and end apart: 1 -> 1, of which waited for: 0 -> 0; matrix products, arithmetic and copies ran while one was open for 5% -> 5% of each run, Pallas kernels for 23% -> 25%
where the time goes in v3:
time: 537 us; the launch traced here: 533 us
  Pallas kernels  437 us (81%)
  local copies, waits for them, and re-layouts  35.5 us (7%)
  other arithmetic  29.4 us (5%)
  matrix products  15.9 us (3%)
  between operations  15 us (3%)
    pallas_call x1, Pallas kernels, back(): pl.pallas_call(functools.partial(back_kernel, n_dp, n_s, nh, P, W), out_s...  158 us
    pallas_call x1, Pallas kernels, fore(): pl.pallas_call(functools.partial(fore_kernel, n_dp, n_s, nh, P, order, n_...  146 us
    pallas_call x1, Pallas kernels, muon(): pl.pallas_call(functools.partial(muon_kernel, n_dp, n_s, tuple(kinds)), o...  133 us
    dot_general x6, matrix products, mm(): lax.dot_general(a, b, (((ca,), (cb,)), ((), ())), preferred_element_type=...  15.9 us
  transfers between devices with their start and end apart: 1, of which 0 were waited for; matrix products, arithmetic and copies ran while one was open for 5% of the time, Pallas kernels for 25%

profile of v3, /device:TPU:31, one launch (start us, length us, event | category | flops | bytes accessed | tf_op | source)
XLA Modules:
  0.0 532.8 jit_solution(7763941956689181287)
XLA Ops:
  7.3 0.8 fusion.58
  8.1 0.8 slice.154
  8.9 0.8 fusion.59
  9.7 1.3 fusion.57
  11.0 1.3 fusion.60
  12.3 0.8 select_reduce_fusion
  14.7 0.6 reshape.476
  17.4 0.7 convert_element_type.480.refs_3_
  18.1 0.7 convert_element_type.479.refs_2_
  18.8 0.7 pad.42.refs_12_.refs_17_
  19.5 0.7 constant_dynamic-slice_fusion
  20.4 0.9 fusion.18.refs_8_.refs_11_
  22.0 0.9 maximum_bitcast_fusion.1.refs_1_
  22.9 0.8 fusion.3.refs_4_
  24.9 0.7 constant_dynamic-slice_fusion.1
  26.2 0.8 maximum_bitcast_fusion.refs_0_
  27.6 146.3 %forward.1 = (bf16[8,4,32,1536]{3,2,1,0:T(8,128)(2,1)}, bf16[8,4,32,1408]{3,2,1,0:T(8,128)(2,1)}, bf16[8,64,1024]{2,1,0:T(8,128)(2,1)}, bf16[8,88,1024]{2,1,0:T(...) custom-call(bf16[4,32,1536]{2,1,0:T(8,128)(2,1)} %maximum_bitcast_fu, ...), custom_call_target="tpu_custom_call" | custom-call | tf_op jit(solution)/shard_map/forward/pallas_call | solution.py:633
  173.9 4.0 fusion.61
  177.9 1.5 multiply_convert_fusion.2
  179.5 2.0 convolution_convert_fusion.3
  181.5 2.0 convolution_convert_fusion.1
  183.5 2.9 convolution_convert_fusion.2
  186.4 3.5 convolution_convert_fusion
  190.5 157.6 %backward.1 = (bf16[4,32,1408]{2,1,0:T(8,128)(2,1)}, bf16[88,1024]{1,0:T(8,128)(2,1)}, bf16[64,1024]{1,0:T(8,128)(2,1)}, bf16[4,32,512]{2,1,0:T(8,128)(2,1)}, bf...) custom-call(bf16[8,128,1408]{2,1,0:T(8,128)(2,1)} %bitcast.178, ...), custom_call_target="tpu_custom_call" | custom-call | tf_op jit(solution)/shard_map/backward/pallas_call | solution.py:809
  348.1 1.4 fusion.54
  349.5 3.1 dynamic_update_slice.21
  352.9 3.1 dynamic_update_slice.22
  356.4 0.8 bitcast_dynamic-update-slice_fusion
  357.2 0.9 bitcast_dynamic-update-slice_fusion.1
  358.1 0.8 slice.177
  358.9 0.8 slice.178
  359.6 0.7 slice.179
  360.3 0.7 concatenate.24
  361.1 0.8 convert_bitcast_fusion.4
  361.9 0.8 convert_bitcast_fusion.6
  364.4 0.9 pad_maximum_fusion.3
  365.3 0.9 fusion.16
  366.6 1.7 convert_bitcast_fusion.2
  368.7 0.8 pad_maximum_fusion.6
  369.5 0.8 fusion.29
  370.8 0.7 pad_maximum_fusion.9
  371.5 0.7 fusion.42
  372.2 1.0 copy.138
  373.2 1.0 copy.139
  374.2 0.9 copy.136
  375.1 0.8 fusion.12
  376.0 0.8 fusion.25
  376.8 0.7 fusion.38
  377.5 1.0 add_convert_fusion
  378.4 0.7 pad.44.refs_7_
  379.1 0.9 add_convert_fusion.1
  380.0 133.0 %muon.1 = (bf16[32,1024]{1,0:T(8,128)(2,1)}, bf16[32,1024]{1,0:T(8,128)(2,1)}, bf16[32,2048]{1,0:T(8,128)(2,1)}, bf16[32,2048]{1,0:T(8,128)(2,1)}, bf16[64,1024]...) custom-call(bf16[32,1024]{1,0:T(8,128)(2,1)} %get-tuple-element.139.refs_0_, ...), custom_call_target="tpu_custom_call" | custom-call | tf_op jit(solution)/shard_map/muon/pallas_call | solution.py:499
  513.0 1.8 add_multiply_fusion
  514.8 1.7 add_multiply_fusion.1
  516.5 0.9 pad_maximum_fusion.5
  517.4 0.8 pad_maximum_fusion.8
  518.3 0.7 pad_maximum_fusion.11
  519.2 0.9 pad_maximum_fusion.4
  520.3 0.8 pad_maximum_fusion.7
  521.2 0.7 pad_maximum_fusion.10
  521.9 1.8 add_divide_fusion.1
  523.7 0.7 copy.162
  524.4 0.7 copy.163
  525.1 0.7 copy.164
  (175 shorter events, 11.4 us)
Async XLA Ops:
  7.2 8.8 %copy-start.8 = (f32[2,32,2048]{2,1,0:T(8,128)S(1)}, f32[2,32,2048]{2,1,0:T(8,128)}, u32[]{:S(2)}) copy-start(f32[2,32,2048]{2,1,0:T(8,128)} %param.19) | copy-start | bytes 1572868
  7.2 514.7 %all-reduce.11.cloned.1.call-start = ((), (), s32[]{:S(2)}) async-start(), calls=%async_computation | async-start | bytes 286720 | tf_op jit(solution)/shard_map/psum | solution.py:1011
  8.1 8.2 %copy-start.15 = (f32[2,32,1024]{2,1,0:T(8,128)S(1)}, f32[2,32,1024]{2,1,0:T(8,128)}, u32[]{:S(2)}) copy-start(f32[2,32,1024]{2,1,0:T(8,128)} %param.18) | copy-start | bytes 786436
  12.3 10.6 %copy-start.39 = (f32[1024]{0:T(1024)}, f32[1024]{0:T(1024)S(1)}, u32[]{:S(2)}) copy-start(f32[1024]{0:T(1024)S(1)} %get-tuple-element.153) | copy-start | bytes 12292
  15.3 1.1 copy-start.3
  16.3 1.0 copy-start
  16.3 1.1 copy-start.4
  16.4 1.7 copy-start.11
  18.1 3.2 copy-start.43
  18.1 3.2 copy-start.44
  20.2 3.5 copy-start.41
  20.2 4.1 slice-start
  173.9 4.0 copy-start.46
  173.9 4.0 copy-start.48
  181.5 2.0 copy-start.45
  183.5 2.9 copy-start.47
  186.4 3.5 copy-start.40
  352.6 3.7 copy-start.42
  352.9 8.2 %copy-start.25 = (bf16[4,32,1024]{2,1,0:T(8,128)(2,1)S(1)}, bf16[4,32,1024]{2,1,0:T(8,128)(2,1)}, u32[]{:S(2)}) copy-start(bf16[4,32,1024]{2,1,0:T(8,128)(2,1)} %get-tuple-element.74) | copy-start | bytes 786436
  356.0 6.7 %copy-start.23 = (bf16[4,32,1408]{2,1,0:T(8,128)(2,1)S(1)}, bf16[4,32,1408]{2,1,0:T(8,128)(2,1)}, u32[]{:S(2)}) copy-start(bf16[4,32,1408]{2,1,0:T(8,128)(2,1)} %get-tuple-element.77) | copy-start | bytes 1081348
  363.9 1.4 copy-start.1
  366.6 3.0 copy-start.2
  368.7 1.7 copy-start.20
  368.7 1.9 copy-start.19
  370.4 1.1 copy-start.10
  370.7 4.3 copy-start.18
  375.1 2.3 copy-start.24
  375.1 2.3 copy-start.31
  376.7 2.4 copy-start.28
  376.8 2.4 copy-start.36
  378.4 134.6 %copy-start.5 = (f32[88,1024]{1,0:T(8,128)S(1)}, f32[88,1024]{1,0:T(8,128)}, u32[]{:S(2)}) copy-start(f32[88,1024]{1,0:T(8,128)} %param.22) | copy-start | bytes 1081348
  379.1 135.7 %copy-start.12 = (f32[64,1024]{1,0:T(8,128)S(1)}, f32[64,1024]{1,0:T(8,128)}, u32[]{:S(2)}) copy-start(f32[64,1024]{1,0:T(8,128)} %param.20) | copy-start | bytes 786436
  380.0 136.5 %copy-start.6 = (f32[1,32,2816]{2,1,0:T(8,128)S(1)}, f32[1,32,2816]{2,1,0:T(8,128)}, u32[]{:S(2)}) copy-start(f32[1,32,2816]{2,1,0:T(8,128)} %get-tuple-element.112) | copy-start | bytes 1081348
  380.0 136.5 %copy-start.7 = (f32[1,32,2816]{2,1,0:T(8,128)S(1)}, f32[1,32,2816]{2,1,0:T(8,128)}, u32[]{:S(2)}) copy-start(f32[1,32,2816]{2,1,0:T(8,128)} %get-tuple-element.113) | copy-start | bytes 1081348
  513.0 4.4 copy-start.13
  513.0 4.4 copy-start.14
  514.8 3.5 copy-start.21
  514.8 3.5 copy-start.22
  516.5 2.5 copy-start.29
  516.5 2.5 copy-start.30
  519.0 1.1 copy-start.9
  519.0 1.1 copy-start.34
  519.0 1.1 copy-start.35
  520.1 1.0 copy-start.16
  520.1 1.0 copy-start.37
  520.1 1.0 copy-start.38
  520.2 1.7 copy-start.32
  520.2 1.7 copy-start.33
  520.3 3.4 copy-start.27
  521.1 3.3 copy-start.26
  521.9 3.2 copy-start.17
Sparse Core Ops, SparseCore 0:
  361.2 146.1 all-reduce.10
